TPU v7x, 512 devices: a whole 4x8x8 slice. The times are simulated.
512 devices in a mesh: row: 16 (over z_hi, y), col: 32 (over x, z_lo, core).
Axes of the slice: x: 4, y: 8, z: 8 (z_hi: 2, z_lo: 4; z = z_hi * 4 + z_lo), core: 2. Of those that a mesh axis runs over, the one named last changes fastest.
Arguments:
- query_act: bfloat16 [768, 16384], P(None, 'row'), may hold values from -6 to 6
- query_grad: bfloat16 [768, 16384], P(None, 'col'), may hold values from -6 to 6
- train_rot: bfloat16 [384, 16384], P(None, 'col'), may hold values from -6 to 6
- basis_in: bfloat16 [16384, 16384], P('row', 'col'), may hold values from -0.046875 to 0.046875
- basis_out: bfloat16 [16384, 16384], P('col', 'row'), may hold values from -0.046875 to 0.046875
- eig_in: float32 [16384], replicated, may hold values from 0.05 to 2
- eig_out: float32 [16384], replicated, may hold values from 0.05 to 2
Outputs:
- predicted: float32 [384, 16384], P('row', 'col')
All inputs are finite; a program needn't handle non-finite values.
Results may differ from a plain program's by a relative error of at most 0.0049.
Values may be sent and summed in bfloat16 or wider, within the bound.
No kernel may reach another device: no remote copies, remote signals or barrier semaphores. Data moves between devices by JAX's collectives and lax.ppermute only.
A program may use at most 64 MiB of HBM per device.

v0:
```python
import jax
import jax.numpy as jnp
from jax import lax
from jax.sharding import Mesh
from jax.sharding import PartitionSpec as P

COL = ("col_0", "col_1", "col_2")


damping_share = 0.1


def rows_for(lines, length):
    spare = -lines.shape[0] % length
    if not spare:
        return lines
    return jnp.concatenate([lines, jnp.zeros((spare, *lines.shape[1:]), lines.dtype)])


def copy_for_each(array, axis):
    length = lax.axis_size(axis)
    return lax.all_to_all(
        jnp.broadcast_to(array[None], (length, *array.shape)), axis, 0, 0, tiled=True
    )


def joined_along(pieces, dim):
    pieces = jnp.moveaxis(pieces, 0, dim)
    shape = pieces.shape
    return pieces.reshape(*shape[:dim], shape[dim] * shape[dim + 1], *shape[dim + 2 :])


def gather_directly(array, axis, dim):
    pieces = copy_for_each(array, axis)
    return joined_along(pieces, dim)


def cut_along(array, dim, length):
    before, after = (array.shape[:dim], array.shape[dim + 1 :])
    return jnp.moveaxis(array.reshape(*before, length, -1, *after), dim, 0)


def sent_and_summed(array, axis, dim):
    length = lax.axis_size(axis)
    pieces = lax.all_to_all(cut_along(array, dim, length), axis, 0, 0, tiled=True)
    return jnp.sum(pieces, axis=0)


def nested_sum(array, axes):
    lines = array.reshape(-1, array.shape[-1])
    padded = rows_for(lines, lax.axis_size(axes))
    whole = gather_directly(sent_and_summed(padded, axes, 0), axes, 0)
    return lax.slice_in_dim(whole, 0, len(lines)).reshape(array.shape)


def sum_by_axis(array, axes, dim):
    far, near = axes
    own = sent_and_summed(cut_along(array, dim, lax.axis_size(far)), near, dim + 1)
    return jnp.sum(lax.all_to_all(own, far, 0, 0, tiled=True), axis=0)


def gather_axes(array, axes, dim):
    far, near = axes
    first = copy_for_each(array, far)
    pieces = jnp.swapaxes(copy_for_each(first, near), 0, 1)
    return joined_along(pieces.reshape(-1, *array.shape), dim)


def nested_sum_2(array, axes):
    lines = array.reshape(-1, array.shape[-1])
    own = sum_by_axis(rows_for(lines, lax.axis_size(axes[0]) * lax.axis_size(axes[1])), axes, 0)
    whole = gather_axes(own, axes, 0)
    return whole[: len(lines)].reshape(array.shape)


def per_device(query_act, query_grad, train_rot, basis_in, basis_out, eig_in, eig_out):
    width_in = eig_in.shape[0]
    out_rows = basis_out.shape[1]
    in_cols = basis_in.shape[1]
    num_queries = query_act.shape[0]
    act_part = jnp.dot(query_act, basis_in, preferred_element_type=jnp.float32)
    grad_part = jnp.dot(query_grad, basis_out, preferred_element_type=jnp.float32)
    act_rot = nested_sum(act_part, "row").astype(jnp.bfloat16)
    grad_rot = nested_sum_2(grad_part, (("col_0", "col_1"), "col_2")).astype(jnp.bfloat16)
    damp = damping_share * jnp.mean(eig_in) * jnp.mean(eig_out)
    out_start = lax.axis_index("row") * out_rows
    in_start = lax.axis_index(COL) * in_cols
    eig_out_part = lax.dynamic_slice_in_dim(eig_out, out_start, out_rows, 0)
    eig_in_part = lax.dynamic_slice_in_dim(eig_in, in_start, in_cols, 0)
    outer = lax.dot_general(
        grad_rot, act_rot, (((0,), (0,)), ((), ())), preferred_element_type=jnp.float32
    )
    scaled = (outer / num_queries / (eig_out_part[:, None] * eig_in_part[None, :] + damp)).astype(
        jnp.bfloat16
    )
    factor = 1.0 / float(width_in) ** 0.5
    partial_inner = lax.dot_general(
        train_rot, scaled, (((1,), (1,)), ((), ())), preferred_element_type=jnp.float32
    )
    inner = (nested_sum_2(partial_inner, (("col_0", "col_1"), "col_2")) * factor).astype(
        jnp.bfloat16
    )
    partial_out = lax.dot_general(
        inner, basis_out, (((1,), (1,)), ((), ())), preferred_element_type=jnp.float32
    )
    return sent_and_summed(partial_out, "row", 0)


def solution(mesh):
    split = Mesh(
        mesh.devices.reshape(mesh.shape["row"], 4, 4, 2), ("row", "col_0", "col_1", "col_2")
    )
    placed = (P(None, "row"), P(None, COL), P(None, COL), P("row", COL), P(COL, "row"), P(), P())
    return jax.shard_map(
        per_device, mesh=split, in_specs=placed, out_specs=P("row", COL), check_vma=False
    )
```

profile of v0, /device:TPU:1, one launch (start us, length us, event | category | flops | bytes accessed | tf_op | source)
XLA Modules:
  0.0 306.8 jit_solution(4879173125177209356)
XLA Ops:
  0.0 2.6 fusion.8
  3.0 13.7 %all_to_all.55 = f32[2,16,24,1024]{3,2,1,0:T(8,128)} all-to-all(f32[2,16,24,1024]{3,2,1,0:T(8,128)S(1)} %bitcast.26), channel_id=1, replica_groups=mesh['row'=16,'col_0'=4,'col_1'=4,'col_2'=2] {'col_2'}, dimensions={0} | all-to-all | bytes 6291456 | tf_op jit(solution)/shard_map/all_to_all | solution.py:45
  16.7 3.4 %reduce_sum.72 = f32[16,24,1024]{2,1,0:T(8,128)} reduce(f32[2,16,24,1024]{3,2,1,0:T(8,128)} %all_to_all.55, f32[]{:T(128)} %constant.14.clone.1), dimensions={0}, to_apply=%region_0.0 | reduce | flops 393216 | bytes 4718596 | tf_op jit(solution)/shard_map/reduce_sum | solution.py:46
  20.2 4.2 %all-to-all-start.1 = ((f32[16,24,1024]{2,1,0:T(8,128)}), f32[16,24,1024]{2,1,0:T(8,128)S(1)}, u32[]{:S(2)}, u32[]{:S(2)}) async-start(f32[16,24,1024]{2,1,0:T(8,128)} %reduce_sum.72), calls=%async_computation.1 | async-start | bytes 3145728 | tf_op jit(solution)/shard_map/all_to_all | solution.py:59
  24.4 3.4 %fusion.9 = f32[768,512]{1,0:T(8,128)} fusion(bf16[768,1024]{1,0:T(8,128)(2,1)S(1)} %copy-done, bf16[1024,512]{1,0:T(8,128)(2,1)} %param.10), kind=kOutput, calls=%fused_computation.14 | convolution fusion | flops 805306368 | bytes 4194304 | tf_op jit(solution)/shard_map/dot_general | solution.py:81
  27.7 35.2 %all-to-all-done.1 = f32[16,24,1024]{2,1,0:T(8,128)S(1)} async-done(((f32[16,24,1024]{2,1,0:T(8,128)}), f32[16,24,1024]{2,1,0:T(8,128)S(1)}, u32[]{:S(2)}, u32[]{:S(2)}) %all-to-all-start.1) | async-done | bytes 1572896 | tf_op jit(solution)/shard_map/all_to_all | solution.py:59
  64.1 12.7 %all-to-all-start.4 = ((f32[16,48,512]{2,1,0:T(8,128)}), f32[16,48,512]{2,1,0:T(8,128)S(1)}, u32[]{:S(2)}, u32[]{:S(2)}) async-start(f32[16,48,512]{2,1,0:T(8,128)} %bitcast.28), calls=%async_computation.4 | async-start | bytes 3145728 | tf_op jit(solution)/shard_map/all_to_all | solution.py:45
  76.7 1.5 reduce_sum.73
  78.2 39.5 %all-to-all-done.4 = f32[16,48,512]{2,1,0:T(8,128)S(1)} async-done(((f32[16,48,512]{2,1,0:T(8,128)}), f32[16,48,512]{2,1,0:T(8,128)S(1)}, u32[]{:S(2)}, u32[]{:S(2)}) %all-to-all-start.4) | async-done | bytes 1572896 | tf_op jit(solution)/shard_map/all_to_all | solution.py:45
  118.8 4.9 %all-to-all-start.2 = ((bf16[16,24,1024]{2,1,0:T(8,128)(2,1)}), bf16[16,24,1024]{2,1,0:T(8,128)(2,1)}, u32[]{:S(2)}, u32[]{:S(2)}) async-start(bf16[16,24,1024]{2,1,0:T(8,128)(2,1)} %broadcast_in_dim.10), calls=%async_computation.2 | async-start | bytes 1572864 | tf_op jit(solution)/shard_map/all_to_all | solution.py:22
  123.8 21.3 %all-to-all-done.2 = bf16[16,24,1024]{2,1,0:T(8,128)(2,1)} async-done(((bf16[16,24,1024]{2,1,0:T(8,128)(2,1)}), bf16[16,24,1024]{2,1,0:T(8,128)(2,1)}, u32[]{:S(2)}, u32[]{:S(2)}) %all-to-all-start.2) | async-done | bytes 786464 | tf_op jit(solution)/shard_map/all_to_all | solution.py:22
  146.4 6.4 %all_to_all.56 = bf16[2,16,24,1024]{3,2,1,0:T(8,128)(2,1)S(1)} all-to-all(bf16[2,16,24,1024]{3,2,1,0:T(8,128)(2,1)S(1)} %broadcast_in_dim.11), channel_id=1, replica_groups=mesh['row'=16,'col_0'=4,'col_1'=4,'col_2'=2] {'col_2'}, dimensions={0} | all-to-all | bytes 3145728 | tf_op jit(solution)/shard_map/all_to_all | solution.py:22
  153.8 13.1 %all-to-all-start.5 = ((bf16[16,48,512]{2,1,0:T(8,128)(2,1)}), bf16[16,48,512]{2,1,0:T(8,128)(2,1)}, u32[]{:S(2)}, u32[]{:S(2)}) async-start(bf16[16,48,512]{2,1,0:T(8,128)(2,1)} %broadcast_in_dim.12), calls=%async_computation.5 | async-start | bytes 1572864 | tf_op jit(solution)/shard_map/all_to_all | solution.py:22
  169.7 1.3 copy.35
  171.0 19.3 %all-to-all-done.5 = bf16[16,48,512]{2,1,0:T(8,128)(2,1)} async-done(((bf16[16,48,512]{2,1,0:T(8,128)(2,1)}), bf16[16,48,512]{2,1,0:T(8,128)(2,1)}, u32[]{:S(2)}, u32[]{:S(2)}) %all-to-all-start.5) | async-done | bytes 786464 | tf_op jit(solution)/shard_map/all_to_all | solution.py:22
  190.3 3.1 %convolution_bitcast_fusion = f32[384,1024]{1,0:T(8,128)S(1)} fusion(bf16[384,512]{1,0:T(8,128)(2,1)S(1)} %copy-done.5, bf16[768,1024]{1,0:T(8,128)(2,1)} %bitcast.29, bf16[768,512]{1,0:T(8,128)(2,1)} %bitcast.5, f32[]{:T(128)S(6)} %mul.47, f32[512]{0:T(512)S(1)} %dynamic_slice.7, f32[1024]{0:T(1024)S(1)} %dynamic-slice-done), kind=kOutput, calls=%fused_computation.4 | convolution fusion | flops 1210580992 | bytes 4331524 | tf_op jit(solution)/shard_map/dot_general | solution.py:97
  193.4 1.5 reshape_reshape.9
  194.9 2.5 copy.27
  197.4 7.8 %all_to_all.57 = f32[2,16,12,1024]{3,1,2,0:T(8,128)S(1)} all-to-all(f32[2,16,12,1024]{3,1,2,0:T(8,128)S(1)} %copy.27), channel_id=1, replica_groups=mesh['row'=16,'col_0'=4,'col_1'=4,'col_2'=2] {'col_2'}, dimensions={0} | all-to-all | bytes 3145728 | tf_op jit(solution)/shard_map/all_to_all | solution.py:45
  206.3 1.6 copy.28
  207.9 29.6 %all_to_all.58 = f32[16,12,1024]{2,1,0:T(8,128)S(1)} all-to-all(f32[16,12,1024]{2,1,0:T(8,128)S(1)} %copy.28), channel_id=1, replica_groups=mesh['row'=16,'col_0'=4,'col_1'=4,'col_2'=2] {'col_0','col_1'}, dimensions={0} | all-to-all | bytes 1572864 | tf_op jit(solution)/shard_map/all_to_all | solution.py:59
  237.7 30.9 %all_to_all.59 = f32[16,12,1024]{2,1,0:T(8,128)S(1)} all-to-all(f32[16,12,1024]{2,1,0:T(8,128)S(1)} %broadcast_in_dim.13), channel_id=1, replica_groups=mesh['row'=16,'col_0'=4,'col_1'=4,'col_2'=2] {'col_0','col_1'}, dimensions={0} | all-to-all | bytes 1572864 | tf_op jit(solution)/shard_map/all_to_all | solution.py:22
  269.2 6.3 %all_to_all.60 = f32[2,16,12,1024]{3,1,2,0:T(8,128)S(1)} all-to-all(f32[2,16,12,1024]{3,1,2,0:T(8,128)S(1)} %broadcast_in_dim.14), channel_id=1, replica_groups=mesh['row'=16,'col_0'=4,'col_1'=4,'col_2'=2] {'col_2'}, dimensions={0} | all-to-all | bytes 3145728 | tf_op jit(solution)/shard_map/all_to_all | solution.py:22
  277.6 28.5 %all_to_all.61 = f32[16,24,512]{2,1,0:T(8,128)S(1)} all-to-all(f32[16,24,512]{2,1,0:T(8,128)S(1)} %fusion), channel_id=1, replica_groups=mesh['row'=16,'col_0'=4,'col_1'=4,'col_2'=2] {'row'}, dimensions={0} | all-to-all | bytes 1572864 | tf_op jit(solution)/shard_map/all_to_all | solution.py:45
  (30 shorter events, 10.9 us)
Async XLA Ops:
  0.0 24.3 %copy-start = (bf16[768,1024]{1,0:T(8,128)(2,1)S(1)}, bf16[768,1024]{1,0:T(8,128)(2,1)}, u32[]{:S(2)}) copy-start(bf16[768,1024]{1,0:T(8,128)(2,1)} %param.7) | copy-start | bytes 4718596
  20.2 42.8 %all-to-all-start.1 = ((f32[16,24,1024]{2,1,0:T(8,128)}), f32[16,24,1024]{2,1,0:T(8,128)S(1)}, u32[]{:S(2)}, u32[]{:S(2)}) async-start(f32[16,24,1024]{2,1,0:T(8,128)} %reduce_sum.72), calls=%async_computation.1 | async-start | bytes 3145728 | tf_op jit(solution)/shard_map/all_to_all | solution.py:59
  62.9 1.1 copy-start.1
  64.1 53.7 %all-to-all-start.4 = ((f32[16,48,512]{2,1,0:T(8,128)}), f32[16,48,512]{2,1,0:T(8,128)S(1)}, u32[]{:S(2)}, u32[]{:S(2)}) async-start(f32[16,48,512]{2,1,0:T(8,128)} %bitcast.28), calls=%async_computation.4 | async-start | bytes 3145728 | tf_op jit(solution)/shard_map/all_to_all | solution.py:45
  118.8 26.4 %all-to-all-start.2 = ((bf16[16,24,1024]{2,1,0:T(8,128)(2,1)}), bf16[16,24,1024]{2,1,0:T(8,128)(2,1)}, u32[]{:S(2)}, u32[]{:S(2)}) async-start(bf16[16,24,1024]{2,1,0:T(8,128)(2,1)} %broadcast_in_dim.10), calls=%async_computation.2 | async-start | bytes 1572864 | tf_op jit(solution)/shard_map/all_to_all | solution.py:22
  152.8 14.1 %copy-start.4 = (f32[16384]{0:T(1024)S(1)}, f32[16384]{0:T(1024)}, u32[]{:S(2)}) copy-start(f32[16384]{0:T(1024)} %param.12) | copy-start | bytes 196612
  152.8 14.8 %copy-start.3 = (f32[16384]{0:T(1024)S(1)}, f32[16384]{0:T(1024)}, u32[]{:S(2)}) copy-start(f32[16384]{0:T(1024)} %param.13) | copy-start | bytes 196612
  153.8 36.5 %all-to-all-start.5 = ((bf16[16,48,512]{2,1,0:T(8,128)(2,1)}), bf16[16,48,512]{2,1,0:T(8,128)(2,1)}, u32[]{:S(2)}, u32[]{:S(2)}) async-start(bf16[16,48,512]{2,1,0:T(8,128)(2,1)} %broadcast_in_dim.12), calls=%async_computation.5 | async-start | bytes 1572864 | tf_op jit(solution)/shard_map/all_to_all | solution.py:22
  169.7 20.6 %dynamic-slice-start = ((f32[16384]{0:T(1024)}, s32[]{:T(128)}), f32[1024]{0:T(1024)S(1)}, s32[]{:S(2)}) async-start(f32[16384]{0:T(1024)} %param.13, s32[]{:T(128)} %select_n.6), calls=%async_computation.11 | async-start | bytes 8704 | tf_op jit(solution)/shard_map/dynamic_slice | solution.py:88
  169.7 20.6 %copy-start.5 = (bf16[384,512]{1,0:T(8,128)(2,1)S(1)}, bf16[384,512]{1,0:T(8,128)(2,1)}, u32[]{:S(2)}) copy-start(bf16[384,512]{1,0:T(8,128)(2,1)} %param.9) | copy-start | bytes 1179652
  275.6 1.2 copy-start.2
where the time goes:
time: 309 us; the launch traced here: 307 us
  blocking collectives  123 us (40%)
  waiting for transfers between devices  115 us (37%)
  starting transfers between devices  34.9 us (11%)
  local copies, waits for them, and re-layouts  13.7 us (4%)
  matrix products  9.79 us (3%)
  other arithmetic  8.29 us (3%)
    all_to_all x3, blocking collectives, sent_and_summed(): lax.all_to_all(cut_along(array, dim, length), axis, 0, 0, tiled=True)  50.1 us
    all_to_all x3, blocking collectives, copy_for_each(): lax.all_to_all(jnp.broadcast_to(array[None], (length, *array.shape)), axi...  43.6 us
    all_to_all x2, waiting for transfers between devices, copy_for_each(): lax.all_to_all(jnp.broadcast_to(array[None], (length, *array.shape)), axi...  40.6 us
    all_to_all x1, waiting for transfers between devices, sent_and_summed(): lax.all_to_all(cut_along(array, dim, length), axis, 0, 0, tiled=True)  39.5 us
    all_to_all x1, waiting for transfers between devices, sum_by_axis(): return jnp.sum(lax.all_to_all(own, far, 0, 0, tiled=True), axis=0)  35.2 us
    all_to_all x1, blocking collectives, sum_by_axis(): return jnp.sum(lax.all_to_all(own, far, 0, 0, tiled=True), axis=0)  29.6 us
    all_to_all x2, starting transfers between devices, copy_for_each(): lax.all_to_all(jnp.broadcast_to(array[None], (length, *array.shape)), axi...  18.1 us
    all_to_all x1, starting transfers between devices, sent_and_summed(): lax.all_to_all(cut_along(array, dim, length), axis, 0, 0, tiled=True)  12.7 us
  transfers between devices with their start and end apart: 4, of which 4 were waited for; matrix products, arithmetic and copies ran while one was open for 3% of the time, Pallas kernels for 0%

commit v1 on v0

v1 whole, which is shorter than its diff:
```python
import functools

import jax
import jax.numpy as jnp
import numpy as np
from jax import lax
from jax.experimental import pallas as pl
from jax.experimental.pallas import tpu as pltpu
from jax.sharding import Mesh
from jax.sharding import PartitionSpec as P

ROW = ("z_hi", "y")
CHIPS = ("x", "z_lo")
COL = ("x", "z_lo", "core")
ALL = ROW + COL
SIZES = (2, 8, 4, 4, 2)
SWAP = [(0, 1), (1, 0)]

damping_share = 0.1

bf16 = jnp.bfloat16
f32 = jnp.float32


def mixed_groups():
    ids = np.arange(np.prod(SIZES)).reshape(16, 16, 2)
    along_row = [ids[:, c, 0].tolist() for c in range(16)]
    along_col = [ids[r, :, 1].tolist() for r in range(16)]
    return along_row + along_col


def dot(a, b):
    return jnp.dot(a, b, preferred_element_type=f32)


def dot_nt(a, b):
    return lax.dot_general(a, b, (((1,), (1,)), ((), ())), preferred_element_type=f32)


def dot_tn(a, b):
    return lax.dot_general(a, b, (((0,), (0,)), ((), ())), preferred_element_type=f32)


def rotate_kernel(core, act, grad, b_in, b_out, b_in_o, grad_o, b_out_o, out):
    tile = 256
    half = b_in.shape[1]

    @pl.when(core[0] == 0)
    def _():
        @pl.loop(0, act.shape[0] // tile)
        def _(m):
            rows = pl.ds(pl.multiple_of(m * tile, tile), tile)
            left = act[rows, :]
            out[rows, :half] = dot(left, b_in[...]).astype(bf16)
            out[rows, half:] = dot(left, b_in_o[...]).astype(bf16)

    @pl.when(core[0] == 1)
    def _():
        @pl.loop(0, act.shape[0] // tile)
        def _(m):
            rows = pl.ds(pl.multiple_of(m * tile, tile), tile)
            out[rows, :] = (
                dot(grad_o[rows, :], b_out_o[...]) + dot(grad[rows, :], b_out[...])
            ).astype(bf16)


def outer_kernel(queries, core, damp, own, other, train, train_o, e_out, e_in, out):
    tile = 256
    half = train.shape[1]

    def body(act, grad, first, left, right):
        @pl.loop(0, half // tile)
        def _(m):
            start = pl.multiple_of(m * tile, tile)
            outer = dot_tn(grad[:, pl.ds(first + start, tile)], act[...])
            scaled = (
                outer / queries / (e_out[pl.ds(start, tile), :] * e_in[...] + damp[0])
            ).astype(bf16)
            out[:, pl.ds(start, tile)] = (
                dot_nt(left[...], scaled[:, :half]) + dot_nt(right[...], scaled[:, half:])
            ).astype(bf16)

    @pl.when(core[0] == 0)
    def _():
        body(own, other, 0, train, train_o)

    @pl.when(core[0] == 1)
    def _():
        body(other, own, half, train_o, train)


def back_kernel(core, own, other, b_out, out):
    half = own.shape[1]

    def body(left, right):
        out[...] = (
            dot_nt(left[...], b_out[:, :half]) + dot_nt(right[...], b_out[:, half:])
        ).astype(bf16)

    @pl.when(core[0] == 0)
    def _():
        body(own, other)

    @pl.when(core[0] == 1)
    def _():
        body(other, own)


def call(kernel, shape, scalars, arrays, flops):
    return pl.pallas_call(
        kernel,
        out_shape=jax.ShapeDtypeStruct(shape, bf16),
        in_specs=[pl.BlockSpec(memory_space=pltpu.SMEM)] * len(scalars)
        + [pl.BlockSpec(memory_space=pltpu.VMEM)] * len(arrays),
        out_specs=pl.BlockSpec(memory_space=pltpu.VMEM),
        compiler_params=pltpu.CompilerParams(vmem_limit_bytes=32 * 1024 * 1024),
        cost_estimate=pl.CostEstimate(flops=flops, bytes_accessed=4 << 20, transcendentals=0),
    )(*scalars, *arrays)


def summed(pieces):
    return jnp.sum(pieces.astype(f32), axis=0)


def spread(array, n):
    return jnp.broadcast_to(array[None], (n, *array.shape))


def per_device(query_act, query_grad, train_rot, basis_in, basis_out, eig_in, eig_out):
    queries, train = query_act.shape[0], train_rot.shape[0]
    width = basis_in.shape[0]
    half = basis_in.shape[1]
    groups = mixed_groups()
    mixed = functools.partial(
        lax.all_to_all,
        axis_name=ALL,
        split_axis=0,
        concat_axis=0,
        axis_index_groups=groups,
        tiled=True,
    )
    core_id = lax.axis_index("core")
    core = core_id.astype(jnp.int32).reshape(1)

    basis_in_o = lax.ppermute(basis_in, "core", [(1, 0)])
    basis_out_o = lax.ppermute(basis_out, "core", [(0, 1)])
    grad_o = lax.ppermute(query_grad, "core", [(0, 1)])
    train_o = lax.ppermute(train_rot, "core", SWAP)

    part = call(
        rotate_kernel,
        (queries, width),
        (core,),
        (query_act, query_grad, basis_in, basis_out, basis_in_o, grad_o, basis_out_o),
        2 * queries * width * width,
    )
    rot = summed(mixed(part.reshape(16, queries // 16, width))).astype(bf16)
    own = mixed(spread(rot, 16)).reshape(queries, width)
    other = lax.ppermute(own, "core", SWAP)

    damp = damping_share * jnp.mean(eig_in) * jnp.mean(eig_out)
    out_start = lax.axis_index(ROW) * width + core_id * half
    in_start = lax.axis_index(CHIPS) * width
    e_out = lax.dynamic_slice_in_dim(eig_out, out_start, half, 0)[:, None]
    e_in = lax.dynamic_slice_in_dim(eig_in, in_start, width, 0)[None, :]
    partial_inner = call(
        functools.partial(outer_kernel, queries),
        (train, half),
        (core, damp.reshape(1)),
        (own, other, train_rot, train_o, e_out, e_in),
        2 * queries * width * half + 2 * train * width * half,
    )
    pieces = lax.all_to_all(
        partial_inner.reshape(16, train // 16, half), CHIPS, 0, 0, tiled=True
    )
    factor = 1.0 / float(eig_in.shape[0]) ** 0.5
    inner_part = (summed(pieces) * factor).astype(bf16)
    inner = lax.all_to_all(spread(inner_part, 16), CHIPS, 0, 0, tiled=True).reshape(train, half)
    inner_o = lax.ppermute(inner, "core", SWAP)
    partial_out = call(
        back_kernel,
        (train, half),
        (core,),
        (inner, inner_o, basis_out),
        2 * train * half * width,
    )
    return summed(
        lax.all_to_all(partial_out.reshape(16, train // 16, half), ROW, 0, 0, tiled=True)
    )


def solution(mesh):
    split = Mesh(mesh.devices.reshape(SIZES), ALL)
    placed = (P(None, ROW), P(None, COL), P(None, COL), P(ROW, COL), P(COL, ROW), P(), P())
    return jax.shard_map(
        per_device, mesh=split, in_specs=placed, out_specs=P(ROW, COL), check_vma=False
    )
```

time: 309 us -> 182 us (0.59)
  waiting for transfers between devices: 115 us -> 4.62 us
  blocking collectives: 123 us -> 141 us
  starting transfers between devices: 34.9 us -> 19.4 us
  matrix products: 9.79 us -> 0 us
  local copies, waits for them, and re-layouts: 13.7 us -> 5.45 us
  other arithmetic: 8.29 us -> 2.35 us
  Pallas kernels: 0 us -> 5.77 us
    all_to_all x4 -> x0, waiting for transfers between devices: 115 us -> none  [the longest x2 40.6 us: copy_for_each(): lax.all_to_all(jnp.broadcast_to(array[None], (length, *array.shape)), axi...]
    all_to_all x4 -> x0, starting transfers between devices: 34.9 us -> none  [the longest x2 18.1 us: copy_for_each(): lax.all_to_all(jnp.broadcast_to(array[None], (length, *array.shape)), axi...]
    ppermute x0 -> x6, starting transfers between devices: none -> 19.4 us  [the longest x1 8.84 us: per_device(): basis_in_o = lax.ppermute(basis_in, 'core', [(1, 0)])]
    all_to_all x7 -> x5, blocking collectives: 123 us -> 141 us  [the longest x1 43.9 us: per_device(): rot = summed(mixed(part.reshape(16, queries // 16, width))).astype(bf16)]
    dot_general x4 -> x0, matrix products: 9.79 us -> none  [the longest x1 3.35 us: per_device(): act_part = jnp.dot(query_act, basis_in, preferred_element_type=jnp.float32)]
    reduce_sum x6 -> x3, other arithmetic: 6.86 us -> 1.04 us  [summed(): return jnp.sum(pieces.astype(f32), axis=0)]
    pallas_call x0 -> x3, Pallas kernels: none -> 5.77 us  [call(): pl.pallas_call(kernel, out_shape=jax.ShapeDtypeStruct(shape, bf16), in_sp...]
    ppermute x0 -> x6, waiting for transfers between devices: none -> 4.62 us  [the longest x1 3.29 us: per_device(): grad_o = lax.ppermute(query_grad, 'core', [(0, 1)])]
  transfers between devices with their start and end apart: 4 -> 6, of which waited for: 4 -> 2; matrix products, arithmetic and copies ran while one was open for 3% -> 1% of each run, Pallas kernels for 0% -> 0%
where the time goes in v1:
time: 182 us; the launch traced here: 180 us
  blocking collectives  141 us (77%)
  starting transfers between devices  19.4 us (11%)
  Pallas kernels  5.77 us (3%)
  local copies, waits for them, and re-layouts  5.45 us (3%)
  waiting for transfers between devices  4.62 us (3%)
  other arithmetic  2.35 us (1%)
    all_to_all x1, blocking collectives, per_device(): rot = summed(mixed(part.reshape(16, queries // 16, width))).astype(bf16)  43.9 us
    all_to_all x1, blocking collectives, per_device(): own = mixed(spread(rot, 16)).reshape(queries, width)  40.3 us
    all_to_all x1, blocking collectives, per_device(): lax.all_to_all(partial_out.reshape(16, train // 16, half), ROW, 0, 0, til...  24.1 us
    all_to_all x1, blocking collectives, per_device(): lax.all_to_all(spread(inner_part, 16), CHIPS, 0, 0, tiled=True)  16.6 us
    all_to_all x1, blocking collectives, per_device(): lax.all_to_all(partial_inner.reshape(16, train // 16, half), CHIPS, 0, 0,...  16.1 us
    ppermute x1, starting transfers between devices, per_device(): basis_in_o = lax.ppermute(basis_in, 'core', [(1, 0)])  8.84 us
    pallas_call x3, Pallas kernels, call(): pl.pallas_call(kernel, out_shape=jax.ShapeDtypeStruct(shape, bf16), in_sp...  5.77 us
    unnamed x14, local copies, waits for them, and re-layouts  5.01 us
  transfers between devices with their start and end apart: 6, of which 2 were waited for; matrix products, arithmetic and copies ran while one was open for 1% of the time, Pallas kernels for 0%

profile of v1, /device:TPU:1, one launch (start us, length us, event | category | flops | bytes accessed | tf_op | source)
XLA Modules:
  0.0 180.1 jit_solution(5886099130406205373)
XLA Ops:
  0.0 8.8 %collective-permute-start = (bf16[1024,512]{1,0:T(8,128)(2,1)}, bf16[1024,512]{1,0:T(8,128)(2,1)S(1)}, u32[]{:S(2)}, u32[]{:S(2)}) collective-permute-start(bf16[1024,512]{1,0:T(8,128)(2,1)} %b_in.1), channel_id=1, source_target_pairs={{1,0},{3,2},{5,4},{7,6},{9,8},{11,10},{13,12},{15,14},{17,16},{19,... | collective-permute-start | bytes 3145736 | tf_op jit(solution)/shard_map/ppermute | solution.py:145
  8.8 1.3 collective-permute-start.2
  10.1 1.3 collective-permute-start.1
  11.4 3.3 %collective-permute-done.1.grad_o = bf16[768,512]{1,0:T(8,128)(2,1)S(1)} collective-permute-done((bf16[768,512]{1,0:T(8,128)(2,1)}, bf16[768,512]{1,0:T(8,128)(2,1)S(1)}, u32[]{:S(2)}, u32[]{:S(2)}) %collective-permute-start.1) | collective-permute-done | bytes 786464 | tf_op jit(solution)/shard_map/ppermute | solution.py:147
  14.7 1.2 copy-done
  16.0 1.4 copy-done.2
  17.4 1.2 copy-done.3
  18.6 1.1 copy-done.4
  19.7 2.1 %shard_map.73 = bf16[768,1024]{1,0:T(8,128)(2,1)S(1)} custom-call(s32[1]{0:T(128)} %bitcast.core, bf16[768,1024]{1,0:T(8,128)(2,1)S(1)} %copy-done.2, bf16[768,512]{1,0:T(8,128)(2,1)S(1)} %copy-done.4, bf16[1024,512]{1,0:T(8,128)(2,1)S(1)} %copy-done.3, bf16[512,1024]{1,0:T(8,128)(2,1)S(1)} %copy-done, bf16[1024,512]{1,0:T(8,128)(2,1)S(1)} %collective-permute-done.b_in_o, ...), custom_call_target="tpu_custom_call" | custom-call | flops 1610612736 | bytes 4194304 | tf_op jit(solution)/shard_map/pallas_call | solution.py:110
  21.9 43.9 %all_to_all.25 = bf16[16,48,1024]{2,1,0:T(8,128)(2,1)S(1)} all-to-all(bf16[16,48,1024]{2,1,0:T(8,128)(2,1)S(1)} %bitcast.11), channel_id=1, replica_groups={{0,32,64,96,128,160,192,224,256,288,320,352,384,416,448,480},{2,34,66,9..., dimensions={0} | all-to-all | bytes 3145728 | tf_op jit(solution)/shard_map/all_to_all | solution.py:157
  65.8 0.3 reduce_sum.50
  66.3 40.3 %all_to_all.26 = bf16[16,48,1024]{2,1,0:T(8,128)(2,1)S(1)} all-to-all(bf16[16,48,1024]{2,1,0:T(8,128)(2,1)S(1)} %broadcast_in_dim.8), channel_id=1, replica_groups={{0,32,64,96,128,160,192,224,256,288,320,352,384,416,448,480},{2,34,66,9..., dimensions={0} | all-to-all | bytes 3145728 | tf_op jit(solution)/shard_map/all_to_all | solution.py:158
  106.7 1.9 %collective-permute-start.3 = (bf16[768,1024]{1,0:T(8,128)(2,1)S(1)}, bf16[768,1024]{1,0:T(8,128)(2,1)S(1)}, u32[]{:S(2)}, u32[]{:S(2)}) collective-permute-start(bf16[768,1024]{1,0:T(8,128)(2,1)S(1)} %bitcast.9), channel_id=1, source_target_pairs={{0,1},{1,0},{2,3},{3,2},{4,5},{5,4},{6,7},{7,6},{8,9},{9,8},{10,11... | collective-permute-start | bytes 4718600 | tf_op jit(solution)/shard_map/ppermute | solution.py:159
  108.6 2.4 %collective-permute-start.4 = (bf16[384,512]{1,0:T(8,128)(2,1)}, bf16[384,512]{1,0:T(8,128)(2,1)}, u32[]{:S(2)}, u32[]{:S(2)}) collective-permute-start(bf16[384,512]{1,0:T(8,128)(2,1)} %train.1), channel_id=1, source_target_pairs={{0,1},{1,0},{2,3},{3,2},{4,5},{5,4},{6,7},{7,6},{8,9},{9,8},{10,11... | collective-permute-start | bytes 1179656 | tf_op jit(solution)/shard_map/ppermute | solution.py:148
  111.0 0.7 reduce_sum.48
  111.7 0.6 reduce_sum.49
  113.9 3.0 %shard_map.74 = bf16[384,512]{1,0:T(8,128)(2,1)S(1)} custom-call(s32[1]{0:T(128)} %bitcast.core, f32[1]{0:T(128)} %bitcast.1.damp, bf16[768,1024]{1,0:T(8,128)(2,1)S(1)} %bitcast.10, bf16[768,1024]{1,0:T(8,128)(2,1)S(1)} %collective-permute-done.3.other, bf16[384,512]{1,0:T(8,128)(2,1)} %train.1, bf16[384,512]{1,0:T(8,128)(2,1)} %collective-permute-done.4.train_o, ...), custom_call_target="tpu_custom_call" | custom-call | flops 1207959552 | bytes 4194304 | tf_op jit(solution)/shard_map/pallas_call | solution.py:110
  116.9 16.1 %all_to_all.27 = bf16[16,24,512]{2,1,0:T(8,128)(2,1)S(1)} all-to-all(bf16[16,24,512]{2,1,0:T(8,128)(2,1)S(1)} %bitcast.14), channel_id=1, replica_groups=mesh['z_hi'=2,'y'=8,'x'=4,'z_lo'=4,'core'=2] {'x','z_lo'}, dimensions={0} | all-to-all | bytes 786432 | tf_op jit(solution)/shard_map/all_to_all | solution.py:173
  133.2 16.6 %all_to_all.28 = bf16[16,24,512]{2,1,0:T(8,128)(2,1)S(1)} all-to-all(bf16[16,24,512]{2,1,0:T(8,128)(2,1)S(1)} %broadcast_in_dim.21), channel_id=1, replica_groups=mesh['z_hi'=2,'y'=8,'x'=4,'z_lo'=4,'core'=2] {'x','z_lo'}, dimensions={0} | all-to-all | bytes 786432 | tf_op jit(solution)/shard_map/all_to_all | solution.py:178
  149.8 3.6 %collective-permute-start.5 = (bf16[384,512]{1,0:T(8,128)(2,1)S(1)}, bf16[384,512]{1,0:T(8,128)(2,1)S(1)}, u32[]{:S(2)}, u32[]{:S(2)}) collective-permute-start(bf16[384,512]{1,0:T(8,128)(2,1)S(1)} %bitcast.12), channel_id=1, source_target_pairs={{0,1},{1,0},{2,3},{3,2},{4,5},{5,4},{6,7},{7,6},{8,9},{9,8},{10,11... | collective-permute-start | bytes 1179656 | tf_op jit(solution)/shard_map/ppermute | solution.py:179
  153.4 1.3 collective-permute-done.5.other
  154.7 0.6 shard_map.75
  155.3 24.1 %all_to_all.29 = bf16[16,24,512]{2,1,0:T(8,128)(2,1)S(1)} all-to-all(bf16[16,24,512]{2,1,0:T(8,128)(2,1)S(1)} %bitcast.15), channel_id=1, replica_groups=mesh['z_hi'=2,'y'=8,'x'=4,'z_lo'=4,'core'=2] {'z_hi','y'}, dimensions={0} | all-to-all | bytes 786432 | tf_op jit(solution)/shard_map/all_to_all | solution.py:188
  179.4 0.7 convert_reduce_fusion
  (21 shorter events, 0.5 us)
Async XLA Ops:
  0.0 14.7 %collective-permute-start = (bf16[1024,512]{1,0:T(8,128)(2,1)}, bf16[1024,512]{1,0:T(8,128)(2,1)S(1)}, u32[]{:S(2)}, u32[]{:S(2)}) collective-permute-start(bf16[1024,512]{1,0:T(8,128)(2,1)} %b_in.1), channel_id=1, source_target_pairs={{1,0},{3,2},{5,4},{7,6},{9,8},{11,10},{13,12},{15,14},{17,16},{19,... | collective-permute-start | bytes 3145736 | tf_op jit(solution)/shard_map/ppermute | solution.py:145
  8.8 5.9 %collective-permute-start.2 = (bf16[512,1024]{1,0:T(8,128)(2,1)}, bf16[512,1024]{1,0:T(8,128)(2,1)S(1)}, u32[]{:S(2)}, u32[]{:S(2)}) collective-permute-start(bf16[512,1024]{1,0:T(8,128)(2,1)} %b_out.3), channel_id=1, source_target_pairs={{0,1},{2,3},{4,5},{6,7},{8,9},{10,11},{12,13},{14,15},{16,17},{18,... | collective-permute-start | bytes 3145736 | tf_op jit(solution)/shard_map/ppermute | solution.py:146
  10.1 4.6 %collective-permute-start.1 = (bf16[768,512]{1,0:T(8,128)(2,1)}, bf16[768,512]{1,0:T(8,128)(2,1)S(1)}, u32[]{:S(2)}, u32[]{:S(2)}) collective-permute-start(bf16[768,512]{1,0:T(8,128)(2,1)} %grad.1), channel_id=1, source_target_pairs={{0,1},{2,3},{4,5},{6,7},{8,9},{10,11},{12,13},{14,15},{16,17},{18,... | collective-permute-start | bytes 2359304 | tf_op jit(solution)/shard_map/ppermute | solution.py:147
  14.7 1.2 copy-start
  16.0 1.4 copy-start.2
  17.4 1.2 copy-start.3
  18.6 1.1 copy-start.4
  66.3 44.7 %copy-start.5 = (f32[16384]{0:T(1024)S(1)}, f32[16384]{0:T(1024)}, u32[]{:S(2)}) copy-start(f32[16384]{0:T(1024)} %param.12) | copy-start | bytes 196612
  66.3 45.4 %copy-start.6 = (f32[16384]{0:T(1024)S(1)}, f32[16384]{0:T(1024)}, u32[]{:S(2)}) copy-start(f32[16384]{0:T(1024)} %param.13) | copy-start | bytes 196612
  106.7 7.2 %collective-permute-start.3 = (bf16[768,1024]{1,0:T(8,128)(2,1)S(1)}, bf16[768,1024]{1,0:T(8,128)(2,1)S(1)}, u32[]{:S(2)}, u32[]{:S(2)}) collective-permute-start(bf16[768,1024]{1,0:T(8,128)(2,1)S(1)} %bitcast.9), channel_id=1, source_target_pairs={{0,1},{1,0},{2,3},{3,2},{4,5},{5,4},{6,7},{7,6},{8,9},{9,8},{10,11... | collective-permute-start | bytes 4718600 | tf_op jit(solution)/shard_map/ppermute | solution.py:159
  108.6 5.2 %collective-permute-start.4 = (bf16[384,512]{1,0:T(8,128)(2,1)}, bf16[384,512]{1,0:T(8,128)(2,1)}, u32[]{:S(2)}, u32[]{:S(2)}) collective-permute-start(bf16[384,512]{1,0:T(8,128)(2,1)} %train.1), channel_id=1, source_target_pairs={{0,1},{1,0},{2,3},{3,2},{4,5},{5,4},{6,7},{7,6},{8,9},{9,8},{10,11... | collective-permute-start | bytes 1179656 | tf_op jit(solution)/shard_map/ppermute | solution.py:148
  116.9 37.8 %copy-start.1 = (bf16[512,1024]{1,0:T(8,128)(2,1)S(1)}, bf16[512,1024]{1,0:T(8,128)(2,1)}, u32[]{:S(2)}) copy-start(bf16[512,1024]{1,0:T(8,128)(2,1)} %b_out.3) | copy-start | bytes 3145732
  149.8 4.9 %collective-permute-start.5 = (bf16[384,512]{1,0:T(8,128)(2,1)S(1)}, bf16[384,512]{1,0:T(8,128)(2,1)S(1)}, u32[]{:S(2)}, u32[]{:S(2)}) collective-permute-start(bf16[384,512]{1,0:T(8,128)(2,1)S(1)} %bitcast.12), channel_id=1, source_target_pairs={{0,1},{1,0},{2,3},{3,2},{4,5},{5,4},{6,7},{7,6},{8,9},{9,8},{10,11... | collective-permute-start | bytes 1179656 | tf_op jit(solution)/shard_map/ppermute | solution.py:179

commit v2 on v1

--- a/solution.py
+++ b/solution.py
@@ -23,10 +23,18 @@
 
 
 def mixed_groups():
-    ids = np.arange(np.prod(SIZES)).reshape(16, 16, 2)
-    along_row = [ids[:, c, 0].tolist() for c in range(16)]
-    along_col = [ids[r, :, 1].tolist() for r in range(16)]
+    ids = np.arange(np.prod(SIZES)).reshape(2, 8, 4, 2, 2, 2)
+    along_row = ids[..., 0].transpose(0, 2, 3, 4, 1).reshape(-1, 8).tolist()
+    along_col = ids[..., 1].transpose(0, 1, 3, 2, 4).reshape(-1, 8).tolist()
     return along_row + along_col
+
+
+def mixed_pairs():
+    ids = np.arange(np.prod(SIZES)).reshape(2, 8, 4, 2, 2, 2)
+    to = np.empty_like(ids)
+    to[..., 0] = ids[::-1, ..., 0]
+    to[..., 1] = ids[:, :, :, ::-1, :, 1]
+    return list(zip(ids.reshape(-1).tolist(), to.reshape(-1).tolist()))
 
 
 def dot(a, b):
@@ -41,26 +49,44 @@
     return lax.dot_general(a, b, (((0,), (0,)), ((), ())), preferred_element_type=f32)
 
 
-def rotate_kernel(core, act, grad, b_in, b_out, b_in_o, grad_o, b_out_o, out):
-    tile = 256
-    half = b_in.shape[1]
+TILE = 256
+
+
+def rotate_kernel(core, b_in_o, grad_o, b_out_o, act, grad, b_in, b_out, out, left, in_w, out_w, sems):
+    half = grad_o.shape[1]
+    steps = left.shape[0] // TILE
+
+    def bring(source, held, weight, room):
+        load = pltpu.make_async_copy(weight, room, sems.at[steps])
+        rows = [
+            pltpu.make_async_copy(
+                source.at[pl.ds(m * TILE, TILE)], held.at[pl.ds(m * TILE, TILE)], sems.at[m]
+            )
+            for m in range(steps)
+        ]
+        rows[0].start()
+        load.start()
+        for copy in rows[1:]:
+            copy.start()
+        rows[0].wait()
+        load.wait()
+        for m, copy in enumerate(rows):
+            if m:
+                copy.wait()
+            yield pl.ds(m * TILE, TILE)
 
     @pl.when(core[0] == 0)
     def _():
-        @pl.loop(0, act.shape[0] // tile)
-        def _(m):
-            rows = pl.ds(pl.multiple_of(m * tile, tile), tile)
-            left = act[rows, :]
-            out[rows, :half] = dot(left, b_in[...]).astype(bf16)
-            out[rows, half:] = dot(left, b_in_o[...]).astype(bf16)
+        for rows in bring(act, left, b_in, in_w):
+            out[rows, :half] = dot(left[rows, :], in_w[...]).astype(bf16)
+            out[rows, half:] = dot(left[rows, :], b_in_o[...]).astype(bf16)
 
     @pl.when(core[0] == 1)
     def _():
-        @pl.loop(0, act.shape[0] // tile)
-        def _(m):
-            rows = pl.ds(pl.multiple_of(m * tile, tile), tile)
+        held = left.at[:, :half]
+        for rows in bring(grad, held, b_out, out_w):
             out[rows, :] = (
-                dot(grad_o[rows, :], b_out_o[...]) + dot(grad[rows, :], b_out[...])
+                dot(grad_o[rows, :], b_out_o[...]) + dot(held[rows, :], out_w[...])
             ).astype(bf16)
 
 
@@ -106,14 +132,18 @@
         body(other, own)
 
 
-def call(kernel, shape, scalars, arrays, flops):
+def call(kernel, shape, scalars, arrays, flops, far=0, scratch=()):
+    anywhere = pl.BlockSpec(memory_space=pl.ANY)
+    in_vmem = pl.BlockSpec(memory_space=pltpu.VMEM)
     return pl.pallas_call(
         kernel,
         out_shape=jax.ShapeDtypeStruct(shape, bf16),
         in_specs=[pl.BlockSpec(memory_space=pltpu.SMEM)] * len(scalars)
-        + [pl.BlockSpec(memory_space=pltpu.VMEM)] * len(arrays),
-        out_specs=pl.BlockSpec(memory_space=pltpu.VMEM),
-        compiler_params=pltpu.CompilerParams(vmem_limit_bytes=32 * 1024 * 1024),
+        + [in_vmem] * (len(arrays) - far)
+        + [anywhere] * far,
+        out_specs=in_vmem,
+        scratch_shapes=scratch,
+        compiler_params=pltpu.CompilerParams(vmem_limit_bytes=(51 if far else 32) * 1024 * 1024),
         cost_estimate=pl.CostEstimate(flops=flops, bytes_accessed=4 << 20, transcendentals=0),
     )(*scalars, *arrays)
 
@@ -145,24 +175,37 @@
     basis_in_o = lax.ppermute(basis_in, "core", [(1, 0)])
     basis_out_o = lax.ppermute(basis_out, "core", [(0, 1)])
     grad_o = lax.ppermute(query_grad, "core", [(0, 1)])
-    train_o = lax.ppermute(train_rot, "core", SWAP)
 
     part = call(
         rotate_kernel,
         (queries, width),
         (core,),
-        (query_act, query_grad, basis_in, basis_out, basis_in_o, grad_o, basis_out_o),
+        (basis_in_o, grad_o, basis_out_o, query_act, query_grad, basis_in, basis_out),
         2 * queries * width * width,
-    )
-    rot = summed(mixed(part.reshape(16, queries // 16, width))).astype(bf16)
-    own = mixed(spread(rot, 16)).reshape(queries, width)
-    other = lax.ppermute(own, "core", SWAP)
-
+        far=4,
+        scratch=(
+            pltpu.VMEM((queries, width), bf16),
+            pltpu.VMEM((width, half), bf16),
+            pltpu.VMEM((half, width), bf16),
+            pltpu.SemaphoreType.DMA((queries // TILE + 1,)),
+        ),
+    )
     damp = damping_share * jnp.mean(eig_in) * jnp.mean(eig_out)
     out_start = lax.axis_index(ROW) * width + core_id * half
     in_start = lax.axis_index(CHIPS) * width
     e_out = lax.dynamic_slice_in_dim(eig_out, out_start, half, 0)[:, None]
     e_in = lax.dynamic_slice_in_dim(eig_in, in_start, width, 0)[None, :]
+    part, damp, e_out, e_in = lax.optimization_barrier((part, damp, e_out, e_in))
+
+    eighth = summed(mixed(part.reshape(8, queries // 8, width)))
+    eighth, train_rot = lax.optimization_barrier((eighth, train_rot))
+    far_sum = lax.ppermute(eighth.astype(bf16), ALL, mixed_pairs())
+    train_o = lax.ppermute(train_rot, "core", SWAP)
+    rot = (eighth + far_sum.astype(f32)).astype(bf16)
+    rot, train_o = lax.optimization_barrier((rot, train_o))
+    own = mixed(spread(rot, 8)).reshape(queries, width)
+    other = lax.ppermute(own, "core", SWAP)
+
     partial_inner = call(
         functools.partial(outer_kernel, queries),
         (train, half),

time: 182 us -> 171 us (0.940)
  blocking collectives: 141 us -> 91.9 us
  starting transfers between devices: 19.4 us -> 51.6 us
  Pallas kernels: 5.77 us -> 8.29 us
    all_to_all x2, blocking collectives: 84.3 us -> 34.8 us  [the longest x1 17.9 us: per_device(): own = mixed(spread(rot, 8)).reshape(queries, width)]
    ppermute x1, starting transfers between devices: 2.41 us -> 21 us  [per_device(): train_o = lax.ppermute(train_rot, 'core', SWAP)]
    ppermute x1, starting transfers between devices: 1.91 us -> 13 us  [per_device(): other = lax.ppermute(own, 'core', SWAP)]
    ppermute x1, waiting for transfers between devices: 3.29 us -> 0.01 us  [per_device(): grad_o = lax.ppermute(query_grad, 'core', [(0, 1)])]
    all_to_all x1, blocking collectives: 16.1 us -> 19.4 us  [per_device(): lax.all_to_all(partial_inner.reshape(16, train // 16, half), CHIPS, 0, 0,...]
    ppermute x1, waiting for transfers between devices: 0.01 us -> 2.86 us  [per_device(): other = lax.ppermute(own, 'core', SWAP)]
    all_to_all x1, blocking collectives: 24.1 us -> 21.4 us  [per_device(): lax.all_to_all(partial_out.reshape(16, train // 16, half), ROW, 0, 0, til...]
    pallas_call x3, Pallas kernels: 5.77 us -> 8.29 us  [call(): pl.pallas_call(kernel, out_shape=jax.ShapeDtypeStruct(shape, bf16), in_sp...]
  transfers between devices with their start and end apart: 6 -> 7, of which waited for: 2 -> 3; matrix products, arithmetic and copies ran while one was open for 1% -> 3% of each run, Pallas kernels for 0% -> 0%
where the time goes in v2:
time: 171 us; the launch traced here: 169 us
  blocking collectives  91.9 us (54%)
  starting transfers between devices  51.6 us (30%)
  Pallas kernels  8.29 us (5%)
  local copies, waits for them, and re-layouts  6.63 us (4%)
  waiting for transfers between devices  5.47 us (3%)
  other arithmetic  4.07 us (2%)
    all_to_all x1, blocking collectives, per_device(): lax.all_to_all(partial_out.reshape(16, train // 16, half), ROW, 0, 0, til...  21.4 us
    ppermute x1, starting transfers between devices, per_device(): train_o = lax.ppermute(train_rot, 'core', SWAP)  21 us
    all_to_all x1, blocking collectives, per_device(): lax.all_to_all(partial_inner.reshape(16, train // 16, half), CHIPS, 0, 0,...  19.4 us
    all_to_all x1, blocking collectives, per_device(): own = mixed(spread(rot, 8)).reshape(queries, width)  17.9 us
    all_to_all x1, blocking collectives, per_device(): eighth = summed(mixed(part.reshape(8, queries // 8, width)))  17 us
    all_to_all x1, blocking collectives, per_device(): lax.all_to_all(spread(inner_part, 16), CHIPS, 0, 0, tiled=True)  16.3 us
    ppermute x1, starting transfers between devices, per_device(): other = lax.ppermute(own, 'core', SWAP)  13 us
    ppermute x1, starting transfers between devices, per_device(): basis_in_o = lax.ppermute(basis_in, 'core', [(1, 0)])  8.84 us
  transfers between devices with their start and end apart: 7, of which 3 were waited for; matrix products, arithmetic and copies ran while one was open for 3% of the time, Pallas kernels for 0%

profile of v2, /device:TPU:1, one launch (start us, length us, event | category | flops | bytes accessed | tf_op | source)
XLA Modules:
  0.0 169.4 jit_solution(5407472133474823449)
XLA Ops:
  0.0 8.8 %collective-permute-start = (bf16[1024,512]{1,0:T(8,128)(2,1)}, bf16[1024,512]{1,0:T(8,128)(2,1)S(1)}, u32[]{:S(2)}, u32[]{:S(2)}) collective-permute-start(bf16[1024,512]{1,0:T(8,128)(2,1)} %b_in.1), channel_id=1, source_target_pairs={{1,0},{3,2},{5,4},{7,6},{9,8},{11,10},{13,12},{15,14},{17,16},{19,... | collective-permute-start | bytes 3145736 | tf_op jit(solution)/shard_map/ppermute | solution.py:175
  8.8 1.3 collective-permute-start.2
  10.1 1.3 collective-permute-start.1
  11.5 1.5 reduce_sum.45
  13.0 1.5 reduce_sum.46
  14.5 0.8 dynamic_slice.6
  17.2 1.0 copy-done.6
  18.2 1.1 copy-done.1
  19.3 5.8 %shard_map.73 = bf16[768,1024]{1,0:T(8,128)(2,1)} custom-call(s32[1]{0:T(128)} %bitcast.core, bf16[1024,512]{1,0:T(8,128)(2,1)S(1)} %collective-permute-done.b_in_o, bf16[768,512]{1,0:T(8,128)(2,1)S(1)} %collective-permute-done.1.grad_o, bf16[512,1024]{1,0:T(8,128)(2,1)} %copy-done.6, bf16[768,1024]{1,0:T(8,128)(2,1)} %act.1, ...), custom_call_target="tpu_custom_call" | custom-call | flops 1610612736 | bytes 4194304 | tf_op jit(solution)/shard_map/pallas_call | solution.py:138
  25.1 17.0 %all_to_all.25 = bf16[8,96,1024]{2,1,0:T(8,128)(2,1)S(1)} all-to-all(bf16[8,96,1024]{2,1,0:T(8,128)(2,1)} %bitcast.16), channel_id=1, replica_groups={{0,32,64,96,128,160,192,224},{2,34,66,98,130,162,194,226},{4,36,68,100,..., dimensions={0} | all-to-all | bytes 3145728 | tf_op jit(solution)/shard_map/all_to_all | solution.py:200
  42.3 2.5 %collective-permute-start.3 = (bf16[96,1024]{1,0:T(8,128)(2,1)S(1)}, bf16[96,1024]{1,0:T(8,128)(2,1)S(1)}, u32[]{:S(2)}, u32[]{:S(2)}) collective-permute-start(bf16[96,1024]{1,0:T(8,128)(2,1)S(1)} %convert_element_type.26), channel_id=1, source_target_pairs={{0,256},{1,5},{2,258},{3,7},{4,260},{5,1},{6,262},{7,3},{8,264},{9... | collective-permute-start | bytes 589832 | tf_op jit(solution)/shard_map/ppermute | solution.py:202
  44.8 21.0 %collective-permute-start.4 = (bf16[384,512]{1,0:T(8,128)(2,1)S(1)}, bf16[384,512]{1,0:T(8,128)(2,1)S(1)}, u32[]{:S(2)}, u32[]{:S(2)}) collective-permute-start(bf16[384,512]{1,0:T(8,128)(2,1)S(1)} %copy-done.2), channel_id=1, source_target_pairs={{0,1},{1,0},{2,3},{3,2},{4,5},{5,4},{6,7},{7,6},{8,9},{9,8},{10,11... | collective-permute-start | bytes 1179656 | tf_op jit(solution)/shard_map/ppermute | solution.py:203
  65.9 1.3 collective-permute-done.4.train_o
  68.1 17.9 %all_to_all.26 = bf16[8,96,1024]{2,1,0:T(8,128)(2,1)S(1)} all-to-all(bf16[8,96,1024]{2,1,0:T(8,128)(2,1)S(1)} %broadcast_in_dim.20), channel_id=1, replica_groups={{0,32,64,96,128,160,192,224},{2,34,66,98,130,162,194,226},{4,36,68,100,..., dimensions={0} | all-to-all | bytes 3145728 | tf_op jit(solution)/shard_map/all_to_all | solution.py:206
  86.0 13.0 %collective-permute-start.5 = (bf16[768,1024]{1,0:T(8,128)(2,1)S(1)}, bf16[768,1024]{1,0:T(8,128)(2,1)S(1)}, u32[]{:S(2)}, u32[]{:S(2)}) collective-permute-start(bf16[768,1024]{1,0:T(8,128)(2,1)S(1)} %bitcast.9), channel_id=1, source_target_pairs={{0,1},{1,0},{2,3},{3,2},{4,5},{5,4},{6,7},{7,6},{8,9},{9,8},{10,11... | collective-permute-start | bytes 4718600 | tf_op jit(solution)/shard_map/ppermute | solution.py:207
  99.2 2.9 %collective-permute-done.5.other = bf16[768,1024]{1,0:T(8,128)(2,1)S(1)} collective-permute-done((bf16[768,1024]{1,0:T(8,128)(2,1)S(1)}, bf16[768,1024]{1,0:T(8,128)(2,1)S(1)}, u32[]{:S(2)}, u32[]{:S(2)}) %collective-permute-start.5) | collective-permute-done | bytes 1572896 | tf_op jit(solution)/shard_map/ppermute | solution.py:207
  102.1 1.0 copy-done.3
  103.1 1.0 copy-done.5
  104.1 1.9 %shard_map.74 = bf16[384,512]{1,0:T(8,128)(2,1)S(1)} custom-call(s32[1]{0:T(128)} %bitcast.core, f32[1]{0:T(128)} %bitcast.3.damp, bf16[768,1024]{1,0:T(8,128)(2,1)S(1)} %bitcast.10, bf16[768,1024]{1,0:T(8,128)(2,1)S(1)} %collective-permute-done.5.other, bf16[384,512]{1,0:T(8,128)(2,1)S(1)} %copy-done.3, bf16[384,512]{1,0:T(8,128)(2,1)S(1)} %copy-done.5, ...), custom_call_target="tpu_custom_call" | custom-call | flops 1207959552 | bytes 4194304 | tf_op jit(solution)/shard_map/pallas_call | solution.py:138
  106.0 19.4 %all_to_all.27 = bf16[16,24,512]{2,1,0:T(8,128)(2,1)S(1)} all-to-all(bf16[16,24,512]{2,1,0:T(8,128)(2,1)S(1)} %bitcast.13), channel_id=1, replica_groups=mesh['z_hi'=2,'y'=8,'x'=4,'z_lo'=4,'core'=2] {'x','z_lo'}, dimensions={0} | all-to-all | bytes 786432 | tf_op jit(solution)/shard_map/all_to_all | solution.py:216
  125.5 16.3 %all_to_all.28 = bf16[16,24,512]{2,1,0:T(8,128)(2,1)S(1)} all-to-all(bf16[16,24,512]{2,1,0:T(8,128)(2,1)S(1)} %broadcast_in_dim.21), channel_id=1, replica_groups=mesh['z_hi'=2,'y'=8,'x'=4,'z_lo'=4,'core'=2] {'x','z_lo'}, dimensions={0} | all-to-all | bytes 786432 | tf_op jit(solution)/shard_map/all_to_all | solution.py:221
  141.8 3.7 %collective-permute-start.6 = (bf16[384,512]{1,0:T(8,128)(2,1)S(1)}, bf16[384,512]{1,0:T(8,128)(2,1)S(1)}, u32[]{:S(2)}, u32[]{:S(2)}) collective-permute-start(bf16[384,512]{1,0:T(8,128)(2,1)S(1)} %bitcast.11), channel_id=1, source_target_pairs={{0,1},{1,0},{2,3},{3,2},{4,5},{5,4},{6,7},{7,6},{8,9},{9,8},{10,11... | collective-permute-start | bytes 1179656 | tf_op jit(solution)/shard_map/ppermute | solution.py:222
  145.4 1.3 collective-permute-done.6.other
  147.4 21.4 %all_to_all.29 = bf16[16,24,512]{2,1,0:T(8,128)(2,1)S(1)} all-to-all(bf16[16,24,512]{2,1,0:T(8,128)(2,1)S(1)} %bitcast.14), channel_id=1, replica_groups=mesh['z_hi'=2,'y'=8,'x'=4,'z_lo'=4,'core'=2] {'z_hi','y'}, dimensions={0} | all-to-all | bytes 786432 | tf_op jit(solution)/shard_map/all_to_all | solution.py:231
  (25 shorter events, 3.5 us)
Async XLA Ops:
  0.0 17.2 %collective-permute-start = (bf16[1024,512]{1,0:T(8,128)(2,1)}, bf16[1024,512]{1,0:T(8,128)(2,1)S(1)}, u32[]{:S(2)}, u32[]{:S(2)}) collective-permute-start(bf16[1024,512]{1,0:T(8,128)(2,1)} %b_in.1), channel_id=1, source_target_pairs={{1,0},{3,2},{5,4},{7,6},{9,8},{11,10},{13,12},{15,14},{17,16},{19,... | collective-permute-start | bytes 3145736 | tf_op jit(solution)/shard_map/ppermute | solution.py:175
  8.8 8.3 %collective-permute-start.2 = (bf16[512,1024]{1,0:T(8,128)(2,1)}, bf16[512,1024]{1,0:T(8,128)(2,1)S(1)}, u32[]{:S(2)}, u32[]{:S(2)}) collective-permute-start(bf16[512,1024]{1,0:T(8,128)(2,1)} %b_out.3), channel_id=1, source_target_pairs={{0,1},{2,3},{4,5},{6,7},{8,9},{10,11},{12,13},{14,15},{16,17},{18,... | collective-permute-start | bytes 3145736 | tf_op jit(solution)/shard_map/ppermute | solution.py:176
  10.1 7.0 %collective-permute-start.1 = (bf16[768,512]{1,0:T(8,128)(2,1)}, bf16[768,512]{1,0:T(8,128)(2,1)S(1)}, u32[]{:S(2)}, u32[]{:S(2)}) collective-permute-start(bf16[768,512]{1,0:T(8,128)(2,1)} %grad.1), channel_id=1, source_target_pairs={{0,1},{2,3},{4,5},{6,7},{8,9},{10,11},{12,13},{14,15},{16,17},{18,... | collective-permute-start | bytes 2359304 | tf_op jit(solution)/shard_map/ppermute | solution.py:177
  17.2 1.0 copy-start.6
  18.2 1.1 copy-start.1
  42.0 2.8 %copy-start.2 = (bf16[384,512]{1,0:T(8,128)(2,1)S(1)}, bf16[384,512]{1,0:T(8,128)(2,1)}, u32[]{:S(2)}) copy-start(bf16[384,512]{1,0:T(8,128)(2,1)} %train) | copy-start | bytes 1179652
  42.3 23.5 %collective-permute-start.3 = (bf16[96,1024]{1,0:T(8,128)(2,1)S(1)}, bf16[96,1024]{1,0:T(8,128)(2,1)S(1)}, u32[]{:S(2)}, u32[]{:S(2)}) collective-permute-start(bf16[96,1024]{1,0:T(8,128)(2,1)S(1)} %convert_element_type.26), channel_id=1, source_target_pairs={{0,256},{1,5},{2,258},{3,7},{4,260},{5,1},{6,262},{7,3},{8,264},{9... | collective-permute-start | bytes 589832 | tf_op jit(solution)/shard_map/ppermute | solution.py:202
  44.8 22.4 %collective-permute-start.4 = (bf16[384,512]{1,0:T(8,128)(2,1)S(1)}, bf16[384,512]{1,0:T(8,128)(2,1)S(1)}, u32[]{:S(2)}, u32[]{:S(2)}) collective-permute-start(bf16[384,512]{1,0:T(8,128)(2,1)S(1)} %copy-done.2), channel_id=1, source_target_pairs={{0,1},{1,0},{2,3},{3,2},{4,5},{5,4},{6,7},{7,6},{8,9},{9,8},{10,11... | collective-permute-start | bytes 1179656 | tf_op jit(solution)/shard_map/ppermute | solution.py:203
  67.2 0.7 copy-start.4
  86.0 16.0 %collective-permute-start.5 = (bf16[768,1024]{1,0:T(8,128)(2,1)S(1)}, bf16[768,1024]{1,0:T(8,128)(2,1)S(1)}, u32[]{:S(2)}, u32[]{:S(2)}) collective-permute-start(bf16[768,1024]{1,0:T(8,128)(2,1)S(1)} %bitcast.9), channel_id=1, source_target_pairs={{0,1},{1,0},{2,3},{3,2},{4,5},{5,4},{6,7},{7,6},{8,9},{9,8},{10,11... | collective-permute-start | bytes 4718600 | tf_op jit(solution)/shard_map/ppermute | solution.py:207
  102.1 1.0 copy-start.3
  103.1 1.0 copy-start.5
  106.0 40.8 %copy-start = (bf16[512,1024]{1,0:T(8,128)(2,1)S(1)}, bf16[512,1024]{1,0:T(8,128)(2,1)}, u32[]{:S(2)}) copy-start(bf16[512,1024]{1,0:T(8,128)(2,1)} %b_out.3) | copy-start | bytes 3145732
  141.8 5.0 %collective-permute-start.6 = (bf16[384,512]{1,0:T(8,128)(2,1)S(1)}, bf16[384,512]{1,0:T(8,128)(2,1)S(1)}, u32[]{:S(2)}, u32[]{:S(2)}) collective-permute-start(bf16[384,512]{1,0:T(8,128)(2,1)S(1)} %bitcast.11), channel_id=1, source_target_pairs={{0,1},{1,0},{2,3},{3,2},{4,5},{5,4},{6,7},{7,6},{8,9},{9,8},{10,11... | collective-permute-start | bytes 1179656 | tf_op jit(solution)/shard_map/ppermute | solution.py:222

commit v3 on v1

v3 whole, which is shorter than its diff:
```python
import functools

import jax
import jax.numpy as jnp
import numpy as np
from jax import lax
from jax.experimental import pallas as pl
from jax.experimental.pallas import tpu as pltpu
from jax.sharding import Mesh
from jax.sharding import PartitionSpec as P

ROW = ("z_hi", "y")
CHIPS = ("x", "z_a", "z_b")
COL = (*CHIPS, "core")
ALL = ROW + COL
SIZES = (2, 8, 4, 2, 2, 2)
NEAR = ("x", "z_b")
SWAP = [(0, 1), (1, 0)]
MIB = 1024 * 1024

damping_share = 0.1

bf16 = jnp.bfloat16
f32 = jnp.float32

SMEM = pl.BlockSpec(memory_space=pltpu.SMEM)
VMEM = pl.BlockSpec(memory_space=pltpu.VMEM)
ANY = pl.BlockSpec(memory_space=pl.ANY)


def mixed_groups():
    ids = np.arange(np.prod(SIZES)).reshape(SIZES)
    along_row = ids[..., 0].transpose(0, 2, 3, 4, 1).reshape(-1, 8).tolist()
    along_col = ids[..., 1].transpose(0, 1, 3, 2, 4).reshape(-1, 8).tolist()
    return along_row + along_col


def mixed_pairs():
    ids = np.arange(np.prod(SIZES)).reshape(SIZES)
    to = np.empty_like(ids)
    to[..., 0] = ids[::-1, ..., 0]
    to[..., 1] = ids[:, :, :, ::-1, :, 1]
    return list(zip(ids.reshape(-1).tolist(), to.reshape(-1).tolist()))


def dot(a, b):
    return jnp.dot(a, b, preferred_element_type=f32)


def dot_nt(a, b):
    return lax.dot_general(a, b, (((1,), (1,)), ((), ())), preferred_element_type=f32)


def dot_tn(a, b):
    return lax.dot_general(a, b, (((0,), (0,)), ((), ())), preferred_element_type=f32)


TILE = 256


def damp_kernel(e_in, e_out, damp):
    damp[0] = (
        damping_share * (jnp.sum(e_in[...]) / e_in.size) * (jnp.sum(e_out[...]) / e_out.size)
    )


def rotate_kernel(place, act, grad, b_in, b_out, b_in_o, grad_o, b_out_o, first, second):
    half = grad.shape[1]
    tile = 128
    steps = first.shape[0] // tile

    def body(product):
        for index, out in enumerate((first, second)):

            @pl.loop(0, steps)
            def _(m):
                to = pl.ds(pl.multiple_of(m * tile, tile), tile)
                product(out, to, pl.ds(pl.multiple_of((index * steps + m) * tile, tile), tile))

    def joined(out, to, rows):
        out[to, :half] = dot(act[rows, :], b_in[...]).astype(bf16)
        out[to, half:] = dot(act[rows, :], b_in_o[...]).astype(bf16)

    def added(out, to, rows):
        out[to, :] = (dot(grad_o[rows, :], b_out_o[...]) + dot(grad[rows, :], b_out[...])).astype(bf16)

    @pl.when(place[0] == 0)
    def _():
        body(joined)

    @pl.when(place[0] == 1)
    def _():
        body(added)


def outer_kernel(queries, place, damp, own_a, own_b, other_a, other_b, train, train_o, e_out, e_in, out):
    half = train.shape[1]
    lanes = e_in.shape[1]
    units = 8 * lanes
    e_rows = e_in[pl.ds(pl.multiple_of(place[1] * 8, 8), 8), :]
    e_row = jnp.concatenate([e_rows[r : r + 1, :] for r in range(units // lanes)], axis=1)
    e_cols = jnp.transpose(e_out[pl.ds(pl.multiple_of(place[2] * 8, 8), 8), :])

    def body(acts, grads, first, left, right):
        for start in range(0, half, TILE):
            outer = sum(
                dot_tn(grad[:, first + start : first + start + TILE], act[...])
                for act, grad in zip(acts, grads)
            )
            r = (first + start) // lanes
            e_col = jnp.concatenate([e_cols[:, r + q : r + q + 1] for q in range(TILE // lanes)], axis=0)
            scaled = (outer / queries / (e_col * e_row + damp[0])).astype(bf16)
            out[:, start : start + TILE] = (
                dot_nt(left[...], scaled[:, :half]) + dot_nt(right[...], scaled[:, half:])
            ).astype(bf16)

    @pl.when(place[0] == 0)
    def _():
        body((own_a, own_b), (other_a, other_b), 0, train, train_o)

    @pl.when(place[0] == 1)
    def _():
        body((other_a, other_b), (own_a, own_b), half, train_o, train)


def back_kernel(place, own, other, b_out, out):
    half = own.shape[1]

    def body(left, right):
        out[...] = (
            dot_nt(left[...], b_out[:, :half]) + dot_nt(right[...], b_out[:, half:])
        ).astype(bf16)

    @pl.when(place[0] == 0)
    def _():
        body(own, other)

    @pl.when(place[0] == 1)
    def _():
        body(other, own)


def call(kernel, args, specs, shapes, out_specs, flops, limit, scratch=()):
    return pl.pallas_call(
        kernel,
        out_shape=shapes,
        in_specs=specs,
        out_specs=out_specs,
        scratch_shapes=scratch,
        compiler_params=pltpu.CompilerParams(vmem_limit_bytes=limit * MIB),
        cost_estimate=pl.CostEstimate(flops=flops, bytes_accessed=4 * MIB, transcendentals=0),
    )(*args)


def summed(pieces):
    return jnp.sum(pieces.astype(f32), axis=0)


def spread(array, n):
    return jnp.broadcast_to(array[None], (n, *array.shape))


def per_device(query_act, query_grad, train_rot, basis_in, basis_out, eig_in, eig_out):
    queries, train = query_act.shape[0], train_rot.shape[0]
    width, half = basis_in.shape
    mixed = functools.partial(
        lax.all_to_all,
        axis_name=ALL,
        split_axis=0,
        concat_axis=0,
        axis_index_groups=mixed_groups(),
        tiled=True,
    )
    near = functools.partial(
        lax.all_to_all, axis_name=NEAR, split_axis=0, concat_axis=0, tiled=True
    )
    shape = jax.ShapeDtypeStruct
    place = jnp.stack(
        [lax.axis_index("core"), lax.axis_index(CHIPS), lax.axis_index(ROW)]
    ).astype(jnp.int32)
    e_in, e_out = (e.reshape(-1, 128) for e in (eig_in, eig_out))

    basis_in_o = lax.ppermute(basis_in, "core", [(1, 0)])
    basis_out_o = lax.ppermute(basis_out, "core", [(0, 1)])
    grad_o = lax.ppermute(query_grad, "core", [(0, 1)])

    damp = call(
        damp_kernel,
        (e_in, e_out),
        [VMEM] * 2,
        shape((1,), f32),
        SMEM,
        6 * 10**9,
        8,
    )
    basis_in_o, basis_out_o, grad_o, damp = lax.optimization_barrier(
        (basis_in_o, basis_out_o, grad_o, damp)
    )
    first, second = call(
        rotate_kernel,
        (place, query_act, query_grad, basis_in, basis_out, basis_in_o, grad_o, basis_out_o),
        [SMEM] + [VMEM] * 7,
        [shape((queries // 2, width), bf16)] * 2,
        [VMEM] * 2,
        2 * queries * width * width,
        32,
    )

    def scatter(part):
        return summed(mixed(part.reshape(8, -1, width)))

    def swap(sums):
        return lax.ppermute(sums.astype(bf16), ALL, mixed_pairs()).astype(f32)

    sum_a = scatter(first)
    sum_a, second, train_rot = lax.optimization_barrier((sum_a, second, train_rot))
    far_a = swap(sum_a)
    train_o = lax.ppermute(train_rot, "core", SWAP)
    sum_b = scatter(second)
    far_a, sum_b, train_o = lax.optimization_barrier((far_a, sum_b, train_o))
    far_b = swap(sum_b)
    own_a = mixed(spread((sum_a + far_a).astype(bf16), 8)).reshape(queries // 2, width)
    far_b, own_a = lax.optimization_barrier((far_b, own_a))
    other_a = lax.ppermute(own_a, "core", SWAP)
    own_b = mixed(spread((sum_b + far_b).astype(bf16), 8)).reshape(queries // 2, width)
    other_b = lax.ppermute(own_b, "core", SWAP)

    partial_inner = call(
        functools.partial(outer_kernel, queries),
        (place, damp, own_a, own_b, other_a, other_b, train_rot, train_o, e_out, e_in),
        [SMEM] * 2 + [VMEM] * 8,
        shape((train, half), bf16),
        VMEM,
        2 * queries * width * half + 2 * train * width * half,
        32,
    )
    inner_sum = summed(near(partial_inner.reshape(8, -1, half)))
    inner_sum = inner_sum + lax.ppermute(inner_sum, "z_a", SWAP)
    factor = 1.0 / float(eig_in.shape[0]) ** 0.5
    inner = near(spread((inner_sum * factor).astype(bf16), 8)).reshape(train, half)
    inner_o = lax.ppermute(inner, "core", SWAP)
    partial_out = call(
        back_kernel,
        (place, inner, inner_o, basis_out),
        [SMEM] + [VMEM] * 3,
        shape((train, half), bf16),
        VMEM,
        2 * train * half * width,
        32,
    )
    return summed(lax.all_to_all(partial_out.reshape(16, -1, half), ROW, 0, 0, tiled=True))


def solution(mesh):
    split = Mesh(mesh.devices.reshape(SIZES), ALL)
    placed = (P(None, ROW), P(None, COL), P(None, COL), P(ROW, COL), P(COL, ROW), P(), P())
    return jax.shard_map(
        per_device, mesh=split, in_specs=placed, out_specs=P(ROW, COL), check_vma=False
    )
```

time: 182 us -> 174 us (0.956)
  blocking collectives: 141 us -> 56 us
  starting transfers between devices: 19.4 us -> 86.1 us
  waiting for transfers between devices: 4.62 us -> 15 us
  Pallas kernels: 5.77 us -> 9.86 us
    all_to_all x5 -> x4, blocking collectives: 141 us -> 56 us  [the longest x1 21.8 us: per_device(): lax.all_to_all(partial_out.reshape(16, -1, half), ROW, 0, 0, tiled=True)]
    ppermute x1 -> x5, starting transfers between devices: 1.91 us -> 45.6 us  [the longest x1 16.1 us: per_device(): other_b = lax.ppermute(own_b, 'core', SWAP)]
    all_to_all x0 -> x3, starting transfers between devices: none -> 13.6 us  [the longest x1 5.82 us: per_device(): mixed(spread((sum_a + far_a).astype(bf16), 8)).reshape(queries // 2, width)]
    ppermute x1 -> x5, waiting for transfers between devices: 0.01 us -> 9.31 us  [the longest x2 4.38 us: swap(): return lax.ppermute(sums.astype(bf16), ALL, mixed_pairs()).astype(f32)]
    ppermute x1, starting transfers between devices: 2.41 us -> 11.2 us  [per_device(): train_o = lax.ppermute(train_rot, 'core', SWAP)]
    pallas_call x3 -> x4, Pallas kernels: 5.77 us -> 9.86 us  [call(): pl.pallas_call(kernel, out_shape=shapes, in_specs=specs, out_specs=out_sp...]
    all_to_all x0 -> x3, waiting for transfers between devices: none -> 3.34 us  [the longest x1 3.34 us: per_device(): mixed(spread((sum_a + far_a).astype(bf16), 8)).reshape(queries // 2, width)]
    unnamed x14 -> x20, local copies, waits for them, and re-layouts: 5.01 us -> 2.28 us
  transfers between devices with their start and end apart: 6 -> 13, of which waited for: 2 -> 7; matrix products, arithmetic and copies ran while one was open for 1% -> 0% of each run, Pallas kernels for 0% -> 0%
where the time goes in v3:
time: 174 us; the launch traced here: 173 us
  starting transfers between devices  86.1 us (49%)
  blocking collectives  56 us (32%)
  waiting for transfers between devices  15 us (9%)
  Pallas kernels  9.86 us (6%)
  local copies, waits for them, and re-layouts  4.31 us (2%)
    all_to_all x1, blocking collectives, per_device(): lax.all_to_all(partial_out.reshape(16, -1, half), ROW, 0, 0, tiled=True)  21.8 us
    ppermute x1, starting transfers between devices, per_device(): other_b = lax.ppermute(own_b, 'core', SWAP)  16.1 us
    ppermute x1, starting transfers between devices, per_device(): other_a = lax.ppermute(own_a, 'core', SWAP)  14.8 us
    all_to_all x1, blocking collectives, per_device(): inner_sum = summed(near(partial_inner.reshape(8, -1, half)))  11.7 us
    all_to_all x1, blocking collectives, scatter(): return summed(mixed(part.reshape(8, -1, width)))  11.4 us
    ppermute x1, starting transfers between devices, per_device(): train_o = lax.ppermute(train_rot, 'core', SWAP)  11.2 us
    all_to_all x1, blocking collectives, per_device(): near(spread((inner_sum * factor).astype(bf16), 8)).reshape(train, half)  11.1 us
    pallas_call x4, Pallas kernels, call(): pl.pallas_call(kernel, out_shape=shapes, in_specs=specs, out_specs=out_sp...  9.86 us
  transfers between devices with their start and end apart: 13, of which 7 were waited for; matrix products, arithmetic and copies ran while one was open for 0% of the time, Pallas kernels for 0%

profile of v3, /device:TPU:1, one launch (start us, length us, event | category | flops | bytes accessed | tf_op | source)
XLA Modules:
  0.0 172.7 jit_solution(5456956151433585975)
XLA Ops:
  0.0 8.8 %collective-permute-start = (bf16[1024,512]{1,0:T(8,128)(2,1)}, bf16[1024,512]{1,0:T(8,128)(2,1)S(1)}, u32[]{:S(2)}, u32[]{:S(2)}) collective-permute-start(bf16[1024,512]{1,0:T(8,128)(2,1)} %b_in.1), channel_id=1, source_target_pairs={{1,0},{3,2},{5,4},{7,6},{9,8},{11,10},{13,12},{15,14},{17,16},{19,... | collective-permute-start | bytes 3145736 | tf_op jit(solution)/shard_map/ppermute | solution.py:183
  8.8 1.3 collective-permute-start.1
  15.5 3.9 %shard_map.74 = (bf16[384,1024]{1,0:T(8,128)(2,1)S(1)}, bf16[384,1024]{1,0:T(8,128)(2,1)S(1)}) custom-call(s32[3]{0:T(128)S(1)} %pad_add_fusion.place, bf16[768,1024]{1,0:T(8,128)(2,1)S(1)} %copy-done.1, bf16[768,512]{1,0:T(8,128)(2,1)S(1)} %copy-done.4, bf16[1024,512]{1,0:T(8,128)(2,1)S(1)} %copy-done.2, bf16[512,1024]{1,0:T(8,128)(2,1)S(1)} %copy-done, ...), custom_call_target="tpu_custom_call" | custom-call | flops 1610612736 | bytes 4194304 | tf_op jit(solution)/shard_map/pallas_call | solution.py:144
  19.3 11.4 %all_to_all.35 = bf16[8,48,1024]{2,1,0:T(8,128)(2,1)S(1)} all-to-all(bf16[8,48,1024]{2,1,0:T(8,128)(2,1)S(1)} %bitcast.20), channel_id=1, replica_groups={{0,32,64,96,128,160,192,224},{2,34,66,98,130,162,194,226},{4,36,68,100,..., dimensions={0} | all-to-all | bytes 1572864 | tf_op jit(solution)/shard_map/all_to_all | solution.py:210
  30.8 3.6 %all-to-all-start.1 = ((bf16[8,48,1024]{2,1,0:T(8,128)(2,1)}), bf16[8,48,1024]{2,1,0:T(8,128)(2,1)S(1)}, u32[]{:S(2)}, u32[]{:S(2)}) async-start(bf16[8,48,1024]{2,1,0:T(8,128)(2,1)} %bitcast.17), calls=%async_computation.1 | async-start | bytes 1572864 | tf_op jit(solution)/shard_map/all_to_all | solution.py:210
  34.4 11.2 %collective-permute-start.4 = (bf16[384,512]{1,0:T(8,128)(2,1)S(1)}, bf16[384,512]{1,0:T(8,128)(2,1)S(1)}, u32[]{:S(2)}, u32[]{:S(2)}) collective-permute-start(bf16[384,512]{1,0:T(8,128)(2,1)S(1)} %copy-done.5), channel_id=1, source_target_pairs={{0,1},{1,0},{2,3},{3,2},{4,5},{5,4},{6,7},{7,6},{8,9},{9,8},{10,11... | collective-permute-start | bytes 1179656 | tf_op jit(solution)/shard_map/ppermute | solution.py:218
  45.7 4.9 %collective-permute-start.3 = (bf16[48,1024]{1,0:T(8,128)(2,1)S(1)}, bf16[48,1024]{1,0:T(8,128)(2,1)S(1)}, u32[]{:S(2)}, u32[]{:S(2)}) collective-permute-start(bf16[48,1024]{1,0:T(8,128)(2,1)S(1)} %convert_element_type.34), channel_id=1, source_target_pairs={{0,256},{1,5},{2,258},{3,7},{4,260},{5,1},{6,262},{7,3},{8,264},{9... | collective-permute-start | bytes 294920 | tf_op jit(solution)/shard_map/ppermute | solution.py:213
  50.6 2.3 %collective-permute-done.3 = bf16[48,1024]{1,0:T(8,128)(2,1)S(1)} collective-permute-done((bf16[48,1024]{1,0:T(8,128)(2,1)S(1)}, bf16[48,1024]{1,0:T(8,128)(2,1)S(1)}, u32[]{:S(2)}, u32[]{:S(2)}) %collective-permute-start.3) | collective-permute-done | bytes 98336 | tf_op jit(solution)/shard_map/ppermute | solution.py:213
  54.1 5.8 %all-to-all-start.2 = ((bf16[8,48,1024]{2,1,0:T(8,128)(2,1)}), bf16[8,48,1024]{2,1,0:T(8,128)(2,1)S(1)}, u32[]{:S(2)}, u32[]{:S(2)}) async-start(bf16[8,48,1024]{2,1,0:T(8,128)(2,1)} %broadcast_in_dim.6), calls=%async_computation.2 | async-start | bytes 1572864 | tf_op jit(solution)/shard_map/all_to_all | solution.py:222
  60.0 4.5 %collective-permute-start.5 = (bf16[48,1024]{1,0:T(8,128)(2,1)S(1)}, bf16[48,1024]{1,0:T(8,128)(2,1)S(1)}, u32[]{:S(2)}, u32[]{:S(2)}) collective-permute-start(bf16[48,1024]{1,0:T(8,128)(2,1)S(1)} %convert_element_type.37), channel_id=1, source_target_pairs={{0,256},{1,5},{2,258},{3,7},{4,260},{5,1},{6,262},{7,3},{8,264},{9... | collective-permute-start | bytes 294920 | tf_op jit(solution)/shard_map/ppermute | solution.py:213
  64.5 2.1 %collective-permute-done.5 = bf16[48,1024]{1,0:T(8,128)(2,1)S(1)} collective-permute-done((bf16[48,1024]{1,0:T(8,128)(2,1)S(1)}, bf16[48,1024]{1,0:T(8,128)(2,1)S(1)}, u32[]{:S(2)}, u32[]{:S(2)}) %collective-permute-start.5) | collective-permute-done | bytes 98336 | tf_op jit(solution)/shard_map/ppermute | solution.py:213
  66.6 3.3 %all-to-all-done.2 = bf16[8,48,1024]{2,1,0:T(8,128)(2,1)S(1)} async-done(((bf16[8,48,1024]{2,1,0:T(8,128)(2,1)}), bf16[8,48,1024]{2,1,0:T(8,128)(2,1)S(1)}, u32[]{:S(2)}, u32[]{:S(2)}) %all-to-all-start.2) | async-done | bytes 786464 | tf_op jit(solution)/shard_map/all_to_all | solution.py:222
  71.0 4.2 %all-to-all-start.3 = ((bf16[8,48,1024]{2,1,0:T(8,128)(2,1)}), bf16[8,48,1024]{2,1,0:T(8,128)(2,1)S(1)}, u32[]{:S(2)}, u32[]{:S(2)}) async-start(bf16[8,48,1024]{2,1,0:T(8,128)(2,1)} %broadcast_in_dim.7), calls=%async_computation.3 | async-start | bytes 1572864 | tf_op jit(solution)/shard_map/all_to_all | solution.py:225
  75.2 14.8 %collective-permute-start.6 = (bf16[384,1024]{1,0:T(8,128)(2,1)S(1)}, bf16[384,1024]{1,0:T(8,128)(2,1)}, u32[]{:S(2)}, u32[]{:S(2)}) collective-permute-start(bf16[384,1024]{1,0:T(8,128)(2,1)S(1)} %bitcast.15), channel_id=1, source_target_pairs={{0,1},{1,0},{2,3},{3,2},{4,5},{5,4},{6,7},{7,6},{8,9},{9,8},{10,11... | collective-permute-start | bytes 2359304 | tf_op jit(solution)/shard_map/ppermute | solution.py:224
  90.0 16.1 %collective-permute-start.7 = (bf16[384,1024]{1,0:T(8,128)(2,1)S(1)}, bf16[384,1024]{1,0:T(8,128)(2,1)S(1)}, u32[]{:S(2)}, u32[]{:S(2)}) collective-permute-start(bf16[384,1024]{1,0:T(8,128)(2,1)S(1)} %bitcast.18), channel_id=1, source_target_pairs={{0,1},{1,0},{2,3},{3,2},{4,5},{5,4},{6,7},{7,6},{8,9},{9,8},{10,11... | collective-permute-start | bytes 2359304 | tf_op jit(solution)/shard_map/ppermute | solution.py:226
  106.2 1.9 %collective-permute-done.7.other_b = bf16[384,1024]{1,0:T(8,128)(2,1)S(1)} collective-permute-done((bf16[384,1024]{1,0:T(8,128)(2,1)S(1)}, bf16[384,1024]{1,0:T(8,128)(2,1)S(1)}, u32[]{:S(2)}, u32[]{:S(2)}) %collective-permute-start.7) | collective-permute-done | bytes 786464 | tf_op jit(solution)/shard_map/ppermute | solution.py:226
  108.1 4.2 %shard_map.75 = bf16[384,512]{1,0:T(8,128)(2,1)S(1)} custom-call(s32[3]{0:T(128)S(1)} %pad_add_fusion.place, f32[1]{0:T(128)} %shard_map.73.damp, bf16[384,1024]{1,0:T(8,128)(2,1)S(1)} %bitcast.16, bf16[384,1024]{1,0:T(8,128)(2,1)S(1)} %bitcast.19, bf16[384,1024]{1,0:T(8,128)(2,1)} %collective-permute-done.6.other_a, ...), custom_call_target="tpu_custom_call" | custom-call | flops 1207959552 | bytes 4194304 | tf_op jit(solution)/shard_map/pallas_call | solution.py:144
  112.2 11.7 %all_to_all.36 = bf16[8,48,512]{2,1,0:T(8,128)(2,1)S(1)} all-to-all(bf16[8,48,512]{2,1,0:T(8,128)(2,1)S(1)} %bitcast.21), channel_id=1, replica_groups=mesh['z_hi'=2,'y'=8,'x'=4,'z_a'=2,'z_b'=2,'core'=2] {'x','z_b'}, dimensions={0} | all-to-all | bytes 786432 | tf_op jit(solution)/shard_map/all_to_all | solution.py:237
  124.0 5.1 %collective-permute-start.8 = (f32[48,512]{1,0:T(8,128)S(1)}, f32[48,512]{1,0:T(8,128)S(1)}, u32[]{:S(2)}, u32[]{:S(2)}) collective-permute-start(f32[48,512]{1,0:T(8,128)S(1)} %convert_reduce_fusion.3), channel_id=1, source_target_pairs={{0,4},{4,0},{1,5},{5,1},{2,6},{6,2},{3,7},{7,3},{8,12},{12,8},{9,1... | collective-permute-start | bytes 294920 | tf_op jit(solution)/shard_map/ppermute | solution.py:238
  129.2 3.0 %collective-permute-done.8 = f32[48,512]{1,0:T(8,128)S(1)} collective-permute-done((f32[48,512]{1,0:T(8,128)S(1)}, f32[48,512]{1,0:T(8,128)S(1)}, u32[]{:S(2)}, u32[]{:S(2)}) %collective-permute-start.8) | collective-permute-done | bytes 98336 | tf_op jit(solution)/shard_map/ppermute | solution.py:238
  132.3 11.1 %all_to_all.37 = bf16[8,48,512]{2,1,0:T(8,128)(2,1)S(1)} all-to-all(bf16[8,48,512]{2,1,0:T(8,128)(2,1)S(1)} %broadcast_in_dim.8), channel_id=1, replica_groups=mesh['z_hi'=2,'y'=8,'x'=4,'z_a'=2,'z_b'=2,'core'=2] {'x','z_b'}, dimensions={0} | all-to-all | bytes 786432 | tf_op jit(solution)/shard_map/all_to_all | solution.py:240
  143.4 4.4 %collective-permute-start.9 = (bf16[384,512]{1,0:T(8,128)(2,1)S(1)}, bf16[384,512]{1,0:T(8,128)(2,1)S(1)}, u32[]{:S(2)}, u32[]{:S(2)}) collective-permute-start(bf16[384,512]{1,0:T(8,128)(2,1)S(1)} %bitcast.12), channel_id=1, source_target_pairs={{0,1},{1,0},{2,3},{3,2},{4,5},{5,4},{6,7},{7,6},{8,9},{9,8},{10,11... | collective-permute-start | bytes 1179656 | tf_op jit(solution)/shard_map/ppermute | solution.py:241
  147.7 1.3 collective-permute-done.9.other
  150.2 21.8 %all_to_all.38 = bf16[16,24,512]{2,1,0:T(8,128)(2,1)S(1)} all-to-all(bf16[16,24,512]{2,1,0:T(8,128)(2,1)S(1)} %bitcast.14), channel_id=1, replica_groups=mesh['z_hi'=2,'y'=8,'x'=4,'z_a'=2,'z_b'=2,'core'=2] {'z_hi','y'}, dimensions={0} | all-to-all | bytes 786432 | tf_op jit(solution)/shard_map/all_to_all | solution.py:251
  (45 shorter events, 9.6 us)
Async XLA Ops:
  0.0 14.9 %collective-permute-start = (bf16[1024,512]{1,0:T(8,128)(2,1)}, bf16[1024,512]{1,0:T(8,128)(2,1)S(1)}, u32[]{:S(2)}, u32[]{:S(2)}) collective-permute-start(bf16[1024,512]{1,0:T(8,128)(2,1)} %b_in.1), channel_id=1, source_target_pairs={{1,0},{3,2},{5,4},{7,6},{9,8},{11,10},{13,12},{15,14},{17,16},{19,... | collective-permute-start | bytes 3145736 | tf_op jit(solution)/shard_map/ppermute | solution.py:183
  8.8 6.0 %collective-permute-start.1 = (bf16[512,1024]{1,0:T(8,128)(2,1)}, bf16[512,1024]{1,0:T(8,128)(2,1)S(1)}, u32[]{:S(2)}, u32[]{:S(2)}) collective-permute-start(bf16[512,1024]{1,0:T(8,128)(2,1)} %b_out.3), channel_id=1, source_target_pairs={{0,1},{2,3},{4,5},{6,7},{8,9},{10,11},{12,13},{14,15},{16,17},{18,... | collective-permute-start | bytes 3145736 | tf_op jit(solution)/shard_map/ppermute | solution.py:184
  10.1 4.7 %collective-permute-start.2 = (bf16[768,512]{1,0:T(8,128)(2,1)}, bf16[768,512]{1,0:T(8,128)(2,1)}, u32[]{:S(2)}, u32[]{:S(2)}) collective-permute-start(bf16[768,512]{1,0:T(8,128)(2,1)} %grad.1), channel_id=1, source_target_pairs={{0,1},{2,3},{4,5},{6,7},{8,9},{10,11},{12,13},{14,15},{16,17},{18,... | collective-permute-start | bytes 2359304 | tf_op jit(solution)/shard_map/ppermute | solution.py:185
  11.5 0.8 copy-start.6
  12.4 0.8 copy-start.8
  13.2 1.7 copy-start
  13.2 1.7 %copy-start.1 = (bf16[768,1024]{1,0:T(8,128)(2,1)S(1)}, bf16[768,1024]{1,0:T(8,128)(2,1)}, u32[]{:S(2)}) copy-start(bf16[768,1024]{1,0:T(8,128)(2,1)} %act.1) | copy-start | bytes 4718596
  13.2 2.0 %copy-start.2 = (bf16[1024,512]{1,0:T(8,128)(2,1)S(1)}, bf16[1024,512]{1,0:T(8,128)(2,1)}, u32[]{:S(2)}) copy-start(bf16[1024,512]{1,0:T(8,128)(2,1)} %b_in.1) | copy-start | bytes 3145732
  13.2 2.2 %copy-start.4 = (bf16[768,512]{1,0:T(8,128)(2,1)S(1)}, bf16[768,512]{1,0:T(8,128)(2,1)}, u32[]{:S(2)}) copy-start(bf16[768,512]{1,0:T(8,128)(2,1)} %grad.1) | copy-start | bytes 2359300
  19.3 11.5 %copy-start.3 = (bf16[384,1024]{1,0:T(8,128)(2,1)}, bf16[384,1024]{1,0:T(8,128)(2,1)S(1)}, u32[]{:S(2)}) copy-start(bf16[384,1024]{1,0:T(8,128)(2,1)S(1)} %get-tuple-element.26) | copy-start | bytes 2359300
  30.7 3.7 %copy-start.5 = (bf16[384,512]{1,0:T(8,128)(2,1)S(1)}, bf16[384,512]{1,0:T(8,128)(2,1)}, u32[]{:S(2)}) copy-start(bf16[384,512]{1,0:T(8,128)(2,1)} %train) | copy-start | bytes 1179652
  30.8 22.1 %all-to-all-start.1 = ((bf16[8,48,1024]{2,1,0:T(8,128)(2,1)}), bf16[8,48,1024]{2,1,0:T(8,128)(2,1)S(1)}, u32[]{:S(2)}, u32[]{:S(2)}) async-start(bf16[8,48,1024]{2,1,0:T(8,128)(2,1)} %bitcast.17), calls=%async_computation.1 | async-start | bytes 1572864 | tf_op jit(solution)/shard_map/all_to_all | solution.py:210
  34.4 18.6 %collective-permute-start.4 = (bf16[384,512]{1,0:T(8,128)(2,1)S(1)}, bf16[384,512]{1,0:T(8,128)(2,1)S(1)}, u32[]{:S(2)}, u32[]{:S(2)}) collective-permute-start(bf16[384,512]{1,0:T(8,128)(2,1)S(1)} %copy-done.5), channel_id=1, source_target_pairs={{0,1},{1,0},{2,3},{3,2},{4,5},{5,4},{6,7},{7,6},{8,9},{9,8},{10,11... | collective-permute-start | bytes 1179656 | tf_op jit(solution)/shard_map/ppermute | solution.py:218
  45.7 7.2 %collective-permute-start.3 = (bf16[48,1024]{1,0:T(8,128)(2,1)S(1)}, bf16[48,1024]{1,0:T(8,128)(2,1)S(1)}, u32[]{:S(2)}, u32[]{:S(2)}) collective-permute-start(bf16[48,1024]{1,0:T(8,128)(2,1)S(1)} %convert_element_type.34), channel_id=1, source_target_pairs={{0,256},{1,5},{2,258},{3,7},{4,260},{5,1},{6,262},{7,3},{8,264},{9... | collective-permute-start | bytes 294920 | tf_op jit(solution)/shard_map/ppermute | solution.py:213
  54.1 15.9 %all-to-all-start.2 = ((bf16[8,48,1024]{2,1,0:T(8,128)(2,1)}), bf16[8,48,1024]{2,1,0:T(8,128)(2,1)S(1)}, u32[]{:S(2)}, u32[]{:S(2)}) async-start(bf16[8,48,1024]{2,1,0:T(8,128)(2,1)} %broadcast_in_dim.6), calls=%async_computation.2 | async-start | bytes 1572864 | tf_op jit(solution)/shard_map/all_to_all | solution.py:222
  59.9 48.1 %copy-start.7 = (f32[16384]{0:T(1024)S(1)}, f32[16384]{0:T(1024)}, u32[]{:S(2)}) copy-start(f32[16384]{0:T(1024)} %param.12) | copy-start | bytes 196612
  60.0 48.1 %copy-start.9 = (f32[16384]{0:T(1024)S(1)}, f32[16384]{0:T(1024)}, u32[]{:S(2)}) copy-start(f32[16384]{0:T(1024)} %param.13) | copy-start | bytes 196612
  60.0 6.6 %collective-permute-start.5 = (bf16[48,1024]{1,0:T(8,128)(2,1)S(1)}, bf16[48,1024]{1,0:T(8,128)(2,1)S(1)}, u32[]{:S(2)}, u32[]{:S(2)}) collective-permute-start(bf16[48,1024]{1,0:T(8,128)(2,1)S(1)} %convert_element_type.37), channel_id=1, source_target_pairs={{0,256},{1,5},{2,258},{3,7},{4,260},{5,1},{6,262},{7,3},{8,264},{9... | collective-permute-start | bytes 294920 | tf_op jit(solution)/shard_map/ppermute | solution.py:213
  71.0 19.0 %all-to-all-start.3 = ((bf16[8,48,1024]{2,1,0:T(8,128)(2,1)}), bf16[8,48,1024]{2,1,0:T(8,128)(2,1)S(1)}, u32[]{:S(2)}, u32[]{:S(2)}) async-start(bf16[8,48,1024]{2,1,0:T(8,128)(2,1)} %broadcast_in_dim.7), calls=%async_computation.3 | async-start | bytes 1572864 | tf_op jit(solution)/shard_map/all_to_all | solution.py:225
  75.2 31.0 %collective-permute-start.6 = (bf16[384,1024]{1,0:T(8,128)(2,1)S(1)}, bf16[384,1024]{1,0:T(8,128)(2,1)}, u32[]{:S(2)}, u32[]{:S(2)}) collective-permute-start(bf16[384,1024]{1,0:T(8,128)(2,1)S(1)} %bitcast.15), channel_id=1, source_target_pairs={{0,1},{1,0},{2,3},{3,2},{4,5},{5,4},{6,7},{7,6},{8,9},{9,8},{10,11... | collective-permute-start | bytes 2359304 | tf_op jit(solution)/shard_map/ppermute | solution.py:224
  90.0 18.0 %collective-permute-start.7 = (bf16[384,1024]{1,0:T(8,128)(2,1)S(1)}, bf16[384,1024]{1,0:T(8,128)(2,1)S(1)}, u32[]{:S(2)}, u32[]{:S(2)}) collective-permute-start(bf16[384,1024]{1,0:T(8,128)(2,1)S(1)} %bitcast.18), channel_id=1, source_target_pairs={{0,1},{1,0},{2,3},{3,2},{4,5},{5,4},{6,7},{7,6},{8,9},{9,8},{10,11... | collective-permute-start | bytes 2359304 | tf_op jit(solution)/shard_map/ppermute | solution.py:226
  124.0 8.2 %collective-permute-start.8 = (f32[48,512]{1,0:T(8,128)S(1)}, f32[48,512]{1,0:T(8,128)S(1)}, u32[]{:S(2)}, u32[]{:S(2)}) collective-permute-start(f32[48,512]{1,0:T(8,128)S(1)} %convert_reduce_fusion.3), channel_id=1, source_target_pairs={{0,4},{4,0},{1,5},{5,1},{2,6},{6,2},{3,7},{7,3},{8,12},{12,8},{9,1... | collective-permute-start | bytes 294920 | tf_op jit(solution)/shard_map/ppermute | solution.py:238
  143.4 5.7 %collective-permute-start.9 = (bf16[384,512]{1,0:T(8,128)(2,1)S(1)}, bf16[384,512]{1,0:T(8,128)(2,1)S(1)}, u32[]{:S(2)}, u32[]{:S(2)}) collective-permute-start(bf16[384,512]{1,0:T(8,128)(2,1)S(1)} %bitcast.12), channel_id=1, source_target_pairs={{0,1},{1,0},{2,3},{3,2},{4,5},{5,4},{6,7},{7,6},{8,9},{9,8},{10,11... | collective-permute-start | bytes 1179656 | tf_op jit(solution)/shard_map/ppermute | solution.py:241

commit v4 on v3

v4 whole, which is shorter than its diff:
```python
import functools

import jax
import jax.numpy as jnp
from jax import lax
from jax.experimental import pallas as pl
from jax.experimental.pallas import tpu as pltpu
from jax.sharding import Mesh
from jax.sharding import PartitionSpec as P

ROW = ("z_hi", "y")
CHIPS = ("x", "z_a", "z_b")
COL = (*CHIPS, "core")
ALL = ROW + COL
SIZES = (2, 8, 4, 2, 2, 2)
NEAR = ("x", "z_b")
SWAP = [(0, 1), (1, 0)]
MIB = 1024 * 1024

damping_share = 0.1

bf16 = jnp.bfloat16
f32 = jnp.float32

SMEM = pl.BlockSpec(memory_space=pltpu.SMEM)
VMEM = pl.BlockSpec(memory_space=pltpu.VMEM)
ANY = pl.BlockSpec(memory_space=pl.ANY)


def dot(a, b):
    return jnp.dot(a, b, preferred_element_type=f32)


def dot_nt(a, b):
    return lax.dot_general(a, b, (((1,), (1,)), ((), ())), preferred_element_type=f32)


def dot_tn(a, b):
    return lax.dot_general(a, b, (((0,), (0,)), ((), ())), preferred_element_type=f32)


TILE = 256


def act_kernel(act, weight, out, held, room, sems):
    steps = act.shape[0] // TILE
    pieces = sems.shape[0] - steps
    depth = weight.shape[0] // pieces
    loads = [
        pltpu.make_async_copy(
            weight.at[pl.ds(p * depth, depth)], room.at[pl.ds(p * depth, depth)], sems.at[steps + p]
        )
        for p in range(pieces)
    ]
    spans = [pl.ds(m * TILE, TILE) for m in range(steps)]
    rows = [
        pltpu.make_async_copy(act.at[span], held.at[span], sems.at[m])
        for m, span in enumerate(spans)
    ]
    for copy in loads + rows:
        copy.start()
    for copy in loads:
        copy.wait()
    for span, copy in zip(spans, rows):
        copy.wait()
        out[span, :] = dot(held[span, :], room[...]).astype(bf16)


def grad_kernel(place, grad, weight, keep, send):
    half = keep.shape[1]

    def body(mine, theirs):
        @pl.loop(0, grad.shape[0] // TILE)
        def _(m):
            rows = pl.ds(pl.multiple_of(m * TILE, TILE), TILE)
            send[rows, :] = dot(grad[rows, :], weight[:, theirs : theirs + half])
            keep[rows, :] = dot(grad[rows, :], weight[:, mine : mine + half])

    @pl.when(place[0] == 0)
    def _():
        body(0, half)

    @pl.when(place[0] == 1)
    def _():
        body(half, 0)


def outer_kernel(queries, place, act, act_o, grad, train, train_o, e_out, e_in, out):
    half = train.shape[1]
    lanes = e_in.shape[1]
    count = half // lanes
    first = place[0] == 0
    damp = damping_share * (jnp.sum(e_in[...]) / e_in.size) * (jnp.sum(e_out[...]) / e_out.size)
    e_rows = e_in[pl.ds(pl.multiple_of(place[1] * 8, 8), 8), :]
    low, high = (
        jnp.concatenate([e_rows[r : r + 1, :] for r in range(k * count, (k + 1) * count)], axis=1)
        for k in range(2)
    )
    e_own, e_other = jnp.where(first, low, high), jnp.where(first, high, low)
    e_cols = jnp.transpose(e_out[pl.ds(pl.multiple_of(place[2] * 8, 8), 8), :])
    for start in range(0, half, TILE):
        r = start // lanes
        e_col = jnp.concatenate(
            [
                jnp.where(
                    first,
                    e_cols[:, r + q : r + q + 1],
                    e_cols[:, count + r + q : count + r + q + 1],
                )
                for q in range(TILE // lanes)
            ],
            axis=0,
        )
        total = None
        for a, e_row, t in ((act, e_own, train), (act_o, e_other, train_o)):
            outer = dot_tn(grad[:, start : start + TILE], a[...])
            scaled = (outer / queries / (e_col * e_row + damp)).astype(bf16)
            product = dot_nt(t[...], scaled)
            total = product if total is None else total + product
        out[:, start : start + TILE] = total.astype(bf16)


def back_kernel(place, own, other, b_out, out):
    half = own.shape[1]

    def body(left, right):
        out[...] = (
            dot_nt(left[...], b_out[:, :half]) + dot_nt(right[...], b_out[:, half:])
        ).astype(bf16)

    @pl.when(place[0] == 0)
    def _():
        body(own, other)

    @pl.when(place[0] == 1)
    def _():
        body(other, own)


def call(kernel, args, specs, shapes, out_specs, flops, limit, scratch=()):
    return pl.pallas_call(
        kernel,
        out_shape=shapes,
        in_specs=specs,
        out_specs=out_specs,
        scratch_shapes=scratch,
        compiler_params=pltpu.CompilerParams(vmem_limit_bytes=limit * MIB),
        cost_estimate=pl.CostEstimate(flops=flops, bytes_accessed=4 * MIB, transcendentals=0),
    )(*args)


def summed(pieces):
    return jnp.sum(pieces.astype(f32), axis=0)


def spread(array, n):
    return jnp.broadcast_to(array[None], (n, *array.shape))


def exchanged(array, axes):
    return lax.all_to_all(array, axes, 0, 0, tiled=True)


def per_device(query_act, query_grad, train_rot, basis_in, basis_out, eig_in, eig_out):
    queries, train = query_act.shape[0], train_rot.shape[0]
    width, half = basis_in.shape
    shape = jax.ShapeDtypeStruct
    place = jnp.stack(
        [lax.axis_index("core"), lax.axis_index(CHIPS), lax.axis_index(ROW)]
    ).astype(jnp.int32)
    e_in, e_out = (e.reshape(-1, 128) for e in (eig_in, eig_out))

    act_part = call(
        act_kernel,
        (query_act, basis_in),
        [ANY] * 2,
        shape((queries, half), bf16),
        VMEM,
        2 * queries * width * half,
        58,
        (
            pltpu.VMEM((queries, width), bf16),
            pltpu.VMEM((width, half), bf16),
            pltpu.SemaphoreType.DMA((queries // TILE + 4,)),
        ),
    )
    act_part, query_grad = lax.optimization_barrier((act_part, query_grad))
    keep, send = call(
        grad_kernel,
        (place, query_grad, basis_out),
        [SMEM] + [VMEM] * 2,
        [shape((queries, half), f32)] * 2,
        [VMEM] * 2,
        2 * queries * width * half,
        32,
    )
    grad_part = (keep + lax.ppermute(send, "core", SWAP)).astype(bf16)

    sum_act = summed(exchanged(act_part.reshape(8, -1, half), "y"))
    sum_act, grad_part = lax.optimization_barrier((sum_act, grad_part))
    far_act = lax.ppermute(sum_act.astype(bf16), "z_hi", SWAP).astype(f32)
    sum_grad = summed(exchanged(grad_part.reshape(8, -1, half), NEAR))
    far_act, sum_grad, train_rot = lax.optimization_barrier((far_act, sum_grad, train_rot))
    far_grad = lax.ppermute(sum_grad, "z_a", SWAP)
    train_o = lax.ppermute(train_rot, "core", SWAP)
    act = exchanged(spread((sum_act + far_act).astype(bf16), 8), "y").reshape(queries, half)
    far_grad, act, train_o = lax.optimization_barrier((far_grad, act, train_o))
    act_o = lax.ppermute(act, "core", SWAP)
    grad = exchanged(spread((sum_grad + far_grad).astype(bf16), 8), NEAR).reshape(queries, half)

    partial_inner = call(
        functools.partial(outer_kernel, queries),
        (place, act, act_o, grad, train_rot, train_o, e_out, e_in),
        [SMEM] + [VMEM] * 7,
        shape((train, half), bf16),
        VMEM,
        2 * queries * width * half + 2 * train * width * half,
        32,
    )
    inner_sum = summed(exchanged(partial_inner.reshape(8, -1, half), NEAR))
    inner_sum = inner_sum + lax.ppermute(inner_sum, "z_a", SWAP)
    factor = 1.0 / float(eig_in.shape[0]) ** 0.5
    inner = exchanged(spread((inner_sum * factor).astype(bf16), 8), NEAR).reshape(train, half)
    inner_o = lax.ppermute(inner, "core", SWAP)
    partial_out = call(
        back_kernel,
        (place, inner, inner_o, basis_out),
        [SMEM] + [VMEM] * 3,
        shape((train, half), bf16),
        VMEM,
        2 * train * half * width,
        32,
    )
    return summed(exchanged(partial_out.reshape(16, -1, half), ROW))


def solution(mesh):
    split = Mesh(mesh.devices.reshape(SIZES), ALL)
    placed = (P(None, ROW), P(None, COL), P(None, COL), P(ROW, COL), P(COL, ROW), P(), P())
    return jax.shard_map(
        per_device, mesh=split, in_specs=placed, out_specs=P(ROW, COL), check_vma=False
    )
```

time: 174 us -> 172 us (0.989)
  starting transfers between devices: 86.1 us -> 57.4 us
  waiting for transfers between devices: 15 us -> 33.9 us
  blocking collectives: 56 us -> 63.8 us
    ppermute x7 -> x4, starting transfers between devices: 51.8 us -> 25.8 us  [the longest x1 9.74 us: per_device(): far_act = lax.ppermute(sum_act.astype(bf16), 'z_hi', SWAP).astype(f32)]
    ppermute x7 -> x4, waiting for transfers between devices: 7.25 us -> 22.1 us  [the longest x1 10.3 us: per_device(): far_grad = lax.ppermute(sum_grad, 'z_a', SWAP)]
    all_to_all x4, blocking collectives: 56 us -> 63.8 us  [exchanged(): return lax.all_to_all(array, axes, 0, 0, tiled=True)]
    ppermute x1, starting transfers between devices: 11.2 us -> 4.8 us  [per_device(): train_o = lax.ppermute(train_rot, 'core', SWAP)]
    all_to_all x3, waiting for transfers between devices: 3.34 us -> 7.42 us  [exchanged(): return lax.all_to_all(array, axes, 0, 0, tiled=True)]
    ppermute x1, starting transfers between devices: 4.35 us -> 7.55 us  [per_device(): inner_o = lax.ppermute(inner, 'core', SWAP)]
  transfers between devices with their start and end apart: 13 -> 10, of which waited for: 7 -> 7; matrix products, arithmetic and copies ran while one was open for 0% -> 0% of each run, Pallas kernels for 0% -> 0%
where the time goes in v4:
time: 172 us; the launch traced here: 171 us
  blocking collectives  63.8 us (37%)
  starting transfers between devices  57.4 us (33%)
  waiting for transfers between devices  33.9 us (20%)
  Pallas kernels  9.35 us (5%)
  local copies, waits for them, and re-layouts  3.97 us (2%)
  other arithmetic  2.27 us (1%)
    all_to_all x4, blocking collectives, exchanged(): return lax.all_to_all(array, axes, 0, 0, tiled=True)  63.8 us
    all_to_all x3, starting transfers between devices, exchanged(): return lax.all_to_all(array, axes, 0, 0, tiled=True)  13.2 us
    ppermute x1, waiting for transfers between devices, per_device(): far_grad = lax.ppermute(sum_grad, 'z_a', SWAP)  10.3 us
    ppermute x1, waiting for transfers between devices, per_device(): far_act = lax.ppermute(sum_act.astype(bf16), 'z_hi', SWAP).astype(f32)  9.85 us
    ppermute x1, starting transfers between devices, per_device(): far_act = lax.ppermute(sum_act.astype(bf16), 'z_hi', SWAP).astype(f32)  9.74 us
    pallas_call x4, Pallas kernels, call(): pl.pallas_call(kernel, out_shape=shapes, in_specs=specs, out_specs=out_sp...  9.35 us
    ppermute x1, starting transfers between devices, per_device(): grad_part = (keep + lax.ppermute(send, 'core', SWAP)).astype(bf16)  8.79 us
    ppermute x1, starting transfers between devices, per_device(): inner_o = lax.ppermute(inner, 'core', SWAP)  7.55 us
  transfers between devices with their start and end apart: 10, of which 7 were waited for; matrix products, arithmetic and copies ran while one was open for 0% of the time, Pallas kernels for 0%

profile of v4, /device:TPU:1, one launch (start us, length us, event | category | flops | bytes accessed | tf_op | source)
XLA Modules:
  0.0 170.9 jit_solution(17778936900792175945)
XLA Ops:
  0.0 3.8 %shard_map.73 = bf16[768,512]{1,0:T(8,128)(2,1)} custom-call(bf16[768,1024]{1,0:T(8,128)(2,1)} %act.1, bf16[1024,512]{1,0:T(8,128)(2,1)} %weight.2), custom_call_target="tpu_custom_call" | custom-call | flops 805306368 | bytes 4194304 | tf_op jit(solution)/shard_map/pallas_call | solution.py:141
  3.9 1.9 %shard_map.74 = (f32[768,512]{1,0:T(8,128)S(1)}, f32[768,512]{1,0:T(8,128)S(1)}) custom-call(s32[3]{0:T(128)S(1)} %pad_add_fusion.place, bf16[768,512]{1,0:T(8,128)(2,1)S(1)} %copy-done.1, bf16[512,1024]{1,0:T(8,128)(2,1)S(1)} %copy-done), custom_call_target="tpu_custom_call" | custom-call | flops 805306368 | bytes 4194304 | tf_op jit(solution)/shard_map/pallas_call | solution.py:141
  5.8 8.8 %collective-permute-start = (f32[768,512]{1,0:T(8,128)S(1)}, f32[768,512]{1,0:T(8,128)S(1)}, u32[]{:S(2)}, u32[]{:S(2)}) collective-permute-start(f32[768,512]{1,0:T(8,128)S(1)} %get-tuple-element.20), channel_id=1, source_target_pairs={{0,1},{1,0},{2,3},{3,2},{4,5},{5,4},{6,7},{7,6},{8,9},{9,8},{10,11... | collective-permute-start | bytes 4718600 | tf_op jit(solution)/shard_map/ppermute | solution.py:197
  14.6 26.0 %all_to_all.35 = bf16[8,96,512]{2,1,0:T(8,128)(2,1)S(1)} all-to-all(bf16[8,96,512]{2,1,0:T(8,128)(2,1)S(1)} %bitcast.21), channel_id=1, replica_groups=mesh['z_hi'=2,'y'=8,'x'=4,'z_a'=2,'z_b'=2,'core'=2] {'y'}, dimensions={0} | all-to-all | bytes 1572864 | tf_op jit(solution)/shard_map/all_to_all | solution.py:161
  41.9 4.6 %all-to-all-start.1 = ((bf16[8,96,512]{2,1,0:T(8,128)(2,1)}), bf16[8,96,512]{2,1,0:T(8,128)(2,1)S(1)}, u32[]{:S(2)}, u32[]{:S(2)}) async-start(bf16[8,96,512]{2,1,0:T(8,128)(2,1)} %bitcast.4), calls=%async_computation.1 | async-start | bytes 1572864 | tf_op jit(solution)/shard_map/all_to_all | solution.py:161
  46.5 9.7 %collective-permute-start.1 = (bf16[96,512]{1,0:T(8,128)(2,1)S(1)}, bf16[96,512]{1,0:T(8,128)(2,1)S(1)}, u32[]{:S(2)}, u32[]{:S(2)}) collective-permute-start(bf16[96,512]{1,0:T(8,128)(2,1)S(1)} %convert_element_type.32), channel_id=1, source_target_pairs={{0,256},{256,0},{1,257},{257,1},{2,258},{258,2},{3,259},{259,3},{4... | collective-permute-start | bytes 294920 | tf_op jit(solution)/shard_map/ppermute | solution.py:201
  56.3 9.9 %collective-permute-done.1 = bf16[96,512]{1,0:T(8,128)(2,1)S(1)} collective-permute-done((bf16[96,512]{1,0:T(8,128)(2,1)S(1)}, bf16[96,512]{1,0:T(8,128)(2,1)S(1)}, u32[]{:S(2)}, u32[]{:S(2)}) %collective-permute-start.1) | collective-permute-done | bytes 98336 | tf_op jit(solution)/shard_map/ppermute | solution.py:201
  67.3 3.5 %all-to-all-start.2 = ((bf16[8,96,512]{2,1,0:T(8,128)(2,1)}), bf16[8,96,512]{2,1,0:T(8,128)(2,1)S(1)}, u32[]{:S(2)}, u32[]{:S(2)}) async-start(bf16[8,96,512]{2,1,0:T(8,128)(2,1)} %broadcast_in_dim.6), calls=%async_computation.2 | async-start | bytes 1572864 | tf_op jit(solution)/shard_map/all_to_all | solution.py:161
  70.9 4.8 %collective-permute-start.3 = (bf16[384,512]{1,0:T(8,128)(2,1)S(1)}, bf16[384,512]{1,0:T(8,128)(2,1)S(1)}, u32[]{:S(2)}, u32[]{:S(2)}) collective-permute-start(bf16[384,512]{1,0:T(8,128)(2,1)S(1)} %copy-done.2), channel_id=1, source_target_pairs={{0,1},{1,0},{2,3},{3,2},{4,5},{5,4},{6,7},{7,6},{8,9},{9,8},{10,11... | collective-permute-start | bytes 1179656 | tf_op jit(solution)/shard_map/ppermute | solution.py:205
  75.7 3.2 %collective-permute-start.2 = (f32[96,512]{1,0:T(8,128)S(1)}, f32[96,512]{1,0:T(8,128)S(1)}, u32[]{:S(2)}, u32[]{:S(2)}) collective-permute-start(f32[96,512]{1,0:T(8,128)S(1)} %convert_reduce_fusion), channel_id=1, source_target_pairs={{0,4},{4,0},{1,5},{5,1},{2,6},{6,2},{3,7},{7,3},{8,12},{12,8},{9,1... | collective-permute-start | bytes 589832 | tf_op jit(solution)/shard_map/ppermute | solution.py:204
  78.9 10.3 %collective-permute-done.2 = f32[96,512]{1,0:T(8,128)S(1)} collective-permute-done((f32[96,512]{1,0:T(8,128)S(1)}, f32[96,512]{1,0:T(8,128)S(1)}, u32[]{:S(2)}, u32[]{:S(2)}) %collective-permute-start.2) | collective-permute-done | bytes 196640 | tf_op jit(solution)/shard_map/ppermute | solution.py:204
  89.2 2.5 %all-to-all-done.2 = bf16[8,96,512]{2,1,0:T(8,128)(2,1)S(1)} async-done(((bf16[8,96,512]{2,1,0:T(8,128)(2,1)}), bf16[8,96,512]{2,1,0:T(8,128)(2,1)S(1)}, u32[]{:S(2)}, u32[]{:S(2)}) %all-to-all-start.2) | async-done | bytes 786464 | tf_op jit(solution)/shard_map/all_to_all | solution.py:161
  92.7 5.0 %all-to-all-start.3 = ((bf16[8,96,512]{2,1,0:T(8,128)(2,1)}), bf16[8,96,512]{2,1,0:T(8,128)(2,1)S(1)}, u32[]{:S(2)}, u32[]{:S(2)}) async-start(bf16[8,96,512]{2,1,0:T(8,128)(2,1)} %broadcast_in_dim.7), calls=%async_computation.3 | async-start | bytes 1572864 | tf_op jit(solution)/shard_map/all_to_all | solution.py:161
  97.7 4.1 %collective-permute-start.4 = (bf16[768,512]{1,0:T(8,128)(2,1)S(1)}, bf16[768,512]{1,0:T(8,128)(2,1)S(1)}, u32[]{:S(2)}, u32[]{:S(2)}) collective-permute-start(bf16[768,512]{1,0:T(8,128)(2,1)S(1)} %bitcast.15), channel_id=1, source_target_pairs={{0,1},{1,0},{2,3},{3,2},{4,5},{5,4},{6,7},{7,6},{8,9},{9,8},{10,11... | collective-permute-start | bytes 2359304 | tf_op jit(solution)/shard_map/ppermute | solution.py:208
  101.8 1.9 %collective-permute-done.4.act_o = bf16[768,512]{1,0:T(8,128)(2,1)S(1)} collective-permute-done((bf16[768,512]{1,0:T(8,128)(2,1)S(1)}, bf16[768,512]{1,0:T(8,128)(2,1)S(1)}, u32[]{:S(2)}, u32[]{:S(2)}) %collective-permute-start.4) | collective-permute-done | bytes 786464 | tf_op jit(solution)/shard_map/ppermute | solution.py:208
  103.7 4.9 %all-to-all-done.3 = bf16[8,96,512]{2,1,0:T(8,128)(2,1)S(1)} async-done(((bf16[8,96,512]{2,1,0:T(8,128)(2,1)}), bf16[8,96,512]{2,1,0:T(8,128)(2,1)S(1)}, u32[]{:S(2)}, u32[]{:S(2)}) %all-to-all-start.3) | async-done | bytes 786464 | tf_op jit(solution)/shard_map/all_to_all | solution.py:161
  110.6 2.6 %shard_map.75 = bf16[384,512]{1,0:T(8,128)(2,1)S(1)} custom-call(s32[3]{0:T(128)S(1)} %pad_add_fusion.place, bf16[768,512]{1,0:T(8,128)(2,1)S(1)} %bitcast.16, bf16[768,512]{1,0:T(8,128)(2,1)S(1)} %collective-permute-done.4.act_o, bf16[768,512]{1,0:T(8,128)(2,1)S(1)} %bitcast.17, bf16[384,512]{1,0:T(8,128)(2,1)S(1)} %copy-done.3, ...), custom_call_target="tpu_custom_call" | custom-call | flops 1207959552 | bytes 4194304 | tf_op jit(solution)/shard_map/pallas_call | solution.py:141
  113.2 10.0 %all_to_all.36 = bf16[8,48,512]{2,1,0:T(8,128)(2,1)S(1)} all-to-all(bf16[8,48,512]{2,1,0:T(8,128)(2,1)S(1)} %bitcast.18), channel_id=1, replica_groups=mesh['z_hi'=2,'y'=8,'x'=4,'z_a'=2,'z_b'=2,'core'=2] {'x','z_b'}, dimensions={0} | all-to-all | bytes 786432 | tf_op jit(solution)/shard_map/all_to_all | solution.py:161
  123.2 6.1 %collective-permute-start.5 = (f32[48,512]{1,0:T(8,128)S(1)}, f32[48,512]{1,0:T(8,128)S(1)}, u32[]{:S(2)}, u32[]{:S(2)}) collective-permute-start(f32[48,512]{1,0:T(8,128)S(1)} %convert_reduce_fusion.3), channel_id=1, source_target_pairs={{0,4},{4,0},{1,5},{5,1},{2,6},{6,2},{3,7},{7,3},{8,12},{12,8},{9,1... | collective-permute-start | bytes 294920 | tf_op jit(solution)/shard_map/ppermute | solution.py:221
  129.3 3.0 %collective-permute-done.5 = f32[48,512]{1,0:T(8,128)S(1)} collective-permute-done((f32[48,512]{1,0:T(8,128)S(1)}, f32[48,512]{1,0:T(8,128)S(1)}, u32[]{:S(2)}, u32[]{:S(2)}) %collective-permute-start.5) | collective-permute-done | bytes 98336 | tf_op jit(solution)/shard_map/ppermute | solution.py:221
  132.4 9.3 %all_to_all.37 = bf16[8,48,512]{2,1,0:T(8,128)(2,1)S(1)} all-to-all(bf16[8,48,512]{2,1,0:T(8,128)(2,1)S(1)} %broadcast_in_dim.8), channel_id=1, replica_groups=mesh['z_hi'=2,'y'=8,'x'=4,'z_a'=2,'z_b'=2,'core'=2] {'x','z_b'}, dimensions={0} | all-to-all | bytes 786432 | tf_op jit(solution)/shard_map/all_to_all | solution.py:161
  141.8 7.6 %collective-permute-start.6 = (bf16[384,512]{1,0:T(8,128)(2,1)S(1)}, bf16[384,512]{1,0:T(8,128)(2,1)S(1)}, u32[]{:S(2)}, u32[]{:S(2)}) collective-permute-start(bf16[384,512]{1,0:T(8,128)(2,1)S(1)} %bitcast.12), channel_id=1, source_target_pairs={{0,1},{1,0},{2,3},{3,2},{4,5},{5,4},{6,7},{7,6},{8,9},{9,8},{10,11... | collective-permute-start | bytes 1179656 | tf_op jit(solution)/shard_map/ppermute | solution.py:224
  149.3 1.3 collective-permute-done.6.other
  151.8 18.4 %all_to_all.38 = bf16[16,24,512]{2,1,0:T(8,128)(2,1)S(1)} all-to-all(bf16[16,24,512]{2,1,0:T(8,128)(2,1)S(1)} %bitcast.14), channel_id=1, replica_groups=mesh['z_hi'=2,'y'=8,'x'=4,'z_a'=2,'z_b'=2,'core'=2] {'z_hi','y'}, dimensions={0} | all-to-all | bytes 786432 | tf_op jit(solution)/shard_map/all_to_all | solution.py:161
  (36 shorter events, 7.4 us)
Async XLA Ops:
  0.0 3.9 %copy-start = (bf16[512,1024]{1,0:T(8,128)(2,1)S(1)}, bf16[512,1024]{1,0:T(8,128)(2,1)}, u32[]{:S(2)}) copy-start(bf16[512,1024]{1,0:T(8,128)(2,1)} %b_out.1) | copy-start | bytes 3145732
  0.0 3.9 %copy-start.1 = (bf16[768,512]{1,0:T(8,128)(2,1)S(1)}, bf16[768,512]{1,0:T(8,128)(2,1)}, u32[]{:S(2)}) copy-start(bf16[768,512]{1,0:T(8,128)(2,1)} %grad) | copy-start | bytes 2359300
  3.8 10.8 %copy-start.8 = (bf16[768,512]{1,0:T(8,128)(2,1)S(1)}, bf16[768,512]{1,0:T(8,128)(2,1)}, u32[]{:S(2)}) copy-start(bf16[768,512]{1,0:T(8,128)(2,1)} %shard_map.73) | copy-start | bytes 2359300
  5.8 35.0 %collective-permute-start = (f32[768,512]{1,0:T(8,128)S(1)}, f32[768,512]{1,0:T(8,128)S(1)}, u32[]{:S(2)}, u32[]{:S(2)}) collective-permute-start(f32[768,512]{1,0:T(8,128)S(1)} %get-tuple-element.20), channel_id=1, source_target_pairs={{0,1},{1,0},{2,3},{3,2},{4,5},{5,4},{6,7},{7,6},{8,9},{9,8},{10,11... | collective-permute-start | bytes 4718600 | tf_op jit(solution)/shard_map/ppermute | solution.py:197
  41.9 24.3 %all-to-all-start.1 = ((bf16[8,96,512]{2,1,0:T(8,128)(2,1)}), bf16[8,96,512]{2,1,0:T(8,128)(2,1)S(1)}, u32[]{:S(2)}, u32[]{:S(2)}) async-start(bf16[8,96,512]{2,1,0:T(8,128)(2,1)} %bitcast.4), calls=%async_computation.1 | async-start | bytes 1572864 | tf_op jit(solution)/shard_map/all_to_all | solution.py:161
  46.5 19.6 %collective-permute-start.1 = (bf16[96,512]{1,0:T(8,128)(2,1)S(1)}, bf16[96,512]{1,0:T(8,128)(2,1)S(1)}, u32[]{:S(2)}, u32[]{:S(2)}) collective-permute-start(bf16[96,512]{1,0:T(8,128)(2,1)S(1)} %convert_element_type.32), channel_id=1, source_target_pairs={{0,256},{256,0},{1,257},{257,1},{2,258},{258,2},{3,259},{259,3},{4... | collective-permute-start | bytes 294920 | tf_op jit(solution)/shard_map/ppermute | solution.py:201
  66.3 4.6 %copy-start.2 = (bf16[384,512]{1,0:T(8,128)(2,1)S(1)}, bf16[384,512]{1,0:T(8,128)(2,1)}, u32[]{:S(2)}) copy-start(bf16[384,512]{1,0:T(8,128)(2,1)} %train) | copy-start | bytes 1179652
  67.3 24.5 %all-to-all-start.2 = ((bf16[8,96,512]{2,1,0:T(8,128)(2,1)}), bf16[8,96,512]{2,1,0:T(8,128)(2,1)S(1)}, u32[]{:S(2)}, u32[]{:S(2)}) async-start(bf16[8,96,512]{2,1,0:T(8,128)(2,1)} %broadcast_in_dim.6), calls=%async_computation.2 | async-start | bytes 1572864 | tf_op jit(solution)/shard_map/all_to_all | solution.py:161
  70.8 37.7 %copy-start.6 = (f32[16384]{0:T(1024)S(1)}, f32[16384]{0:T(1024)}, u32[]{:S(2)}) copy-start(f32[16384]{0:T(1024)} %param.13) | copy-start | bytes 196612
  70.9 37.7 %copy-start.7 = (f32[16384]{0:T(1024)S(1)}, f32[16384]{0:T(1024)}, u32[]{:S(2)}) copy-start(f32[16384]{0:T(1024)} %param.12) | copy-start | bytes 196612
  70.9 18.3 %collective-permute-start.3 = (bf16[384,512]{1,0:T(8,128)(2,1)S(1)}, bf16[384,512]{1,0:T(8,128)(2,1)S(1)}, u32[]{:S(2)}, u32[]{:S(2)}) collective-permute-start(bf16[384,512]{1,0:T(8,128)(2,1)S(1)} %copy-done.2), channel_id=1, source_target_pairs={{0,1},{1,0},{2,3},{3,2},{4,5},{5,4},{6,7},{7,6},{8,9},{9,8},{10,11... | collective-permute-start | bytes 1179656 | tf_op jit(solution)/shard_map/ppermute | solution.py:205
  75.7 13.5 %collective-permute-start.2 = (f32[96,512]{1,0:T(8,128)S(1)}, f32[96,512]{1,0:T(8,128)S(1)}, u32[]{:S(2)}, u32[]{:S(2)}) collective-permute-start(f32[96,512]{1,0:T(8,128)S(1)} %convert_reduce_fusion), channel_id=1, source_target_pairs={{0,4},{4,0},{1,5},{5,1},{2,6},{6,2},{3,7},{7,3},{8,12},{12,8},{9,1... | collective-permute-start | bytes 589832 | tf_op jit(solution)/shard_map/ppermute | solution.py:204
  89.2 3.5 %copy-start.4 = (bf16[384,512]{1,0:T(8,128)(2,1)}, bf16[384,512]{1,0:T(8,128)(2,1)S(1)}, u32[]{:S(2)}) copy-start(bf16[384,512]{1,0:T(8,128)(2,1)S(1)} %collective-permute-done.3.train_o) | copy-start | bytes 1179652
  92.7 15.9 %all-to-all-start.3 = ((bf16[8,96,512]{2,1,0:T(8,128)(2,1)}), bf16[8,96,512]{2,1,0:T(8,128)(2,1)S(1)}, u32[]{:S(2)}, u32[]{:S(2)}) async-start(bf16[8,96,512]{2,1,0:T(8,128)(2,1)} %broadcast_in_dim.7), calls=%async_computation.3 | async-start | bytes 1572864 | tf_op jit(solution)/shard_map/all_to_all | solution.py:161
  97.7 6.0 %collective-permute-start.4 = (bf16[768,512]{1,0:T(8,128)(2,1)S(1)}, bf16[768,512]{1,0:T(8,128)(2,1)S(1)}, u32[]{:S(2)}, u32[]{:S(2)}) collective-permute-start(bf16[768,512]{1,0:T(8,128)(2,1)S(1)} %bitcast.15), channel_id=1, source_target_pairs={{0,1},{1,0},{2,3},{3,2},{4,5},{5,4},{6,7},{7,6},{8,9},{9,8},{10,11... | collective-permute-start | bytes 2359304 | tf_op jit(solution)/shard_map/ppermute | solution.py:208
  108.6 1.0 copy-start.3
  109.6 1.0 copy-start.5
  123.2 9.2 %collective-permute-start.5 = (f32[48,512]{1,0:T(8,128)S(1)}, f32[48,512]{1,0:T(8,128)S(1)}, u32[]{:S(2)}, u32[]{:S(2)}) collective-permute-start(f32[48,512]{1,0:T(8,128)S(1)} %convert_reduce_fusion.3), channel_id=1, source_target_pairs={{0,4},{4,0},{1,5},{5,1},{2,6},{6,2},{3,7},{7,3},{8,12},{12,8},{9,1... | collective-permute-start | bytes 294920 | tf_op jit(solution)/shard_map/ppermute | solution.py:221
  141.8 8.9 %collective-permute-start.6 = (bf16[384,512]{1,0:T(8,128)(2,1)S(1)}, bf16[384,512]{1,0:T(8,128)(2,1)S(1)}, u32[]{:S(2)}, u32[]{:S(2)}) collective-permute-start(bf16[384,512]{1,0:T(8,128)(2,1)S(1)} %bitcast.12), channel_id=1, source_target_pairs={{0,1},{1,0},{2,3},{3,2},{4,5},{5,4},{6,7},{7,6},{8,9},{9,8},{10,11... | collective-permute-start | bytes 1179656 | tf_op jit(solution)/shard_map/ppermute | solution.py:224

commit v5 on v3

--- a/solution.py
+++ b/solution.py
@@ -64,25 +64,22 @@
     )
 
 
-def rotate_kernel(place, act, grad, b_in, b_out, b_in_o, grad_o, b_out_o, first, second):
+def rotate_kernel(place, act, grad, b_in, b_out, b_in_o, grad_o, b_out_o, out):
     half = grad.shape[1]
-    tile = 128
-    steps = first.shape[0] // tile
 
     def body(product):
-        for index, out in enumerate((first, second)):
-
-            @pl.loop(0, steps)
-            def _(m):
-                to = pl.ds(pl.multiple_of(m * tile, tile), tile)
-                product(out, to, pl.ds(pl.multiple_of((index * steps + m) * tile, tile), tile))
-
-    def joined(out, to, rows):
-        out[to, :half] = dot(act[rows, :], b_in[...]).astype(bf16)
-        out[to, half:] = dot(act[rows, :], b_in_o[...]).astype(bf16)
-
-    def added(out, to, rows):
-        out[to, :] = (dot(grad_o[rows, :], b_out_o[...]) + dot(grad[rows, :], b_out[...])).astype(bf16)
+        @pl.loop(0, out.shape[0] // TILE)
+        def _(m):
+            product(pl.ds(pl.multiple_of(m * TILE, TILE), TILE))
+
+    def joined(rows):
+        out[rows, :half] = dot(act[rows, :], b_in[...]).astype(bf16)
+        out[rows, half:] = dot(act[rows, :], b_in_o[...]).astype(bf16)
+
+    def added(rows):
+        out[rows, :] = (dot(grad_o[rows, :], b_out_o[...]) + dot(grad[rows, :], b_out[...])).astype(
+            bf16
+        )
 
     @pl.when(place[0] == 0)
     def _():
@@ -93,20 +90,16 @@
         body(added)
 
 
-def outer_kernel(queries, place, damp, own_a, own_b, other_a, other_b, train, train_o, e_out, e_in, out):
+def outer_kernel(queries, place, damp, own, other, train, train_o, e_out, e_in, out):
     half = train.shape[1]
     lanes = e_in.shape[1]
-    units = 8 * lanes
     e_rows = e_in[pl.ds(pl.multiple_of(place[1] * 8, 8), 8), :]
-    e_row = jnp.concatenate([e_rows[r : r + 1, :] for r in range(units // lanes)], axis=1)
+    e_row = jnp.concatenate([e_rows[r : r + 1, :] for r in range(8)], axis=1)
     e_cols = jnp.transpose(e_out[pl.ds(pl.multiple_of(place[2] * 8, 8), 8), :])
 
-    def body(acts, grads, first, left, right):
+    def body(act, grad, first, left, right):
         for start in range(0, half, TILE):
-            outer = sum(
-                dot_tn(grad[:, first + start : first + start + TILE], act[...])
-                for act, grad in zip(acts, grads)
-            )
+            outer = dot_tn(grad[:, first + start : first + start + TILE], act[...])
             r = (first + start) // lanes
             e_col = jnp.concatenate([e_cols[:, r + q : r + q + 1] for q in range(TILE // lanes)], axis=0)
             scaled = (outer / queries / (e_col * e_row + damp[0])).astype(bf16)
@@ -116,11 +109,11 @@
 
     @pl.when(place[0] == 0)
     def _():
-        body((own_a, own_b), (other_a, other_b), 0, train, train_o)
+        body(own, other, 0, train, train_o)
 
     @pl.when(place[0] == 1)
     def _():
-        body((other_a, other_b), (own_a, own_b), half, train_o, train)
+        body(other, own, half, train_o, train)
 
 
 def back_kernel(place, own, other, b_out, out):
@@ -196,39 +189,28 @@
     basis_in_o, basis_out_o, grad_o, damp = lax.optimization_barrier(
         (basis_in_o, basis_out_o, grad_o, damp)
     )
-    first, second = call(
+    part = call(
         rotate_kernel,
         (place, query_act, query_grad, basis_in, basis_out, basis_in_o, grad_o, basis_out_o),
         [SMEM] + [VMEM] * 7,
-        [shape((queries // 2, width), bf16)] * 2,
-        [VMEM] * 2,
+        shape((queries, width), bf16),
+        VMEM,
         2 * queries * width * width,
         32,
     )
-
-    def scatter(part):
-        return summed(mixed(part.reshape(8, -1, width)))
-
-    def swap(sums):
-        return lax.ppermute(sums.astype(bf16), ALL, mixed_pairs()).astype(f32)
-
-    sum_a = scatter(first)
-    sum_a, second, train_rot = lax.optimization_barrier((sum_a, second, train_rot))
-    far_a = swap(sum_a)
+    eighth = summed(mixed(part.reshape(8, -1, width)))
+    eighth, train_rot = lax.optimization_barrier((eighth, train_rot))
+    far = lax.ppermute(eighth.astype(bf16), ALL, mixed_pairs()).astype(f32)
     train_o = lax.ppermute(train_rot, "core", SWAP)
-    sum_b = scatter(second)
-    far_a, sum_b, train_o = lax.optimization_barrier((far_a, sum_b, train_o))
-    far_b = swap(sum_b)
-    own_a = mixed(spread((sum_a + far_a).astype(bf16), 8)).reshape(queries // 2, width)
-    far_b, own_a = lax.optimization_barrier((far_b, own_a))
-    other_a = lax.ppermute(own_a, "core", SWAP)
-    own_b = mixed(spread((sum_b + far_b).astype(bf16), 8)).reshape(queries // 2, width)
-    other_b = lax.ppermute(own_b, "core", SWAP)
+    rot = (eighth + far).astype(bf16)
+    rot, train_o = lax.optimization_barrier((rot, train_o))
+    own = mixed(spread(rot, 8)).reshape(queries, width)
+    other = lax.ppermute(own, "core", SWAP)
 
     partial_inner = call(
         functools.partial(outer_kernel, queries),
-        (place, damp, own_a, own_b, other_a, other_b, train_rot, train_o, e_out, e_in),
-        [SMEM] * 2 + [VMEM] * 8,
+        (place, damp, own, other, train_rot, train_o, e_out, e_in),
+        [SMEM] * 2 + [VMEM] * 6,
         shape((train, half), bf16),
         VMEM,
         2 * queries * width * half + 2 * train * width * half,

time: 174 us -> 160 us (0.920)
  starting transfers between devices: 86.1 us -> 57.8 us
  blocking collectives: 56 us -> 78.4 us
  waiting for transfers between devices: 15 us -> 10.7 us
  Pallas kernels: 9.86 us -> 7.8 us
    ppermute x4 -> x2, starting transfers between devices: 40.4 us -> 16.4 us  [the longest x1 13 us: per_device(): other = lax.ppermute(own, 'core', SWAP)]
    all_to_all x1 -> x2, blocking collectives: 11.4 us -> 33.9 us  [the longest x1 18 us: per_device(): own = mixed(spread(rot, 8)).reshape(queries, width)]
    all_to_all x3 -> x0, starting transfers between devices: 13.6 us -> none  [the longest x1 5.82 us: per_device(): mixed(spread((sum_a + far_a).astype(bf16), 8)).reshape(queries // 2, width)]
    ppermute x1, starting transfers between devices: 11.2 us -> 20.9 us  [per_device(): train_o = lax.ppermute(train_rot, 'core', SWAP)]
    all_to_all x3 -> x0, waiting for transfers between devices: 3.34 us -> none  [the longest x1 3.34 us: per_device(): mixed(spread((sum_a + far_a).astype(bf16), 8)).reshape(queries // 2, width)]
    ppermute x4 -> x2, waiting for transfers between devices: 6.26 us -> 3.02 us  [the longest x1 3.01 us: per_device(): other = lax.ppermute(own, 'core', SWAP)]
    ppermute x1, starting transfers between devices: 5.13 us -> 3.03 us  [per_device(): inner_sum = inner_sum + lax.ppermute(inner_sum, 'z_a', SWAP)]
    pallas_call x4, Pallas kernels: 9.86 us -> 7.8 us  [call(): pl.pallas_call(kernel, out_shape=shapes, in_specs=specs, out_specs=out_sp...]
  transfers between devices with their start and end apart: 13 -> 8, of which waited for: 7 -> 5; matrix products, arithmetic and copies ran while one was open for 0% -> 0% of each run, Pallas kernels for 0% -> 0%
where the time goes in v5:
time: 160 us; the launch traced here: 159 us
  blocking collectives  78.4 us (49%)
  starting transfers between devices  57.8 us (36%)
  waiting for transfers between devices  10.7 us (7%)
  Pallas kernels  7.8 us (5%)
  local copies, waits for them, and re-layouts  2.62 us (2%)
    all_to_all x1, blocking collectives, per_device(): lax.all_to_all(partial_out.reshape(16, -1, half), ROW, 0, 0, tiled=True)  22 us
    ppermute x1, starting transfers between devices, per_device(): train_o = lax.ppermute(train_rot, 'core', SWAP)  20.9 us
    all_to_all x1, blocking collectives, per_device(): own = mixed(spread(rot, 8)).reshape(queries, width)  18 us
    all_to_all x1, blocking collectives, per_device(): eighth = summed(mixed(part.reshape(8, -1, width)))  15.9 us
    all_to_all x1, blocking collectives, per_device(): inner_sum = summed(near(partial_inner.reshape(8, -1, half)))  13.2 us
    ppermute x1, starting transfers between devices, per_device(): other = lax.ppermute(own, 'core', SWAP)  13 us
    all_to_all x1, blocking collectives, per_device(): near(spread((inner_sum * factor).astype(bf16), 8)).reshape(train, half)  9.34 us
    ppermute x1, starting transfers between devices, per_device(): basis_in_o = lax.ppermute(basis_in, 'core', [(1, 0)])  8.84 us
  transfers between devices with their start and end apart: 8, of which 5 were waited for; matrix products, arithmetic and copies ran while one was open for 0% of the time, Pallas kernels for 0%

profile of v5, /device:TPU:1, one launch (start us, length us, event | category | flops | bytes accessed | tf_op | source)
XLA Modules:
  0.0 158.8 jit_solution(10654296915599395475)
XLA Ops:
  0.0 8.8 %collective-permute-start = (bf16[1024,512]{1,0:T(8,128)(2,1)}, bf16[1024,512]{1,0:T(8,128)(2,1)S(1)}, u32[]{:S(2)}, u32[]{:S(2)}) collective-permute-start(bf16[1024,512]{1,0:T(8,128)(2,1)} %b_in.1), channel_id=1, source_target_pairs={{1,0},{3,2},{5,4},{7,6},{9,8},{11,10},{13,12},{15,14},{17,16},{19,... | collective-permute-start | bytes 3145736 | tf_op jit(solution)/shard_map/ppermute | solution.py:176
  8.8 1.3 collective-permute-start.1
  10.1 1.3 collective-permute-start.2
  11.5 0.8 copy-done.5
  12.4 0.8 copy-done.7
  13.9 0.8 collective-permute-done.2.grad_o
  15.5 2.7 %shard_map.74 = bf16[768,1024]{1,0:T(8,128)(2,1)S(1)} custom-call(s32[3]{0:T(128)S(1)} %pad_add_fusion.place, bf16[768,1024]{1,0:T(8,128)(2,1)S(1)} %copy-done.1, bf16[768,512]{1,0:T(8,128)(2,1)S(1)} %copy-done.3, bf16[1024,512]{1,0:T(8,128)(2,1)S(1)} %copy-done.2, bf16[512,1024]{1,0:T(8,128)(2,1)S(1)} %copy-done, ...), custom_call_target="tpu_custom_call" | custom-call | flops 1610612736 | bytes 4194304 | tf_op jit(solution)/shard_map/pallas_call | solution.py:137
  18.2 15.9 %all_to_all.25 = bf16[8,96,1024]{2,1,0:T(8,128)(2,1)S(1)} all-to-all(bf16[8,96,1024]{2,1,0:T(8,128)(2,1)S(1)} %bitcast.10), channel_id=1, replica_groups={{0,32,64,96,128,160,192,224},{2,34,66,98,130,162,194,226},{4,36,68,100,..., dimensions={0} | all-to-all | bytes 3145728 | tf_op jit(solution)/shard_map/all_to_all | solution.py:201
  34.4 3.3 %collective-permute-start.3 = (bf16[96,1024]{1,0:T(8,128)(2,1)S(1)}, bf16[96,1024]{1,0:T(8,128)(2,1)S(1)}, u32[]{:S(2)}, u32[]{:S(2)}) collective-permute-start(bf16[96,1024]{1,0:T(8,128)(2,1)S(1)} %convert_element_type.22), channel_id=1, source_target_pairs={{0,256},{1,5},{2,258},{3,7},{4,260},{5,1},{6,262},{7,3},{8,264},{9... | collective-permute-start | bytes 589832 | tf_op jit(solution)/shard_map/ppermute | solution.py:203
  37.7 20.9 %collective-permute-start.4 = (bf16[384,512]{1,0:T(8,128)(2,1)S(1)}, bf16[384,512]{1,0:T(8,128)(2,1)S(1)}, u32[]{:S(2)}, u32[]{:S(2)}) collective-permute-start(bf16[384,512]{1,0:T(8,128)(2,1)S(1)} %copy-done.4), channel_id=1, source_target_pairs={{0,1},{1,0},{2,3},{3,2},{4,5},{5,4},{6,7},{7,6},{8,9},{9,8},{10,11... | collective-permute-start | bytes 1179656 | tf_op jit(solution)/shard_map/ppermute | solution.py:204
  58.7 1.3 collective-permute-done.4.train_o
  60.2 18.0 %all_to_all.26 = bf16[8,96,1024]{2,1,0:T(8,128)(2,1)S(1)} all-to-all(bf16[8,96,1024]{2,1,0:T(8,128)(2,1)S(1)} %broadcast_in_dim.4), channel_id=1, replica_groups={{0,32,64,96,128,160,192,224},{2,34,66,98,130,162,194,226},{4,36,68,100,..., dimensions={0} | all-to-all | bytes 3145728 | tf_op jit(solution)/shard_map/all_to_all | solution.py:207
  78.2 13.0 %collective-permute-start.5 = (bf16[768,1024]{1,0:T(8,128)(2,1)S(1)}, bf16[768,1024]{1,0:T(8,128)(2,1)S(1)}, u32[]{:S(2)}, u32[]{:S(2)}) collective-permute-start(bf16[768,1024]{1,0:T(8,128)(2,1)S(1)} %bitcast.11), channel_id=1, source_target_pairs={{0,1},{1,0},{2,3},{3,2},{4,5},{5,4},{6,7},{7,6},{8,9},{9,8},{10,11... | collective-permute-start | bytes 4718600 | tf_op jit(solution)/shard_map/ppermute | solution.py:208
  91.2 3.0 %collective-permute-done.5.other = bf16[768,1024]{1,0:T(8,128)(2,1)S(1)} collective-permute-done((bf16[768,1024]{1,0:T(8,128)(2,1)S(1)}, bf16[768,1024]{1,0:T(8,128)(2,1)S(1)}, u32[]{:S(2)}, u32[]{:S(2)}) %collective-permute-start.5) | collective-permute-done | bytes 1572896 | tf_op jit(solution)/shard_map/ppermute | solution.py:208
  94.2 3.3 %shard_map.75 = bf16[384,512]{1,0:T(8,128)(2,1)S(1)} custom-call(s32[3]{0:T(128)S(1)} %pad_add_fusion.place, f32[1]{0:T(128)} %shard_map.73.damp, bf16[768,1024]{1,0:T(8,128)(2,1)S(1)} %bitcast.12, bf16[768,1024]{1,0:T(8,128)(2,1)S(1)} %collective-permute-done.5.other, bf16[384,512]{1,0:T(8,128)(2,1)S(1)} %copy-done.4, ...), custom_call_target="tpu_custom_call" | custom-call | flops 1207959552 | bytes 4194304 | tf_op jit(solution)/shard_map/pallas_call | solution.py:137
  97.6 13.2 %all_to_all.27 = bf16[8,48,512]{2,1,0:T(8,128)(2,1)S(1)} all-to-all(bf16[8,48,512]{2,1,0:T(8,128)(2,1)S(1)} %bitcast.16), channel_id=1, replica_groups=mesh['z_hi'=2,'y'=8,'x'=4,'z_a'=2,'z_b'=2,'core'=2] {'x','z_b'}, dimensions={0} | all-to-all | bytes 786432 | tf_op jit(solution)/shard_map/all_to_all | solution.py:219
  110.8 3.0 %collective-permute-start.6 = (f32[48,512]{1,0:T(8,128)S(1)}, f32[48,512]{1,0:T(8,128)S(1)}, u32[]{:S(2)}, u32[]{:S(2)}) collective-permute-start(f32[48,512]{1,0:T(8,128)S(1)} %convert_reduce_fusion.2), channel_id=1, source_target_pairs={{0,4},{4,0},{1,5},{5,1},{2,6},{6,2},{3,7},{7,3},{8,12},{12,8},{9,1... | collective-permute-start | bytes 294920 | tf_op jit(solution)/shard_map/ppermute | solution.py:220
  113.9 4.3 %collective-permute-done.6 = f32[48,512]{1,0:T(8,128)S(1)} collective-permute-done((f32[48,512]{1,0:T(8,128)S(1)}, f32[48,512]{1,0:T(8,128)S(1)}, u32[]{:S(2)}, u32[]{:S(2)}) %collective-permute-start.6) | collective-permute-done | bytes 98336 | tf_op jit(solution)/shard_map/ppermute | solution.py:220
  118.2 9.3 %all_to_all.28 = bf16[8,48,512]{2,1,0:T(8,128)(2,1)S(1)} all-to-all(bf16[8,48,512]{2,1,0:T(8,128)(2,1)S(1)} %broadcast_in_dim.5), channel_id=1, replica_groups=mesh['z_hi'=2,'y'=8,'x'=4,'z_a'=2,'z_b'=2,'core'=2] {'x','z_b'}, dimensions={0} | all-to-all | bytes 786432 | tf_op jit(solution)/shard_map/all_to_all | solution.py:222
  127.5 6.1 %collective-permute-start.7 = (bf16[384,512]{1,0:T(8,128)(2,1)S(1)}, bf16[384,512]{1,0:T(8,128)(2,1)S(1)}, u32[]{:S(2)}, u32[]{:S(2)}) collective-permute-start(bf16[384,512]{1,0:T(8,128)(2,1)S(1)} %bitcast.13), channel_id=1, source_target_pairs={{0,1},{1,0},{2,3},{3,2},{4,5},{5,4},{6,7},{7,6},{8,9},{9,8},{10,11... | collective-permute-start | bytes 1179656 | tf_op jit(solution)/shard_map/ppermute | solution.py:223
  133.6 1.3 collective-permute-done.7.other
  135.0 1.2 shard_map.76
  136.1 22.0 %all_to_all.29 = bf16[16,24,512]{2,1,0:T(8,128)(2,1)S(1)} all-to-all(bf16[16,24,512]{2,1,0:T(8,128)(2,1)S(1)} %bitcast.15), channel_id=1, replica_groups=mesh['z_hi'=2,'y'=8,'x'=4,'z_a'=2,'z_b'=2,'core'=2] {'z_hi','y'}, dimensions={0} | all-to-all | bytes 786432 | tf_op jit(solution)/shard_map/all_to_all | solution.py:233
  158.1 0.7 convert_reduce_fusion.1
  (28 shorter events, 2.1 us)
Async XLA Ops:
  0.0 14.7 %collective-permute-start = (bf16[1024,512]{1,0:T(8,128)(2,1)}, bf16[1024,512]{1,0:T(8,128)(2,1)S(1)}, u32[]{:S(2)}, u32[]{:S(2)}) collective-permute-start(bf16[1024,512]{1,0:T(8,128)(2,1)} %b_in.1), channel_id=1, source_target_pairs={{1,0},{3,2},{5,4},{7,6},{9,8},{11,10},{13,12},{15,14},{17,16},{19,... | collective-permute-start | bytes 3145736 | tf_op jit(solution)/shard_map/ppermute | solution.py:176
  8.8 5.9 %collective-permute-start.1 = (bf16[512,1024]{1,0:T(8,128)(2,1)}, bf16[512,1024]{1,0:T(8,128)(2,1)S(1)}, u32[]{:S(2)}, u32[]{:S(2)}) collective-permute-start(bf16[512,1024]{1,0:T(8,128)(2,1)} %b_out.3), channel_id=1, source_target_pairs={{0,1},{2,3},{4,5},{6,7},{8,9},{10,11},{12,13},{14,15},{16,17},{18,... | collective-permute-start | bytes 3145736 | tf_op jit(solution)/shard_map/ppermute | solution.py:177
  10.1 4.6 %collective-permute-start.2 = (bf16[768,512]{1,0:T(8,128)(2,1)}, bf16[768,512]{1,0:T(8,128)(2,1)S(1)}, u32[]{:S(2)}, u32[]{:S(2)}) collective-permute-start(bf16[768,512]{1,0:T(8,128)(2,1)} %grad.1), channel_id=1, source_target_pairs={{0,1},{2,3},{4,5},{6,7},{8,9},{10,11},{12,13},{14,15},{16,17},{18,... | collective-permute-start | bytes 2359304 | tf_op jit(solution)/shard_map/ppermute | solution.py:178
  11.5 0.8 copy-start.5
  12.4 0.8 copy-start.7
  13.2 1.5 copy-start
  13.2 1.7 %copy-start.1 = (bf16[768,1024]{1,0:T(8,128)(2,1)S(1)}, bf16[768,1024]{1,0:T(8,128)(2,1)}, u32[]{:S(2)}) copy-start(bf16[768,1024]{1,0:T(8,128)(2,1)} %act.1) | copy-start | bytes 4718596
  13.2 2.0 %copy-start.2 = (bf16[1024,512]{1,0:T(8,128)(2,1)S(1)}, bf16[1024,512]{1,0:T(8,128)(2,1)}, u32[]{:S(2)}) copy-start(bf16[1024,512]{1,0:T(8,128)(2,1)} %b_in.1) | copy-start | bytes 3145732
  13.2 2.2 %copy-start.3 = (bf16[768,512]{1,0:T(8,128)(2,1)S(1)}, bf16[768,512]{1,0:T(8,128)(2,1)}, u32[]{:S(2)}) copy-start(bf16[768,512]{1,0:T(8,128)(2,1)} %grad.1) | copy-start | bytes 2359300
  34.0 3.7 %copy-start.4 = (bf16[384,512]{1,0:T(8,128)(2,1)S(1)}, bf16[384,512]{1,0:T(8,128)(2,1)}, u32[]{:S(2)}) copy-start(bf16[384,512]{1,0:T(8,128)(2,1)} %train) | copy-start | bytes 1179652
  34.4 24.3 %collective-permute-start.3 = (bf16[96,1024]{1,0:T(8,128)(2,1)S(1)}, bf16[96,1024]{1,0:T(8,128)(2,1)S(1)}, u32[]{:S(2)}, u32[]{:S(2)}) collective-permute-start(bf16[96,1024]{1,0:T(8,128)(2,1)S(1)} %convert_element_type.22), channel_id=1, source_target_pairs={{0,256},{1,5},{2,258},{3,7},{4,260},{5,1},{6,262},{7,3},{8,264},{9... | collective-permute-start | bytes 589832 | tf_op jit(solution)/shard_map/ppermute | solution.py:203
  37.7 22.3 %collective-permute-start.4 = (bf16[384,512]{1,0:T(8,128)(2,1)S(1)}, bf16[384,512]{1,0:T(8,128)(2,1)S(1)}, u32[]{:S(2)}, u32[]{:S(2)}) collective-permute-start(bf16[384,512]{1,0:T(8,128)(2,1)S(1)} %copy-done.4), channel_id=1, source_target_pairs={{0,1},{1,0},{2,3},{3,2},{4,5},{5,4},{6,7},{7,6},{8,9},{9,8},{10,11... | collective-permute-start | bytes 1179656 | tf_op jit(solution)/shard_map/ppermute | solution.py:204
  60.2 34.1 %copy-start.6 = (f32[16384]{0:T(1024)S(1)}, f32[16384]{0:T(1024)}, u32[]{:S(2)}) copy-start(f32[16384]{0:T(1024)} %param.12) | copy-start | bytes 196612
  60.2 34.1 %copy-start.8 = (f32[16384]{0:T(1024)S(1)}, f32[16384]{0:T(1024)}, u32[]{:S(2)}) copy-start(f32[16384]{0:T(1024)} %param.13) | copy-start | bytes 196612
  78.2 16.0 %collective-permute-start.5 = (bf16[768,1024]{1,0:T(8,128)(2,1)S(1)}, bf16[768,1024]{1,0:T(8,128)(2,1)S(1)}, u32[]{:S(2)}, u32[]{:S(2)}) collective-permute-start(bf16[768,1024]{1,0:T(8,128)(2,1)S(1)} %bitcast.11), channel_id=1, source_target_pairs={{0,1},{1,0},{2,3},{3,2},{4,5},{5,4},{6,7},{7,6},{8,9},{9,8},{10,11... | collective-permute-start | bytes 4718600 | tf_op jit(solution)/shard_map/ppermute | solution.py:208
  110.8 7.3 %collective-permute-start.6 = (f32[48,512]{1,0:T(8,128)S(1)}, f32[48,512]{1,0:T(8,128)S(1)}, u32[]{:S(2)}, u32[]{:S(2)}) collective-permute-start(f32[48,512]{1,0:T(8,128)S(1)} %convert_reduce_fusion.2), channel_id=1, source_target_pairs={{0,4},{4,0},{1,5},{5,1},{2,6},{6,2},{3,7},{7,3},{8,12},{12,8},{9,1... | collective-permute-start | bytes 294920 | tf_op jit(solution)/shard_map/ppermute | solution.py:220
  127.5 7.4 %collective-permute-start.7 = (bf16[384,512]{1,0:T(8,128)(2,1)S(1)}, bf16[384,512]{1,0:T(8,128)(2,1)S(1)}, u32[]{:S(2)}, u32[]{:S(2)}) collective-permute-start(bf16[384,512]{1,0:T(8,128)(2,1)S(1)} %bitcast.13), channel_id=1, source_target_pairs={{0,1},{1,0},{2,3},{3,2},{4,5},{5,4},{6,7},{7,6},{8,9},{9,8},{10,11... | collective-permute-start | bytes 1179656 | tf_op jit(solution)/shard_map/ppermute | solution.py:223

commit v6 on v4

--- a/solution.py
+++ b/solution.py
@@ -198,15 +198,18 @@
 
     sum_act = summed(exchanged(act_part.reshape(8, -1, half), "y"))
     sum_act, grad_part = lax.optimization_barrier((sum_act, grad_part))
+    sum_grad = summed(exchanged(grad_part.reshape(8, -1, half), NEAR))
+    sum_act, sum_grad, train_rot = lax.optimization_barrier((sum_act, sum_grad, train_rot))
     far_act = lax.ppermute(sum_act.astype(bf16), "z_hi", SWAP).astype(f32)
-    sum_grad = summed(exchanged(grad_part.reshape(8, -1, half), NEAR))
-    far_act, sum_grad, train_rot = lax.optimization_barrier((far_act, sum_grad, train_rot))
-    far_grad = lax.ppermute(sum_grad, "z_a", SWAP)
+    far_grad = lax.ppermute(sum_grad.astype(bf16), "z_a", SWAP).astype(f32)
+    act_sum, grad_sum = (sum_act + far_act).astype(bf16), (sum_grad + far_grad).astype(bf16)
+    act_sum, grad_sum, train_rot = lax.optimization_barrier((act_sum, grad_sum, train_rot))
+    act = exchanged(spread(act_sum, 8), "y").reshape(queries, half)
+    grad_sum, act, train_rot = lax.optimization_barrier((grad_sum, act, train_rot))
+    act_o = lax.ppermute(act, "core", SWAP)
+    train_rot = train_rot.reshape(2, 8, -1, half).swapaxes(0, 1).reshape(train, half)
     train_o = lax.ppermute(train_rot, "core", SWAP)
-    act = exchanged(spread((sum_act + far_act).astype(bf16), 8), "y").reshape(queries, half)
-    far_grad, act, train_o = lax.optimization_barrier((far_grad, act, train_o))
-    act_o = lax.ppermute(act, "core", SWAP)
-    grad = exchanged(spread((sum_grad + far_grad).astype(bf16), 8), NEAR).reshape(queries, half)
+    grad = exchanged(spread(grad_sum, 8), NEAR).reshape(queries, half)
 
     partial_inner = call(
         functools.partial(outer_kernel, queries),
@@ -231,7 +234,10 @@
         2 * train * half * width,
         32,
     )
-    return summed(exchanged(partial_out.reshape(16, -1, half), ROW))
+    rows = summed(exchanged(partial_out.reshape(8, -1, half), "y")).reshape(2, -1, half)
+    z = lax.axis_index("z_hi")
+    mine, theirs = (lax.dynamic_index_in_dim(rows, i, 0, keepdims=False) for i in (z, 1 - z))
+    return mine + lax.ppermute(theirs, "z_hi", SWAP)
 
 
 def solution(mesh):

time: 172 us -> 190 us (1.10)
  blocking collectives: 63.8 us -> 85.4 us
  starting transfers between devices: 57.4 us -> 52.9 us
    all_to_all x4 -> x5, blocking collectives: 63.8 us -> 85.4 us  [exchanged(): return lax.all_to_all(array, axes, 0, 0, tiled=True)]
    all_to_all x3 -> x2, waiting for transfers between devices: 7.42 us -> 18.1 us  [exchanged(): return lax.all_to_all(array, axes, 0, 0, tiled=True)]
    ppermute x1, waiting for transfers between devices: 9.85 us -> 0.01 us  [per_device(): far_act = lax.ppermute(sum_act.astype(bf16), 'z_hi', SWAP).astype(f32)]
    ppermute x1 -> x2, starting transfers between devices: 3.18 us -> 8.93 us  [the longest x1 4.92 us: per_device(): return mine + lax.ppermute(theirs, 'z_hi', SWAP)]
    all_to_all x3 -> x2, starting transfers between devices: 13.2 us -> 7.63 us  [exchanged(): return lax.all_to_all(array, axes, 0, 0, tiled=True)]
    ppermute x1, starting transfers between devices: 4.8 us -> 1.92 us  [per_device(): train_o = lax.ppermute(train_rot, 'core', SWAP)]
    ppermute x1 -> x2, waiting for transfers between devices: 10.3 us -> 11.1 us  [the longest x1 6.44 us: per_device(): far_grad = lax.ppermute(sum_grad.astype(bf16), 'z_a', SWAP).astype(f32)]
where the time goes in v6:
time: 190 us
  blocking collectives  85.4 us (45%)
  starting transfers between devices  52.9 us (28%)
  waiting for transfers between devices  35.2 us (19%)
  Pallas kernels  10 us (5%)
  local copies, waits for them, and re-layouts  4.28 us (2%)
    all_to_all x5, blocking collectives, exchanged(): return lax.all_to_all(array, axes, 0, 0, tiled=True)  85.4 us
    all_to_all x2, waiting for transfers between devices, exchanged(): return lax.all_to_all(array, axes, 0, 0, tiled=True)  18.1 us
    pallas_call x4, Pallas kernels, call(): pl.pallas_call(kernel, out_shape=shapes, in_specs=specs, out_specs=out_sp...  10 us
    ppermute x1, starting transfers between devices, per_device(): far_act = lax.ppermute(sum_act.astype(bf16), 'z_hi', SWAP).astype(f32)  9.74 us
    ppermute x1, starting transfers between devices, per_device(): grad_part = (keep + lax.ppermute(send, 'core', SWAP)).astype(bf16)  8.79 us
    all_to_all x2, starting transfers between devices, exchanged(): return lax.all_to_all(array, axes, 0, 0, tiled=True)  7.63 us
    ppermute x1, waiting for transfers between devices, per_device(): far_grad = lax.ppermute(sum_grad.astype(bf16), 'z_a', SWAP).astype(f32)  6.44 us
    ppermute x1, starting transfers between devices, per_device(): inner_o = lax.ppermute(inner, 'core', SWAP)  6.13 us
  transfers between devices with their start and end apart: 10, of which 7 were waited for; matrix products, arithmetic and copies ran while one was open for 0% of the time, Pallas kernels for 0%

profile of v6, /device:TPU:1, one launch (start us, length us, event | category | flops | bytes accessed | tf_op | source)
XLA Modules:
  0.0 189.6 jit_solution(2401087595402074960)
XLA Ops:
  0.0 3.7 %shard_map.73 = bf16[768,512]{1,0:T(8,128)(2,1)} custom-call(bf16[768,1024]{1,0:T(8,128)(2,1)} %act.1, bf16[1024,512]{1,0:T(8,128)(2,1)} %weight.2), custom_call_target="tpu_custom_call" | custom-call | flops 805306368 | bytes 4194304 | tf_op jit(solution)/shard_map/pallas_call | solution.py:141
  4.9 1.9 shard_map.74
  6.8 8.8 %collective-permute-start = (f32[768,512]{1,0:T(8,128)S(1)}, f32[768,512]{1,0:T(8,128)S(1)}, u32[]{:S(2)}, u32[]{:S(2)}) collective-permute-start(f32[768,512]{1,0:T(8,128)S(1)} %get-tuple-element.23), channel_id=1, source_target_pairs={{0,1},{1,0},{2,3},{3,2},{4,5},{5,4},{6,7},{7,6},{8,9},{9,8},{10,11... | collective-permute-start | bytes 4718600 | tf_op jit(solution)/shard_map/ppermute | solution.py:197
  15.6 26.0 %all_to_all.35 = bf16[8,96,512]{2,1,0:T(8,128)(2,1)S(1)} all-to-all(bf16[8,96,512]{2,1,0:T(8,128)(2,1)S(1)} %bitcast.31), channel_id=1, replica_groups=mesh['z_hi'=2,'y'=8,'x'=4,'z_a'=2,'z_b'=2,'core'=2] {'y'}, dimensions={0} | all-to-all | bytes 1572864 | tf_op jit(solution)/shard_map/all_to_all | solution.py:161
  42.2 16.4 %all_to_all.36 = bf16[8,96,512]{2,1,0:T(8,128)(2,1)S(1)} all-to-all(bf16[8,96,512]{2,1,0:T(8,128)(2,1)S(1)} %bitcast.32), channel_id=1, replica_groups=mesh['z_hi'=2,'y'=8,'x'=4,'z_a'=2,'z_b'=2,'core'=2] {'x','z_b'}, dimensions={0} | all-to-all | bytes 1572864 | tf_op jit(solution)/shard_map/all_to_all | solution.py:161
  58.8 9.7 %collective-permute-start.1 = (bf16[96,512]{1,0:T(8,128)(2,1)S(1)}, bf16[96,512]{1,0:T(8,128)(2,1)S(1)}, u32[]{:S(2)}, u32[]{:S(2)}) collective-permute-start(bf16[96,512]{1,0:T(8,128)(2,1)S(1)} %convert_element_type.39), channel_id=1, source_target_pairs={{0,256},{256,0},{1,257},{257,1},{2,258},{258,2},{3,259},{259,3},{4... | collective-permute-start | bytes 294920 | tf_op jit(solution)/shard_map/ppermute | solution.py:203
  68.5 4.0 %collective-permute-start.2 = (bf16[96,512]{1,0:T(8,128)(2,1)S(1)}, bf16[96,512]{1,0:T(8,128)(2,1)S(1)}, u32[]{:S(2)}, u32[]{:S(2)}) collective-permute-start(bf16[96,512]{1,0:T(8,128)(2,1)S(1)} %convert_element_type.42), channel_id=1, source_target_pairs={{0,4},{4,0},{1,5},{5,1},{2,6},{6,2},{3,7},{7,3},{8,12},{12,8},{9,1... | collective-permute-start | bytes 294920 | tf_op jit(solution)/shard_map/ppermute | solution.py:204
  72.6 6.4 %collective-permute-done.2 = bf16[96,512]{1,0:T(8,128)(2,1)S(1)} collective-permute-done((bf16[96,512]{1,0:T(8,128)(2,1)S(1)}, bf16[96,512]{1,0:T(8,128)(2,1)S(1)}, u32[]{:S(2)}, u32[]{:S(2)}) %collective-permute-start.2) | collective-permute-done | bytes 98336 | tf_op jit(solution)/shard_map/ppermute | solution.py:204
  79.1 24.1 %all_to_all.37 = bf16[8,96,512]{2,1,0:T(8,128)(2,1)S(1)} all-to-all(bf16[8,96,512]{2,1,0:T(8,128)(2,1)S(1)} %broadcast_in_dim.6), channel_id=1, replica_groups=mesh['z_hi'=2,'y'=8,'x'=4,'z_a'=2,'z_b'=2,'core'=2] {'y'}, dimensions={0} | all-to-all | bytes 1572864 | tf_op jit(solution)/shard_map/all_to_all | solution.py:161
  104.2 4.2 %all-to-all-start.3 = ((bf16[8,96,512]{2,1,0:T(8,128)(2,1)}), bf16[8,96,512]{2,1,0:T(8,128)(2,1)S(1)}, u32[]{:S(2)}, u32[]{:S(2)}) async-start(bf16[8,96,512]{2,1,0:T(8,128)(2,1)} %broadcast_in_dim.7), calls=%async_computation.3 | async-start | bytes 1572864 | tf_op jit(solution)/shard_map/all_to_all | solution.py:161
  108.4 3.7 %collective-permute-start.3 = (bf16[768,512]{1,0:T(8,128)(2,1)S(1)}, bf16[768,512]{1,0:T(8,128)(2,1)S(1)}, u32[]{:S(2)}, u32[]{:S(2)}) collective-permute-start(bf16[768,512]{1,0:T(8,128)(2,1)S(1)} %bitcast.23), channel_id=1, source_target_pairs={{0,1},{1,0},{2,3},{3,2},{4,5},{5,4},{6,7},{7,6},{8,9},{9,8},{10,11... | collective-permute-start | bytes 2359304 | tf_op jit(solution)/shard_map/ppermute | solution.py:209
  112.1 1.9 %collective-permute-start.4 = (bf16[384,512]{1,0:T(8,128)(2,1)S(1)}, bf16[384,512]{1,0:T(8,128)(2,1)S(1)}, u32[]{:S(2)}, u32[]{:S(2)}) collective-permute-start(bf16[384,512]{1,0:T(8,128)(2,1)S(1)} %bitcast.26), channel_id=1, source_target_pairs={{0,1},{1,0},{2,3},{3,2},{4,5},{5,4},{6,7},{7,6},{8,9},{9,8},{10,11... | collective-permute-start | bytes 1179656 | tf_op jit(solution)/shard_map/ppermute | solution.py:211
  116.6 3.0 %all-to-all-done.3 = bf16[8,96,512]{2,1,0:T(8,128)(2,1)S(1)} async-done(((bf16[8,96,512]{2,1,0:T(8,128)(2,1)}), bf16[8,96,512]{2,1,0:T(8,128)(2,1)S(1)}, u32[]{:S(2)}, u32[]{:S(2)}) %all-to-all-start.3) | async-done | bytes 786464 | tf_op jit(solution)/shard_map/all_to_all | solution.py:161
  120.8 2.6 %shard_map.75 = bf16[384,512]{1,0:T(8,128)(2,1)S(1)} custom-call(s32[3]{0:T(128)S(1)} %pad_add_fusion.place, bf16[768,512]{1,0:T(8,128)(2,1)S(1)} %bitcast.24, bf16[768,512]{1,0:T(8,128)(2,1)S(1)} %copy-done.3, bf16[768,512]{1,0:T(8,128)(2,1)S(1)} %bitcast.25, bf16[384,512]{1,0:T(8,128)(2,1)S(1)} %bitcast.27, ...), custom_call_target="tpu_custom_call" | custom-call | flops 1207959552 | bytes 4194304 | tf_op jit(solution)/shard_map/pallas_call | solution.py:141
  123.4 9.5 %all_to_all.38 = bf16[8,48,512]{2,1,0:T(8,128)(2,1)S(1)} all-to-all(bf16[8,48,512]{2,1,0:T(8,128)(2,1)S(1)} %bitcast.28), channel_id=1, replica_groups=mesh['z_hi'=2,'y'=8,'x'=4,'z_a'=2,'z_b'=2,'core'=2] {'x','z_b'}, dimensions={0} | all-to-all | bytes 786432 | tf_op jit(solution)/shard_map/all_to_all | solution.py:161
  132.9 6.1 %collective-permute-start.5 = (f32[48,512]{1,0:T(8,128)S(1)}, f32[48,512]{1,0:T(8,128)S(1)}, u32[]{:S(2)}, u32[]{:S(2)}) collective-permute-start(f32[48,512]{1,0:T(8,128)S(1)} %convert_reduce_fusion.3), channel_id=1, source_target_pairs={{0,4},{4,0},{1,5},{5,1},{2,6},{6,2},{3,7},{7,3},{8,12},{12,8},{9,1... | collective-permute-start | bytes 294920 | tf_op jit(solution)/shard_map/ppermute | solution.py:224
  139.0 3.0 %collective-permute-done.5 = f32[48,512]{1,0:T(8,128)S(1)} collective-permute-done((f32[48,512]{1,0:T(8,128)S(1)}, f32[48,512]{1,0:T(8,128)S(1)}, u32[]{:S(2)}, u32[]{:S(2)}) %collective-permute-start.5) | collective-permute-done | bytes 98336 | tf_op jit(solution)/shard_map/ppermute | solution.py:224
  142.1 9.3 %all_to_all.39 = bf16[8,48,512]{2,1,0:T(8,128)(2,1)S(1)} all-to-all(bf16[8,48,512]{2,1,0:T(8,128)(2,1)S(1)} %broadcast_in_dim.8), channel_id=1, replica_groups=mesh['z_hi'=2,'y'=8,'x'=4,'z_a'=2,'z_b'=2,'core'=2] {'x','z_b'}, dimensions={0} | all-to-all | bytes 786432 | tf_op jit(solution)/shard_map/all_to_all | solution.py:161
  151.4 6.1 %collective-permute-start.6 = (bf16[384,512]{1,0:T(8,128)(2,1)S(1)}, bf16[384,512]{1,0:T(8,128)(2,1)S(1)}, u32[]{:S(2)}, u32[]{:S(2)}) collective-permute-start(bf16[384,512]{1,0:T(8,128)(2,1)S(1)} %bitcast.21), channel_id=1, source_target_pairs={{0,1},{1,0},{2,3},{3,2},{4,5},{5,4},{6,7},{7,6},{8,9},{9,8},{10,11... | collective-permute-start | bytes 1179656 | tf_op jit(solution)/shard_map/ppermute | solution.py:227
  158.9 1.9 shard_map.76
  160.8 3.5 %all-to-all-start.6 = ((bf16[8,48,512]{2,1,0:T(8,128)(2,1)}), bf16[8,48,512]{2,1,0:T(8,128)(2,1)S(1)}, u32[]{:S(2)}, u32[]{:S(2)}) async-start(bf16[8,48,512]{2,1,0:T(8,128)(2,1)} %bitcast.15), calls=%async_computation.6 | async-start | bytes 786432 | tf_op jit(solution)/shard_map/all_to_all | solution.py:161
  164.2 15.1 %all-to-all-done.6 = bf16[8,48,512]{2,1,0:T(8,128)(2,1)S(1)} async-done(((bf16[8,48,512]{2,1,0:T(8,128)(2,1)}), bf16[8,48,512]{2,1,0:T(8,128)(2,1)S(1)}, u32[]{:S(2)}, u32[]{:S(2)}) %all-to-all-start.6) | async-done | bytes 393248 | tf_op jit(solution)/shard_map/all_to_all | solution.py:161
  179.4 4.9 %collective-permute-start.7 = (f32[24,512]{1,0:T(8,128)S(1)}, f32[24,512]{1,0:T(8,128)S(1)}, u32[]{:S(2)}, u32[]{:S(2)}) collective-permute-start(f32[24,512]{1,0:T(8,128)S(1)} %dynamic-slice_bitcast_fusion), channel_id=1, source_target_pairs={{0,256},{256,0},{1,257},{257,1},{2,258},{258,2},{3,259},{259,3},{4... | collective-permute-start | bytes 147464 | tf_op jit(solution)/shard_map/ppermute | solution.py:240
  184.3 4.7 %collective-permute-done.7 = f32[24,512]{1,0:T(8,128)S(1)} collective-permute-done((f32[24,512]{1,0:T(8,128)S(1)}, f32[24,512]{1,0:T(8,128)S(1)}, u32[]{:S(2)}, u32[]{:S(2)}) %collective-permute-start.7) | collective-permute-done | bytes 49184 | tf_op jit(solution)/shard_map/ppermute | solution.py:240
  (38 shorter events, 8.8 us)
Async XLA Ops:
  0.0 3.8 %copy-start = (bf16[512,1024]{1,0:T(8,128)(2,1)S(1)}, bf16[512,1024]{1,0:T(8,128)(2,1)}, u32[]{:S(2)}) copy-start(bf16[512,1024]{1,0:T(8,128)(2,1)} %b_out.1) | copy-start | bytes 3145732
  3.8 1.1 copy-start.1
  4.9 10.7 %copy-start.6 = (bf16[768,512]{1,0:T(8,128)(2,1)S(1)}, bf16[768,512]{1,0:T(8,128)(2,1)}, u32[]{:S(2)}) copy-start(bf16[768,512]{1,0:T(8,128)(2,1)} %shard_map.73) | copy-start | bytes 2359300
  6.8 35.0 %collective-permute-start = (f32[768,512]{1,0:T(8,128)S(1)}, f32[768,512]{1,0:T(8,128)S(1)}, u32[]{:S(2)}, u32[]{:S(2)}) collective-permute-start(f32[768,512]{1,0:T(8,128)S(1)} %get-tuple-element.23), channel_id=1, source_target_pairs={{0,1},{1,0},{2,3},{3,2},{4,5},{5,4},{6,7},{7,6},{8,9},{9,8},{10,11... | collective-permute-start | bytes 4718600 | tf_op jit(solution)/shard_map/ppermute | solution.py:197
  58.8 13.8 %collective-permute-start.1 = (bf16[96,512]{1,0:T(8,128)(2,1)S(1)}, bf16[96,512]{1,0:T(8,128)(2,1)S(1)}, u32[]{:S(2)}, u32[]{:S(2)}) collective-permute-start(bf16[96,512]{1,0:T(8,128)(2,1)S(1)} %convert_element_type.39), channel_id=1, source_target_pairs={{0,256},{256,0},{1,257},{257,1},{2,258},{258,2},{3,259},{259,3},{4... | collective-permute-start | bytes 294920 | tf_op jit(solution)/shard_map/ppermute | solution.py:203
  68.5 10.5 %collective-permute-start.2 = (bf16[96,512]{1,0:T(8,128)(2,1)S(1)}, bf16[96,512]{1,0:T(8,128)(2,1)S(1)}, u32[]{:S(2)}, u32[]{:S(2)}) collective-permute-start(bf16[96,512]{1,0:T(8,128)(2,1)S(1)} %convert_element_type.42), channel_id=1, source_target_pairs={{0,4},{4,0},{1,5},{5,1},{2,6},{6,2},{3,7},{7,3},{8,12},{12,8},{9,1... | collective-permute-start | bytes 294920 | tf_op jit(solution)/shard_map/ppermute | solution.py:204
  103.2 8.9 %copy-start.7 = (bf16[384,512]{1,0:T(8,128)(2,1)S(1)}, bf16[384,512]{1,0:T(8,128)(2,1)}, u32[]{:S(2)}) copy-start(bf16[384,512]{1,0:T(8,128)(2,1)} %param.9) | copy-start | bytes 1179652
  103.2 16.4 %copy-start.4 = (f32[16384]{0:T(1024)S(1)}, f32[16384]{0:T(1024)}, u32[]{:S(2)}) copy-start(f32[16384]{0:T(1024)} %param.13) | copy-start | bytes 196612
  103.2 16.4 %copy-start.5 = (f32[16384]{0:T(1024)S(1)}, f32[16384]{0:T(1024)}, u32[]{:S(2)}) copy-start(f32[16384]{0:T(1024)} %param.12) | copy-start | bytes 196612
  104.2 15.5 %all-to-all-start.3 = ((bf16[8,96,512]{2,1,0:T(8,128)(2,1)}), bf16[8,96,512]{2,1,0:T(8,128)(2,1)S(1)}, u32[]{:S(2)}, u32[]{:S(2)}) async-start(bf16[8,96,512]{2,1,0:T(8,128)(2,1)} %broadcast_in_dim.7), calls=%async_computation.3 | async-start | bytes 1572864 | tf_op jit(solution)/shard_map/all_to_all | solution.py:161
  108.4 7.4 %collective-permute-start.3 = (bf16[768,512]{1,0:T(8,128)(2,1)S(1)}, bf16[768,512]{1,0:T(8,128)(2,1)S(1)}, u32[]{:S(2)}, u32[]{:S(2)}) collective-permute-start(bf16[768,512]{1,0:T(8,128)(2,1)S(1)} %bitcast.23), channel_id=1, source_target_pairs={{0,1},{1,0},{2,3},{3,2},{4,5},{5,4},{6,7},{7,6},{8,9},{9,8},{10,11... | collective-permute-start | bytes 2359304 | tf_op jit(solution)/shard_map/ppermute | solution.py:209
  112.1 3.6 %collective-permute-start.4 = (bf16[384,512]{1,0:T(8,128)(2,1)S(1)}, bf16[384,512]{1,0:T(8,128)(2,1)S(1)}, u32[]{:S(2)}, u32[]{:S(2)}) collective-permute-start(bf16[384,512]{1,0:T(8,128)(2,1)S(1)} %bitcast.26), channel_id=1, source_target_pairs={{0,1},{1,0},{2,3},{3,2},{4,5},{5,4},{6,7},{7,6},{8,9},{9,8},{10,11... | collective-permute-start | bytes 1179656 | tf_op jit(solution)/shard_map/ppermute | solution.py:211
  115.7 0.9 copy-start.2
  119.6 1.1 copy-start.3
  132.9 9.1 %collective-permute-start.5 = (f32[48,512]{1,0:T(8,128)S(1)}, f32[48,512]{1,0:T(8,128)S(1)}, u32[]{:S(2)}, u32[]{:S(2)}) collective-permute-start(f32[48,512]{1,0:T(8,128)S(1)} %convert_reduce_fusion.3), channel_id=1, source_target_pairs={{0,4},{4,0},{1,5},{5,1},{2,6},{6,2},{3,7},{7,3},{8,12},{12,8},{9,1... | collective-permute-start | bytes 294920 | tf_op jit(solution)/shard_map/ppermute | solution.py:224
  151.4 7.5 %collective-permute-start.6 = (bf16[384,512]{1,0:T(8,128)(2,1)S(1)}, bf16[384,512]{1,0:T(8,128)(2,1)S(1)}, u32[]{:S(2)}, u32[]{:S(2)}) collective-permute-start(bf16[384,512]{1,0:T(8,128)(2,1)S(1)} %bitcast.21), channel_id=1, source_target_pairs={{0,1},{1,0},{2,3},{3,2},{4,5},{5,4},{6,7},{7,6},{8,9},{9,8},{10,11... | collective-permute-start | bytes 1179656 | tf_op jit(solution)/shard_map/ppermute | solution.py:227
  160.8 18.5 %all-to-all-start.6 = ((bf16[8,48,512]{2,1,0:T(8,128)(2,1)}), bf16[8,48,512]{2,1,0:T(8,128)(2,1)S(1)}, u32[]{:S(2)}, u32[]{:S(2)}) async-start(bf16[8,48,512]{2,1,0:T(8,128)(2,1)} %bitcast.15), calls=%async_computation.6 | async-start | bytes 786432 | tf_op jit(solution)/shard_map/all_to_all | solution.py:161
  179.4 9.6 %collective-permute-start.7 = (f32[24,512]{1,0:T(8,128)S(1)}, f32[24,512]{1,0:T(8,128)S(1)}, u32[]{:S(2)}, u32[]{:S(2)}) collective-permute-start(f32[24,512]{1,0:T(8,128)S(1)} %dynamic-slice_bitcast_fusion), channel_id=1, source_target_pairs={{0,256},{256,0},{1,257},{257,1},{2,258},{258,2},{3,259},{259,3},{4... | collective-permute-start | bytes 147464 | tf_op jit(solution)/shard_map/ppermute | solution.py:240

commit v7 on v5

--- a/solution.py
+++ b/solution.py
@@ -28,18 +28,22 @@
 ANY = pl.BlockSpec(memory_space=pl.ANY)
 
 
+def device_ids():
+    return np.arange(np.prod(SIZES)).reshape(2, 8, 2, 2, 4, 2)
+
+
 def mixed_groups():
-    ids = np.arange(np.prod(SIZES)).reshape(SIZES)
+    ids = device_ids()
     along_row = ids[..., 0].transpose(0, 2, 3, 4, 1).reshape(-1, 8).tolist()
-    along_col = ids[..., 1].transpose(0, 1, 3, 2, 4).reshape(-1, 8).tolist()
+    along_col = ids[..., 1].reshape(-1, 8).tolist()
     return along_row + along_col
 
 
 def mixed_pairs():
-    ids = np.arange(np.prod(SIZES)).reshape(SIZES)
+    ids = device_ids()
     to = np.empty_like(ids)
     to[..., 0] = ids[::-1, ..., 0]
-    to[..., 1] = ids[:, :, :, ::-1, :, 1]
+    to[..., 1] = ids[:, :, ::-1, :, :, 1]
     return list(zip(ids.reshape(-1).tolist(), to.reshape(-1).tolist()))
 
 
@@ -58,13 +62,11 @@
 TILE = 256
 
 
-def damp_kernel(e_in, e_out, damp):
-    damp[0] = (
-        damping_share * (jnp.sum(e_in[...]) / e_in.size) * (jnp.sum(e_out[...]) / e_out.size)
-    )
-
-
-def rotate_kernel(place, act, grad, b_in, b_out, b_in_o, grad_o, b_out_o, out):
+def first_kernel(core, token):
+    token[0] = core[0]
+
+
+def rotate_kernel(core, act, grad, b_in, b_out, b_in_o, grad_o, b_out_o, out):
     half = grad.shape[1]
 
     def body(product):
@@ -81,18 +83,19 @@
             bf16
         )
 
-    @pl.when(place[0] == 0)
+    @pl.when(core[0] == 0)
     def _():
         body(joined)
 
-    @pl.when(place[0] == 1)
+    @pl.when(core[0] == 1)
     def _():
         body(added)
 
 
-def outer_kernel(queries, place, damp, own, other, train, train_o, e_out, e_in, out):
+def outer_kernel(queries, place, token, own, other, train, train_o, e_out, e_in, out):
     half = train.shape[1]
     lanes = e_in.shape[1]
+    damp = damping_share * (jnp.sum(e_in[...]) / e_in.size) * (jnp.sum(e_out[...]) / e_out.size)
     e_rows = e_in[pl.ds(pl.multiple_of(place[1] * 8, 8), 8), :]
     e_row = jnp.concatenate([e_rows[r : r + 1, :] for r in range(8)], axis=1)
     e_cols = jnp.transpose(e_out[pl.ds(pl.multiple_of(place[2] * 8, 8), 8), :])
@@ -102,7 +105,7 @@
             outer = dot_tn(grad[:, first + start : first + start + TILE], act[...])
             r = (first + start) // lanes
             e_col = jnp.concatenate([e_cols[:, r + q : r + q + 1] for q in range(TILE // lanes)], axis=0)
-            scaled = (outer / queries / (e_col * e_row + damp[0])).astype(bf16)
+            scaled = (outer / queries / (e_col * e_row + damp)).astype(bf16)
             out[:, start : start + TILE] = (
                 dot_nt(left[...], scaled[:, :half]) + dot_nt(right[...], scaled[:, half:])
             ).astype(bf16)
@@ -116,7 +119,7 @@
         body(other, own, half, train_o, train)
 
 
-def back_kernel(place, own, other, b_out, out):
+def back_kernel(core, own, other, b_out, out):
     half = own.shape[1]
 
     def body(left, right):
@@ -124,11 +127,11 @@
             dot_nt(left[...], b_out[:, :half]) + dot_nt(right[...], b_out[:, half:])
         ).astype(bf16)
 
-    @pl.when(place[0] == 0)
+    @pl.when(core[0] == 0)
     def _():
         body(own, other)
 
-    @pl.when(place[0] == 1)
+    @pl.when(core[0] == 1)
     def _():
         body(other, own)
 
@@ -171,23 +174,24 @@
     place = jnp.stack(
         [lax.axis_index("core"), lax.axis_index(CHIPS), lax.axis_index(ROW)]
     ).astype(jnp.int32)
+    core = lax.axis_index("core").astype(jnp.int32).reshape(1)
     e_in, e_out = (e.reshape(-1, 128) for e in (eig_in, eig_out))
 
     basis_in_o = lax.ppermute(basis_in, "core", [(1, 0)])
     basis_out_o = lax.ppermute(basis_out, "core", [(0, 1)])
     grad_o = lax.ppermute(query_grad, "core", [(0, 1)])
 
-    damp = call(
-        damp_kernel,
-        (e_in, e_out),
-        [VMEM] * 2,
-        shape((1,), f32),
+    token = call(
+        first_kernel,
+        (core,),
+        [SMEM],
+        shape((1,), jnp.int32),
         SMEM,
         6 * 10**9,
         8,
     )
-    basis_in_o, basis_out_o, grad_o, damp = lax.optimization_barrier(
-        (basis_in_o, basis_out_o, grad_o, damp)
+    basis_in_o, basis_out_o, grad_o, token = lax.optimization_barrier(
+        (basis_in_o, basis_out_o, grad_o, token)
     )
     part = call(
         rotate_kernel,
@@ -209,7 +213,7 @@
 
     partial_inner = call(
         functools.partial(outer_kernel, queries),
-        (place, damp, own, other, train_rot, train_o, e_out, e_in),
+        (place, token, own, other, train_rot, train_o, e_out, e_in),
         [SMEM] * 2 + [VMEM] * 6,
         shape((train, half), bf16),
         VMEM,
@@ -223,7 +227,7 @@
     inner_o = lax.ppermute(inner, "core", SWAP)
     partial_out = call(
         back_kernel,
-        (place, inner, inner_o, basis_out),
+        (core, inner, inner_o, basis_out),
         [SMEM] + [VMEM] * 3,
         shape((train, half), bf16),
         VMEM,

time: 160 us -> 158 us (0.988)
  starting transfers between devices: 57.8 us -> 39.6 us
  blocking collectives: 78.4 us -> 95.6 us
  local copies, waits for them, and re-layouts: 2.62 us -> 0.24 us
  waiting for transfers between devices: 10.7 us -> 12.5 us
    ppermute x1, starting transfers between devices: 20.9 us -> 11.1 us  [per_device(): train_o = lax.ppermute(train_rot, 'core', SWAP)]
    all_to_all x1, blocking collectives: 18 us -> 26.5 us  [per_device(): own = mixed(spread(rot, 8)).reshape(queries, width)]
    ppermute x1, starting transfers between devices: 13 us -> 4.58 us  [per_device(): other = lax.ppermute(own, 'core', SWAP)]
    all_to_all x1, blocking collectives: 15.9 us -> 23.7 us  [per_device(): eighth = summed(mixed(part.reshape(8, -1, width)))]
    unnamed x18 -> x14, local copies, waits for them, and re-layouts: 2.41 us -> 0.03 us
    ppermute x1, waiting for transfers between devices: 0.85 us -> 2.66 us  [per_device(): grad_o = lax.ppermute(query_grad, 'core', [(0, 1)])]
where the time goes in v7:
time: 158 us; the launch traced here: 157 us
  blocking collectives  95.6 us (61%)
  starting transfers between devices  39.6 us (25%)
  waiting for transfers between devices  12.5 us (8%)
  Pallas kernels  7.2 us (5%)
    all_to_all x1, blocking collectives, per_device(): own = mixed(spread(rot, 8)).reshape(queries, width)  26.5 us
    all_to_all x1, blocking collectives, per_device(): eighth = summed(mixed(part.reshape(8, -1, width)))  23.7 us
    all_to_all x1, blocking collectives, per_device(): lax.all_to_all(partial_out.reshape(16, -1, half), ROW, 0, 0, tiled=True)  22 us
    all_to_all x1, blocking collectives, per_device(): inner_sum = summed(near(partial_inner.reshape(8, -1, half)))  13.2 us
    ppermute x1, starting transfers between devices, per_device(): train_o = lax.ppermute(train_rot, 'core', SWAP)  11.1 us
    all_to_all x1, blocking collectives, per_device(): near(spread((inner_sum * factor).astype(bf16), 8)).reshape(train, half)  10.3 us
    ppermute x1, starting transfers between devices, per_device(): basis_in_o = lax.ppermute(basis_in, 'core', [(1, 0)])  8.84 us
    pallas_call x4, Pallas kernels, call(): pl.pallas_call(kernel, out_shape=shapes, in_specs=specs, out_specs=out_sp...  7.2 us
  transfers between devices with their start and end apart: 8, of which 5 were waited for; matrix products, arithmetic and copies ran while one was open for 0% of the time, Pallas kernels for 0%

profile of v7, /device:TPU:1, one launch (start us, length us, event | category | flops | bytes accessed | tf_op | source)
XLA Modules:
  0.0 156.6 jit_solution(12405857481237890624)
XLA Ops:
  0.0 8.8 %collective-permute-start = (bf16[1024,512]{1,0:T(8,128)(2,1)}, bf16[1024,512]{1,0:T(8,128)(2,1)S(1)}, u32[]{:S(2)}, u32[]{:S(2)}) collective-permute-start(bf16[1024,512]{1,0:T(8,128)(2,1)} %b_in.1), channel_id=1, source_target_pairs={{1,0},{3,2},{5,4},{7,6},{9,8},{11,10},{13,12},{15,14},{17,16},{19,... | collective-permute-start | bytes 3145736 | tf_op jit(solution)/shard_map/ppermute | solution.py:180
  8.8 1.3 collective-permute-start.1
  10.1 1.3 collective-permute-start.2
  11.6 0.5 shard_map.73.token
  12.1 2.7 %collective-permute-done.2.grad_o = bf16[768,512]{1,0:T(8,128)(2,1)S(1)} collective-permute-done((bf16[768,512]{1,0:T(8,128)(2,1)}, bf16[768,512]{1,0:T(8,128)(2,1)S(1)}, u32[]{:S(2)}, u32[]{:S(2)}) %collective-permute-start.2) | collective-permute-done | bytes 786464 | tf_op jit(solution)/shard_map/ppermute | solution.py:182
  14.8 2.7 %shard_map.74 = bf16[768,1024]{1,0:T(8,128)(2,1)S(1)} custom-call(s32[3]{0:T(128)S(1)} %pad_add_fusion.core.place, bf16[768,1024]{1,0:T(8,128)(2,1)S(1)} %copy-done.1, bf16[768,512]{1,0:T(8,128)(2,1)S(1)} %copy-done.3, bf16[1024,512]{1,0:T(8,128)(2,1)S(1)} %copy-done.2, bf16[512,1024]{1,0:T(8,128)(2,1)S(1)} %copy-done, ...), custom_call_target="tpu_custom_call" | custom-call | flops 1610612736 | bytes 4194304 | tf_op jit(solution)/shard_map/pallas_call | solution.py:140
  17.5 23.7 %all_to_all.25 = bf16[8,96,1024]{2,1,0:T(8,128)(2,1)S(1)} all-to-all(bf16[8,96,1024]{2,1,0:T(8,128)(2,1)S(1)} %bitcast.10), channel_id=1, replica_groups={{0,32,64,96,128,160,192,224},{2,34,66,98,130,162,194,226},{4,36,68,100,..., dimensions={0} | all-to-all | bytes 3145728 | tf_op jit(solution)/shard_map/all_to_all | solution.py:205
  41.2 0.3 convert_reduce_fusion
  41.5 4.3 %collective-permute-start.3 = (bf16[96,1024]{1,0:T(8,128)(2,1)S(1)}, bf16[96,1024]{1,0:T(8,128)(2,1)S(1)}, u32[]{:S(2)}, u32[]{:S(2)}) collective-permute-start(bf16[96,1024]{1,0:T(8,128)(2,1)S(1)} %convert_element_type.22), channel_id=1, source_target_pairs={{0,256},{1,17},{2,258},{3,19},{4,260},{5,21},{6,262},{7,23},{8,264... | collective-permute-start | bytes 589832 | tf_op jit(solution)/shard_map/ppermute | solution.py:207
  45.8 11.1 %collective-permute-start.4 = (bf16[384,512]{1,0:T(8,128)(2,1)S(1)}, bf16[384,512]{1,0:T(8,128)(2,1)S(1)}, u32[]{:S(2)}, u32[]{:S(2)}) collective-permute-start(bf16[384,512]{1,0:T(8,128)(2,1)S(1)} %copy-done.4), channel_id=1, source_target_pairs={{0,1},{1,0},{2,3},{3,2},{4,5},{5,4},{6,7},{7,6},{8,9},{9,8},{10,11... | collective-permute-start | bytes 1179656 | tf_op jit(solution)/shard_map/ppermute | solution.py:208
  57.0 1.3 collective-permute-done.4.train_o
  58.5 26.5 %all_to_all.26 = bf16[8,96,1024]{2,1,0:T(8,128)(2,1)S(1)} all-to-all(bf16[8,96,1024]{2,1,0:T(8,128)(2,1)S(1)} %broadcast_in_dim.4), channel_id=1, replica_groups={{0,32,64,96,128,160,192,224},{2,34,66,98,130,162,194,226},{4,36,68,100,..., dimensions={0} | all-to-all | bytes 3145728 | tf_op jit(solution)/shard_map/all_to_all | solution.py:211
  85.0 4.6 %collective-permute-start.5 = (bf16[768,1024]{1,0:T(8,128)(2,1)S(1)}, bf16[768,1024]{1,0:T(8,128)(2,1)S(1)}, u32[]{:S(2)}, u32[]{:S(2)}) collective-permute-start(bf16[768,1024]{1,0:T(8,128)(2,1)S(1)} %bitcast.11), channel_id=1, source_target_pairs={{0,1},{1,0},{2,3},{3,2},{4,5},{5,4},{6,7},{7,6},{8,9},{9,8},{10,11... | collective-permute-start | bytes 4718600 | tf_op jit(solution)/shard_map/ppermute | solution.py:212
  89.5 3.0 %collective-permute-done.5.other = bf16[768,1024]{1,0:T(8,128)(2,1)S(1)} collective-permute-done((bf16[768,1024]{1,0:T(8,128)(2,1)S(1)}, bf16[768,1024]{1,0:T(8,128)(2,1)S(1)}, u32[]{:S(2)}, u32[]{:S(2)}) %collective-permute-start.5) | collective-permute-done | bytes 1572896 | tf_op jit(solution)/shard_map/ppermute | solution.py:212
  92.6 3.4 %shard_map.75 = bf16[384,512]{1,0:T(8,128)(2,1)S(1)} custom-call(s32[3]{0:T(128)S(1)} %pad_add_fusion.core.place, s32[1]{0:T(128)} %shard_map.73.token, bf16[768,1024]{1,0:T(8,128)(2,1)S(1)} %bitcast.12, bf16[768,1024]{1,0:T(8,128)(2,1)S(1)} %collective-permute-done.5.other, bf16[384,512]{1,0:T(8,128)(2,1)S(1)} %copy-done.4, ...), custom_call_target="tpu_custom_call" | custom-call | flops 1207959552 | bytes 4194304 | tf_op jit(solution)/shard_map/pallas_call | solution.py:140
  96.0 13.2 %all_to_all.27 = bf16[8,48,512]{2,1,0:T(8,128)(2,1)S(1)} all-to-all(bf16[8,48,512]{2,1,0:T(8,128)(2,1)S(1)} %bitcast.16), channel_id=1, replica_groups=mesh['z_hi'=2,'y'=8,'x'=4,'z_a'=2,'z_b'=2,'core'=2] {'x','z_b'}, dimensions={0} | all-to-all | bytes 786432 | tf_op jit(solution)/shard_map/all_to_all | solution.py:223
  109.2 3.0 %collective-permute-start.6 = (f32[48,512]{1,0:T(8,128)S(1)}, f32[48,512]{1,0:T(8,128)S(1)}, u32[]{:S(2)}, u32[]{:S(2)}) collective-permute-start(f32[48,512]{1,0:T(8,128)S(1)} %convert_reduce_fusion.2), channel_id=1, source_target_pairs={{0,4},{4,0},{1,5},{5,1},{2,6},{6,2},{3,7},{7,3},{8,12},{12,8},{9,1... | collective-permute-start | bytes 294920 | tf_op jit(solution)/shard_map/ppermute | solution.py:224
  112.3 4.3 %collective-permute-done.6 = f32[48,512]{1,0:T(8,128)S(1)} collective-permute-done((f32[48,512]{1,0:T(8,128)S(1)}, f32[48,512]{1,0:T(8,128)S(1)}, u32[]{:S(2)}, u32[]{:S(2)}) %collective-permute-start.6) | collective-permute-done | bytes 98336 | tf_op jit(solution)/shard_map/ppermute | solution.py:224
  116.6 10.3 %all_to_all.28 = bf16[8,48,512]{2,1,0:T(8,128)(2,1)S(1)} all-to-all(bf16[8,48,512]{2,1,0:T(8,128)(2,1)S(1)} %broadcast_in_dim.5), channel_id=1, replica_groups=mesh['z_hi'=2,'y'=8,'x'=4,'z_a'=2,'z_b'=2,'core'=2] {'x','z_b'}, dimensions={0} | all-to-all | bytes 786432 | tf_op jit(solution)/shard_map/all_to_all | solution.py:226
  126.8 5.2 %collective-permute-start.7 = (bf16[384,512]{1,0:T(8,128)(2,1)S(1)}, bf16[384,512]{1,0:T(8,128)(2,1)S(1)}, u32[]{:S(2)}, u32[]{:S(2)}) collective-permute-start(bf16[384,512]{1,0:T(8,128)(2,1)S(1)} %bitcast.13), channel_id=1, source_target_pairs={{0,1},{1,0},{2,3},{3,2},{4,5},{5,4},{6,7},{7,6},{8,9},{9,8},{10,11... | collective-permute-start | bytes 1179656 | tf_op jit(solution)/shard_map/ppermute | solution.py:227
  132.0 1.3 collective-permute-done.7.other
  133.4 0.6 shard_map.76
  134.0 22.0 %all_to_all.29 = bf16[16,24,512]{2,1,0:T(8,128)(2,1)S(1)} all-to-all(bf16[16,24,512]{2,1,0:T(8,128)(2,1)S(1)} %bitcast.15), channel_id=1, replica_groups=mesh['z_hi'=2,'y'=8,'x'=4,'z_a'=2,'z_b'=2,'core'=2] {'z_hi','y'}, dimensions={0} | all-to-all | bytes 786432 | tf_op jit(solution)/shard_map/all_to_all | solution.py:237
  155.9 0.7 convert_reduce_fusion.1
  (24 shorter events, 0.5 us)
Async XLA Ops:
  0.0 14.7 %collective-permute-start = (bf16[1024,512]{1,0:T(8,128)(2,1)}, bf16[1024,512]{1,0:T(8,128)(2,1)S(1)}, u32[]{:S(2)}, u32[]{:S(2)}) collective-permute-start(bf16[1024,512]{1,0:T(8,128)(2,1)} %b_in.1), channel_id=1, source_target_pairs={{1,0},{3,2},{5,4},{7,6},{9,8},{11,10},{13,12},{15,14},{17,16},{19,... | collective-permute-start | bytes 3145736 | tf_op jit(solution)/shard_map/ppermute | solution.py:180
  8.8 5.9 %collective-permute-start.1 = (bf16[512,1024]{1,0:T(8,128)(2,1)}, bf16[512,1024]{1,0:T(8,128)(2,1)S(1)}, u32[]{:S(2)}, u32[]{:S(2)}) collective-permute-start(bf16[512,1024]{1,0:T(8,128)(2,1)} %b_out.3), channel_id=1, source_target_pairs={{0,1},{2,3},{4,5},{6,7},{8,9},{10,11},{12,13},{14,15},{16,17},{18,... | collective-permute-start | bytes 3145736 | tf_op jit(solution)/shard_map/ppermute | solution.py:181
  10.1 4.6 %collective-permute-start.2 = (bf16[768,512]{1,0:T(8,128)(2,1)}, bf16[768,512]{1,0:T(8,128)(2,1)S(1)}, u32[]{:S(2)}, u32[]{:S(2)}) collective-permute-start(bf16[768,512]{1,0:T(8,128)(2,1)} %grad.1), channel_id=1, source_target_pairs={{0,1},{2,3},{4,5},{6,7},{8,9},{10,11},{12,13},{14,15},{16,17},{18,... | collective-permute-start | bytes 2359304 | tf_op jit(solution)/shard_map/ppermute | solution.py:182
  11.5 3.2 %copy-start = (bf16[512,1024]{1,0:T(8,128)(2,1)S(1)}, bf16[512,1024]{1,0:T(8,128)(2,1)}, u32[]{:S(2)}) copy-start(bf16[512,1024]{1,0:T(8,128)(2,1)} %b_out.3) | copy-start | bytes 3145732
  11.5 3.2 %copy-start.1 = (bf16[768,1024]{1,0:T(8,128)(2,1)S(1)}, bf16[768,1024]{1,0:T(8,128)(2,1)}, u32[]{:S(2)}) copy-start(bf16[768,1024]{1,0:T(8,128)(2,1)} %act.1) | copy-start | bytes 4718596
  11.5 3.2 %copy-start.2 = (bf16[1024,512]{1,0:T(8,128)(2,1)S(1)}, bf16[1024,512]{1,0:T(8,128)(2,1)}, u32[]{:S(2)}) copy-start(bf16[1024,512]{1,0:T(8,128)(2,1)} %b_in.1) | copy-start | bytes 3145732
  11.5 3.2 %copy-start.3 = (bf16[768,512]{1,0:T(8,128)(2,1)S(1)}, bf16[768,512]{1,0:T(8,128)(2,1)}, u32[]{:S(2)}) copy-start(bf16[768,512]{1,0:T(8,128)(2,1)} %grad.1) | copy-start | bytes 2359300
  41.2 4.6 %copy-start.4 = (bf16[384,512]{1,0:T(8,128)(2,1)S(1)}, bf16[384,512]{1,0:T(8,128)(2,1)}, u32[]{:S(2)}) copy-start(bf16[384,512]{1,0:T(8,128)(2,1)} %train) | copy-start | bytes 1179652
  41.5 15.4 %collective-permute-start.3 = (bf16[96,1024]{1,0:T(8,128)(2,1)S(1)}, bf16[96,1024]{1,0:T(8,128)(2,1)S(1)}, u32[]{:S(2)}, u32[]{:S(2)}) collective-permute-start(bf16[96,1024]{1,0:T(8,128)(2,1)S(1)} %convert_element_type.22), channel_id=1, source_target_pairs={{0,256},{1,17},{2,258},{3,19},{4,260},{5,21},{6,262},{7,23},{8,264... | collective-permute-start | bytes 589832 | tf_op jit(solution)/shard_map/ppermute | solution.py:207
  45.8 12.5 %collective-permute-start.4 = (bf16[384,512]{1,0:T(8,128)(2,1)S(1)}, bf16[384,512]{1,0:T(8,128)(2,1)S(1)}, u32[]{:S(2)}, u32[]{:S(2)}) collective-permute-start(bf16[384,512]{1,0:T(8,128)(2,1)S(1)} %copy-done.4), channel_id=1, source_target_pairs={{0,1},{1,0},{2,3},{3,2},{4,5},{5,4},{6,7},{7,6},{8,9},{9,8},{10,11... | collective-permute-start | bytes 1179656 | tf_op jit(solution)/shard_map/ppermute | solution.py:208
  58.5 34.1 %copy-start.5 = (f32[16384]{0:T(1024)S(1)}, f32[16384]{0:T(1024)}, u32[]{:S(2)}) copy-start(f32[16384]{0:T(1024)} %param.13) | copy-start | bytes 196612
  58.5 34.1 %copy-start.6 = (f32[16384]{0:T(1024)S(1)}, f32[16384]{0:T(1024)}, u32[]{:S(2)}) copy-start(f32[16384]{0:T(1024)} %param.12) | copy-start | bytes 196612
  85.0 7.6 %collective-permute-start.5 = (bf16[768,1024]{1,0:T(8,128)(2,1)S(1)}, bf16[768,1024]{1,0:T(8,128)(2,1)S(1)}, u32[]{:S(2)}, u32[]{:S(2)}) collective-permute-start(bf16[768,1024]{1,0:T(8,128)(2,1)S(1)} %bitcast.11), channel_id=1, source_target_pairs={{0,1},{1,0},{2,3},{3,2},{4,5},{5,4},{6,7},{7,6},{8,9},{9,8},{10,11... | collective-permute-start | bytes 4718600 | tf_op jit(solution)/shard_map/ppermute | solution.py:212
  109.2 7.3 %collective-permute-start.6 = (f32[48,512]{1,0:T(8,128)S(1)}, f32[48,512]{1,0:T(8,128)S(1)}, u32[]{:S(2)}, u32[]{:S(2)}) collective-permute-start(f32[48,512]{1,0:T(8,128)S(1)} %convert_reduce_fusion.2), channel_id=1, source_target_pairs={{0,4},{4,0},{1,5},{5,1},{2,6},{6,2},{3,7},{7,3},{8,12},{12,8},{9,1... | collective-permute-start | bytes 294920 | tf_op jit(solution)/shard_map/ppermute | solution.py:224
  126.8 6.5 %collective-permute-start.7 = (bf16[384,512]{1,0:T(8,128)(2,1)S(1)}, bf16[384,512]{1,0:T(8,128)(2,1)S(1)}, u32[]{:S(2)}, u32[]{:S(2)}) collective-permute-start(bf16[384,512]{1,0:T(8,128)(2,1)S(1)} %bitcast.13), channel_id=1, source_target_pairs={{0,1},{1,0},{2,3},{3,2},{4,5},{5,4},{6,7},{7,6},{8,9},{9,8},{10,11... | collective-permute-start | bytes 1179656 | tf_op jit(solution)/shard_map/ppermute | solution.py:227

commit v8 on v7

--- a/solution.py
+++ b/solution.py
@@ -28,23 +28,40 @@
 ANY = pl.BlockSpec(memory_space=pl.ANY)
 
 
-def device_ids():
-    return np.arange(np.prod(SIZES)).reshape(2, 8, 2, 2, 4, 2)
+def parity():
+    z_hi, y, x, _, z_b = np.indices(SIZES[:-1])
+    return (z_hi + y + x + z_b) % 2
+
+
+def role_ids():
+    ids = np.arange(np.prod(SIZES)).reshape(SIZES)
+    first = parity()[..., None]
+    return np.take_along_axis(ids, np.concatenate([first, 1 - first], axis=-1), axis=-1)
 
 
 def mixed_groups():
-    ids = device_ids()
+    ids = role_ids()
     along_row = ids[..., 0].transpose(0, 2, 3, 4, 1).reshape(-1, 8).tolist()
-    along_col = ids[..., 1].reshape(-1, 8).tolist()
+    along_col = ids[..., 1].transpose(0, 1, 3, 2, 4).reshape(-1, 8).tolist()
     return along_row + along_col
 
 
 def mixed_pairs():
-    ids = device_ids()
+    ids = role_ids()
     to = np.empty_like(ids)
     to[..., 0] = ids[::-1, ..., 0]
-    to[..., 1] = ids[:, :, ::-1, :, :, 1]
+    to[..., 1] = ids[:, :, :, ::-1, :, 1]
     return list(zip(ids.reshape(-1).tolist(), to.reshape(-1).tolist()))
+
+
+def final_groups():
+    ids = np.arange(np.prod(SIZES)).reshape(2, 2, 2, 2, -1)
+    return ids.transpose(3, 2, 1, 0, 4).reshape(16, -1).T.tolist()
+
+
+def role_pairs(source):
+    ids = role_ids().reshape(-1, 2)
+    return list(zip(ids[:, source].tolist(), ids[:, 1 - source].tolist()))
 
 
 def dot(a, b):
@@ -59,37 +76,28 @@
     return lax.dot_general(a, b, (((0,), (0,)), ((), ())), preferred_element_type=f32)
 
 
-TILE = 256
-
-
 def first_kernel(core, token):
     token[0] = core[0]
 
 
-def rotate_kernel(core, act, grad, b_in, b_out, b_in_o, grad_o, b_out_o, out):
+def rotate_kernel(place, act, grad, b_in, b_out, b_in_o, grad_o, b_out_o, out):
     half = grad.shape[1]
 
-    def body(product):
-        @pl.loop(0, out.shape[0] // TILE)
-        def _(m):
-            product(pl.ds(pl.multiple_of(m * TILE, TILE), TILE))
-
-    def joined(rows):
-        out[rows, :half] = dot(act[rows, :], b_in[...]).astype(bf16)
-        out[rows, half:] = dot(act[rows, :], b_in_o[...]).astype(bf16)
-
-    def added(rows):
-        out[rows, :] = (dot(grad_o[rows, :], b_out_o[...]) + dot(grad[rows, :], b_out[...])).astype(
-            bf16
-        )
-
-    @pl.when(core[0] == 0)
-    def _():
-        body(joined)
-
-    @pl.when(core[0] == 1)
-    def _():
-        body(added)
+    def joined(low, high):
+        out[:, :half] = dot(act[...], low[...]).astype(bf16)
+        out[:, half:] = dot(act[...], high[...]).astype(bf16)
+
+    @pl.when((place[3] == 0) & (place[0] == 0))
+    def _():
+        joined(b_in, b_in_o)
+
+    @pl.when((place[3] == 0) & (place[0] == 1))
+    def _():
+        joined(b_in_o, b_in)
+
+    @pl.when(place[3] == 1)
+    def _():
+        out[...] = (dot(grad_o[...], b_out_o[...]) + dot(grad[...], b_out[...])).astype(bf16)
 
 
 def outer_kernel(queries, place, token, own, other, train, train_o, e_out, e_in, out):
@@ -101,22 +109,20 @@
     e_cols = jnp.transpose(e_out[pl.ds(pl.multiple_of(place[2] * 8, 8), 8), :])
 
     def body(act, grad, first, left, right):
-        for start in range(0, half, TILE):
-            outer = dot_tn(grad[:, first + start : first + start + TILE], act[...])
-            r = (first + start) // lanes
-            e_col = jnp.concatenate([e_cols[:, r + q : r + q + 1] for q in range(TILE // lanes)], axis=0)
-            scaled = (outer / queries / (e_col * e_row + damp)).astype(bf16)
-            out[:, start : start + TILE] = (
-                dot_nt(left[...], scaled[:, :half]) + dot_nt(right[...], scaled[:, half:])
-            ).astype(bf16)
-
-    @pl.when(place[0] == 0)
-    def _():
-        body(own, other, 0, train, train_o)
-
-    @pl.when(place[0] == 1)
-    def _():
-        body(other, own, half, train_o, train)
+        outer = dot_tn(grad[:, first : first + half], act[...])
+        r = first // lanes
+        e_col = jnp.concatenate([e_cols[:, r + q : r + q + 1] for q in range(half // lanes)], axis=0)
+        scaled = (outer / ((e_col * queries) * e_row + damp * queries)).astype(bf16)
+        out[...] = (
+            dot_nt(left[...], scaled[:, :half]) + dot_nt(right[...], scaled[:, half:])
+        ).astype(bf16)
+
+    for role, (act, grad) in enumerate(((own, other), (other, own))):
+        for core, (left, right) in enumerate(((train, train_o), (train_o, train))):
+
+            @pl.when((place[3] == role) & (place[0] == core))
+            def _():
+                body(act, grad, core * half, left, right)
 
 
 def back_kernel(core, own, other, b_out, out):
@@ -171,15 +177,16 @@
         lax.all_to_all, axis_name=NEAR, split_axis=0, concat_axis=0, tiled=True
     )
     shape = jax.ShapeDtypeStruct
+    spots = [lax.axis_index(axis) for axis in ("z_hi", "y", "x", "z_b", "core")]
     place = jnp.stack(
-        [lax.axis_index("core"), lax.axis_index(CHIPS), lax.axis_index(ROW)]
+        [spots[-1], lax.axis_index(CHIPS), lax.axis_index(ROW), sum(spots) % 2]
     ).astype(jnp.int32)
     core = lax.axis_index("core").astype(jnp.int32).reshape(1)
     e_in, e_out = (e.reshape(-1, 128) for e in (eig_in, eig_out))
 
-    basis_in_o = lax.ppermute(basis_in, "core", [(1, 0)])
-    basis_out_o = lax.ppermute(basis_out, "core", [(0, 1)])
-    grad_o = lax.ppermute(query_grad, "core", [(0, 1)])
+    basis_in_o = lax.ppermute(basis_in, ALL, role_pairs(1))
+    basis_out_o = lax.ppermute(basis_out, ALL, role_pairs(0))
+    grad_o = lax.ppermute(query_grad, ALL, role_pairs(0))
 
     token = call(
         first_kernel,
@@ -205,6 +212,8 @@
     eighth = summed(mixed(part.reshape(8, -1, width)))
     eighth, train_rot = lax.optimization_barrier((eighth, train_rot))
     far = lax.ppermute(eighth.astype(bf16), ALL, mixed_pairs()).astype(f32)
+    train_rot = train_rot.reshape(2, 2, 2, 2, -1, half).transpose(3, 2, 1, 0, 4, 5)
+    train_rot = train_rot.reshape(train, half)
     train_o = lax.ppermute(train_rot, "core", SWAP)
     rot = (eighth + far).astype(bf16)
     rot, train_o = lax.optimization_barrier((rot, train_o))
@@ -234,7 +243,10 @@
         2 * train * half * width,
         32,
     )
-    return summed(lax.all_to_all(partial_out.reshape(16, -1, half), ROW, 0, 0, tiled=True))
+    final = lax.all_to_all(
+        partial_out.reshape(16, -1, half), ALL, 0, 0, axis_index_groups=final_groups(), tiled=True
+    )
+    return summed(final)
 
 
 def solution(mesh):

time: 158 us -> 158 us (level)
  starting transfers between devices: 39.6 us -> 50.1 us
  blocking collectives: 95.6 us -> 85.2 us
  waiting for transfers between devices: 12.5 us -> 14.3 us
    all_to_all x1, blocking collectives: 23.7 us -> 16 us  [per_device(): eighth = summed(mixed(part.reshape(8, -1, width)))]
    all_to_all x1, blocking collectives: 26.5 us -> 19.7 us  [per_device(): own = mixed(spread(rot, 8)).reshape(queries, width)]
    ppermute x1, starting transfers between devices: 11.1 us -> 17.8 us  [per_device(): train_o = lax.ppermute(train_rot, 'core', SWAP)]
    ppermute x1, starting transfers between devices: 4.58 us -> 10.5 us  [per_device(): other = lax.ppermute(own, 'core', SWAP)]
    all_to_all x1, blocking collectives: 22 us -> 25.6 us  [per_device(): lax.all_to_all(partial_out.reshape(16, -1, half), ALL, 0, 0, axis_index_g...]
    ppermute x1, waiting for transfers between devices: 4.27 us -> 6.01 us  [per_device(): inner_sum = inner_sum + lax.ppermute(inner_sum, 'z_a', SWAP)]
where the time goes in v8:
time: 158 us
  blocking collectives  85.2 us (54%)
  starting transfers between devices  50.1 us (32%)
  waiting for transfers between devices  14.3 us (9%)
  Pallas kernels  6.42 us (4%)
    all_to_all x1, blocking collectives, per_device(): lax.all_to_all(partial_out.reshape(16, -1, half), ALL, 0, 0, axis_index_g...  25.6 us
    all_to_all x1, blocking collectives, per_device(): own = mixed(spread(rot, 8)).reshape(queries, width)  19.7 us
    ppermute x1, starting transfers between devices, per_device(): train_o = lax.ppermute(train_rot, 'core', SWAP)  17.8 us
    all_to_all x1, blocking collectives, per_device(): eighth = summed(mixed(part.reshape(8, -1, width)))  16 us
    all_to_all x1, blocking collectives, per_device(): inner_sum = summed(near(partial_inner.reshape(8, -1, half)))  14.1 us
    ppermute x1, starting transfers between devices, per_device(): other = lax.ppermute(own, 'core', SWAP)  10.5 us
    all_to_all x1, blocking collectives, per_device(): near(spread((inner_sum * factor).astype(bf16), 8)).reshape(train, half)  9.76 us
    ppermute x1, starting transfers between devices, per_device(): basis_in_o = lax.ppermute(basis_in, ALL, role_pairs(1))  8.84 us
  transfers between devices with their start and end apart: 8, of which 5 were waited for; matrix products, arithmetic and copies ran while one was open for 0% of the time, Pallas kernels for 0%

profile of v8, /device:TPU:1, one launch (start us, length us, event | category | flops | bytes accessed | tf_op | source)
XLA Modules:
  0.0 157.7 jit_solution(2223280887882324254)
XLA Ops:
  0.0 8.8 %collective-permute-start = (bf16[1024,512]{1,0:T(8,128)(2,1)}, bf16[1024,512]{1,0:T(8,128)(2,1)S(1)}, u32[]{:S(2)}, u32[]{:S(2)}) collective-permute-start(bf16[1024,512]{1,0:T(8,128)(2,1)} %b_in.1), channel_id=1, source_target_pairs={{1,0},{2,3},{5,4},{6,7},{8,9},{11,10},{12,13},{15,14},{17,16},{18,... | collective-permute-start | bytes 3145736 | tf_op jit(solution)/shard_map/ppermute | solution.py:187
  8.8 1.3 collective-permute-start.1
  10.1 1.3 collective-permute-start.2
  11.6 0.5 shard_map.73.token
  12.1 2.7 %collective-permute-done.2.grad_o = bf16[768,512]{1,0:T(8,128)(2,1)S(1)} collective-permute-done((bf16[768,512]{1,0:T(8,128)(2,1)}, bf16[768,512]{1,0:T(8,128)(2,1)S(1)}, u32[]{:S(2)}, u32[]{:S(2)}) %collective-permute-start.2) | collective-permute-done | bytes 786464 | tf_op jit(solution)/shard_map/ppermute | solution.py:189
  14.8 2.4 %shard_map.74 = bf16[768,1024]{1,0:T(8,128)(2,1)S(1)} custom-call(s32[4]{0:T(128)S(1)} %pad_add_fusion.place, bf16[768,1024]{1,0:T(8,128)(2,1)S(1)} %copy-done.1, bf16[768,512]{1,0:T(8,128)(2,1)S(1)} %copy-done.3, bf16[1024,512]{1,0:T(8,128)(2,1)S(1)} %copy-done.2, bf16[512,1024]{1,0:T(8,128)(2,1)S(1)} %copy-done, ...), custom_call_target="tpu_custom_call" | custom-call | flops 1610612736 | bytes 4194304 | tf_op jit(solution)/shard_map/pallas_call | solution.py:146
  17.1 16.0 %all_to_all.25 = bf16[8,96,1024]{2,1,0:T(8,128)(2,1)S(1)} all-to-all(bf16[8,96,1024]{2,1,0:T(8,128)(2,1)S(1)} %bitcast.15), channel_id=1, replica_groups={{0,33,64,97,128,161,192,225},{3,34,67,98,131,162,195,226},{4,37,68,101,..., dimensions={0} | all-to-all | bytes 3145728 | tf_op jit(solution)/shard_map/all_to_all | solution.py:212
  33.2 0.3 convert_reduce_fusion
  33.5 3.3 %collective-permute-start.3 = (bf16[96,1024]{1,0:T(8,128)(2,1)S(1)}, bf16[96,1024]{1,0:T(8,128)(2,1)S(1)}, u32[]{:S(2)}, u32[]{:S(2)}) collective-permute-start(bf16[96,1024]{1,0:T(8,128)(2,1)S(1)} %convert_element_type.22), channel_id=1, source_target_pairs={{0,257},{1,5},{3,258},{2,6},{4,261},{5,1},{7,262},{6,2},{9,264},{8... | collective-permute-start | bytes 589832 | tf_op jit(solution)/shard_map/ppermute | solution.py:214
  36.8 17.8 %collective-permute-start.4 = (bf16[384,512]{1,0:T(8,128)(2,1)S(1)}, bf16[384,512]{1,0:T(8,128)(2,1)S(1)}, u32[]{:S(2)}, u32[]{:S(2)}) collective-permute-start(bf16[384,512]{1,0:T(8,128)(2,1)S(1)} %bitcast.21), channel_id=1, source_target_pairs={{0,1},{1,0},{2,3},{3,2},{4,5},{5,4},{6,7},{7,6},{8,9},{9,8},{10,11... | collective-permute-start | bytes 1179656 | tf_op jit(solution)/shard_map/ppermute | solution.py:217
  54.7 1.3 collective-permute-done.4.train_o
  56.2 19.7 %all_to_all.26 = bf16[8,96,1024]{2,1,0:T(8,128)(2,1)S(1)} all-to-all(bf16[8,96,1024]{2,1,0:T(8,128)(2,1)S(1)} %broadcast_in_dim.4), channel_id=1, replica_groups={{0,33,64,97,128,161,192,225},{3,34,67,98,131,162,195,226},{4,37,68,101,..., dimensions={0} | all-to-all | bytes 3145728 | tf_op jit(solution)/shard_map/all_to_all | solution.py:220
  75.9 10.5 %collective-permute-start.5 = (bf16[768,1024]{1,0:T(8,128)(2,1)S(1)}, bf16[768,1024]{1,0:T(8,128)(2,1)S(1)}, u32[]{:S(2)}, u32[]{:S(2)}) collective-permute-start(bf16[768,1024]{1,0:T(8,128)(2,1)S(1)} %bitcast.16), channel_id=1, source_target_pairs={{0,1},{1,0},{2,3},{3,2},{4,5},{5,4},{6,7},{7,6},{8,9},{9,8},{10,11... | collective-permute-start | bytes 4718600 | tf_op jit(solution)/shard_map/ppermute | solution.py:221
  86.4 3.0 %collective-permute-done.5.other = bf16[768,1024]{1,0:T(8,128)(2,1)S(1)} collective-permute-done((bf16[768,1024]{1,0:T(8,128)(2,1)S(1)}, bf16[768,1024]{1,0:T(8,128)(2,1)S(1)}, u32[]{:S(2)}, u32[]{:S(2)}) %collective-permute-start.5) | collective-permute-done | bytes 1572896 | tf_op jit(solution)/shard_map/ppermute | solution.py:221
  89.4 2.9 %shard_map.75 = bf16[384,512]{1,0:T(8,128)(2,1)S(1)} custom-call(s32[4]{0:T(128)S(1)} %pad_add_fusion.place, s32[1]{0:T(128)} %shard_map.73.token, bf16[768,1024]{1,0:T(8,128)(2,1)S(1)} %bitcast.17, bf16[768,1024]{1,0:T(8,128)(2,1)S(1)} %collective-permute-done.5.other, bf16[384,512]{1,0:T(8,128)(2,1)S(1)} %bitcast.22, ...), custom_call_target="tpu_custom_call" | custom-call | flops 1207959552 | bytes 4194304 | tf_op jit(solution)/shard_map/pallas_call | solution.py:146
  92.4 14.1 %all_to_all.27 = bf16[8,48,512]{2,1,0:T(8,128)(2,1)S(1)} all-to-all(bf16[8,48,512]{2,1,0:T(8,128)(2,1)S(1)} %bitcast.23), channel_id=1, replica_groups=mesh['z_hi'=2,'y'=8,'x'=4,'z_a'=2,'z_b'=2,'core'=2] {'x','z_b'}, dimensions={0} | all-to-all | bytes 786432 | tf_op jit(solution)/shard_map/all_to_all | solution.py:232
  106.5 2.8 %collective-permute-start.6 = (f32[48,512]{1,0:T(8,128)S(1)}, f32[48,512]{1,0:T(8,128)S(1)}, u32[]{:S(2)}, u32[]{:S(2)}) collective-permute-start(f32[48,512]{1,0:T(8,128)S(1)} %convert_reduce_fusion.2), channel_id=1, source_target_pairs={{0,4},{4,0},{1,5},{5,1},{2,6},{6,2},{3,7},{7,3},{8,12},{12,8},{9,1... | collective-permute-start | bytes 294920 | tf_op jit(solution)/shard_map/ppermute | solution.py:233
  109.4 6.0 %collective-permute-done.6 = f32[48,512]{1,0:T(8,128)S(1)} collective-permute-done((f32[48,512]{1,0:T(8,128)S(1)}, f32[48,512]{1,0:T(8,128)S(1)}, u32[]{:S(2)}, u32[]{:S(2)}) %collective-permute-start.6) | collective-permute-done | bytes 98336 | tf_op jit(solution)/shard_map/ppermute | solution.py:233
  115.4 9.8 %all_to_all.28 = bf16[8,48,512]{2,1,0:T(8,128)(2,1)S(1)} all-to-all(bf16[8,48,512]{2,1,0:T(8,128)(2,1)S(1)} %broadcast_in_dim.5), channel_id=1, replica_groups=mesh['z_hi'=2,'y'=8,'x'=4,'z_a'=2,'z_b'=2,'core'=2] {'x','z_b'}, dimensions={0} | all-to-all | bytes 786432 | tf_op jit(solution)/shard_map/all_to_all | solution.py:235
  125.2 4.3 %collective-permute-start.7 = (bf16[384,512]{1,0:T(8,128)(2,1)S(1)}, bf16[384,512]{1,0:T(8,128)(2,1)S(1)}, u32[]{:S(2)}, u32[]{:S(2)}) collective-permute-start(bf16[384,512]{1,0:T(8,128)(2,1)S(1)} %bitcast.18), channel_id=1, source_target_pairs={{0,1},{1,0},{2,3},{3,2},{4,5},{5,4},{6,7},{7,6},{8,9},{9,8},{10,11... | collective-permute-start | bytes 1179656 | tf_op jit(solution)/shard_map/ppermute | solution.py:236
  129.5 1.3 collective-permute-done.7.other
  130.8 0.6 shard_map.76
  131.4 25.6 %all_to_all.29 = bf16[16,24,512]{2,1,0:T(8,128)(2,1)S(1)} all-to-all(bf16[16,24,512]{2,1,0:T(8,128)(2,1)S(1)} %bitcast.20), channel_id=1, replica_groups={{0,256,128,384,64,320,192,448,32,288,160,416,96,352,224,480},{1,257,129..., dimensions={0} | all-to-all | bytes 786432 | tf_op jit(solution)/shard_map/all_to_all | solution.py:246
  157.1 0.7 convert_reduce_fusion.1
  (25 shorter events, 0.5 us)
Async XLA Ops:
  0.0 14.7 %collective-permute-start = (bf16[1024,512]{1,0:T(8,128)(2,1)}, bf16[1024,512]{1,0:T(8,128)(2,1)S(1)}, u32[]{:S(2)}, u32[]{:S(2)}) collective-permute-start(bf16[1024,512]{1,0:T(8,128)(2,1)} %b_in.1), channel_id=1, source_target_pairs={{1,0},{2,3},{5,4},{6,7},{8,9},{11,10},{12,13},{15,14},{17,16},{18,... | collective-permute-start | bytes 3145736 | tf_op jit(solution)/shard_map/ppermute | solution.py:187
  8.8 5.9 %collective-permute-start.1 = (bf16[512,1024]{1,0:T(8,128)(2,1)}, bf16[512,1024]{1,0:T(8,128)(2,1)S(1)}, u32[]{:S(2)}, u32[]{:S(2)}) collective-permute-start(bf16[512,1024]{1,0:T(8,128)(2,1)} %b_out.3), channel_id=1, source_target_pairs={{0,1},{3,2},{4,5},{7,6},{9,8},{10,11},{13,12},{14,15},{16,17},{19,... | collective-permute-start | bytes 3145736 | tf_op jit(solution)/shard_map/ppermute | solution.py:188
  10.1 4.6 %collective-permute-start.2 = (bf16[768,512]{1,0:T(8,128)(2,1)}, bf16[768,512]{1,0:T(8,128)(2,1)S(1)}, u32[]{:S(2)}, u32[]{:S(2)}) collective-permute-start(bf16[768,512]{1,0:T(8,128)(2,1)} %grad.1), channel_id=1, source_target_pairs={{0,1},{3,2},{4,5},{7,6},{9,8},{10,11},{13,12},{14,15},{16,17},{19,... | collective-permute-start | bytes 2359304 | tf_op jit(solution)/shard_map/ppermute | solution.py:189
  11.5 3.2 %copy-start = (bf16[512,1024]{1,0:T(8,128)(2,1)S(1)}, bf16[512,1024]{1,0:T(8,128)(2,1)}, u32[]{:S(2)}) copy-start(bf16[512,1024]{1,0:T(8,128)(2,1)} %b_out.3) | copy-start | bytes 3145732
  11.5 3.2 %copy-start.1 = (bf16[768,1024]{1,0:T(8,128)(2,1)S(1)}, bf16[768,1024]{1,0:T(8,128)(2,1)}, u32[]{:S(2)}) copy-start(bf16[768,1024]{1,0:T(8,128)(2,1)} %act.1) | copy-start | bytes 4718596
  11.6 3.2 %copy-start.2 = (bf16[1024,512]{1,0:T(8,128)(2,1)S(1)}, bf16[1024,512]{1,0:T(8,128)(2,1)}, u32[]{:S(2)}) copy-start(bf16[1024,512]{1,0:T(8,128)(2,1)} %b_in.1) | copy-start | bytes 3145732
  11.6 3.2 %copy-start.3 = (bf16[768,512]{1,0:T(8,128)(2,1)S(1)}, bf16[768,512]{1,0:T(8,128)(2,1)}, u32[]{:S(2)}) copy-start(bf16[768,512]{1,0:T(8,128)(2,1)} %grad.1) | copy-start | bytes 2359300
  33.2 3.6 %copy-start.6 = (bf16[384,512]{1,0:T(8,128)(2,1)S(1)}, bf16[384,512]{1,0:T(8,128)(2,1)}, u32[]{:S(2)}) copy-start(bf16[384,512]{1,0:T(8,128)(2,1)} %param.9) | copy-start | bytes 1179652
  33.5 21.1 %collective-permute-start.3 = (bf16[96,1024]{1,0:T(8,128)(2,1)S(1)}, bf16[96,1024]{1,0:T(8,128)(2,1)S(1)}, u32[]{:S(2)}, u32[]{:S(2)}) collective-permute-start(bf16[96,1024]{1,0:T(8,128)(2,1)S(1)} %convert_element_type.22), channel_id=1, source_target_pairs={{0,257},{1,5},{3,258},{2,6},{4,261},{5,1},{7,262},{6,2},{9,264},{8... | collective-permute-start | bytes 589832 | tf_op jit(solution)/shard_map/ppermute | solution.py:214
  36.8 19.2 %collective-permute-start.4 = (bf16[384,512]{1,0:T(8,128)(2,1)S(1)}, bf16[384,512]{1,0:T(8,128)(2,1)S(1)}, u32[]{:S(2)}, u32[]{:S(2)}) collective-permute-start(bf16[384,512]{1,0:T(8,128)(2,1)S(1)} %bitcast.21), channel_id=1, source_target_pairs={{0,1},{1,0},{2,3},{3,2},{4,5},{5,4},{6,7},{7,6},{8,9},{9,8},{10,11... | collective-permute-start | bytes 1179656 | tf_op jit(solution)/shard_map/ppermute | solution.py:217
  56.2 33.2 %copy-start.4 = (f32[16384]{0:T(1024)S(1)}, f32[16384]{0:T(1024)}, u32[]{:S(2)}) copy-start(f32[16384]{0:T(1024)} %param.13) | copy-start | bytes 196612
  56.2 33.2 %copy-start.5 = (f32[16384]{0:T(1024)S(1)}, f32[16384]{0:T(1024)}, u32[]{:S(2)}) copy-start(f32[16384]{0:T(1024)} %param.12) | copy-start | bytes 196612
  75.9 13.6 %collective-permute-start.5 = (bf16[768,1024]{1,0:T(8,128)(2,1)S(1)}, bf16[768,1024]{1,0:T(8,128)(2,1)S(1)}, u32[]{:S(2)}, u32[]{:S(2)}) collective-permute-start(bf16[768,1024]{1,0:T(8,128)(2,1)S(1)} %bitcast.16), channel_id=1, source_target_pairs={{0,1},{1,0},{2,3},{3,2},{4,5},{5,4},{6,7},{7,6},{8,9},{9,8},{10,11... | collective-permute-start | bytes 4718600 | tf_op jit(solution)/shard_map/ppermute | solution.py:221
  106.5 8.8 %collective-permute-start.6 = (f32[48,512]{1,0:T(8,128)S(1)}, f32[48,512]{1,0:T(8,128)S(1)}, u32[]{:S(2)}, u32[]{:S(2)}) collective-permute-start(f32[48,512]{1,0:T(8,128)S(1)} %convert_reduce_fusion.2), channel_id=1, source_target_pairs={{0,4},{4,0},{1,5},{5,1},{2,6},{6,2},{3,7},{7,3},{8,12},{12,8},{9,1... | collective-permute-start | bytes 294920 | tf_op jit(solution)/shard_map/ppermute | solution.py:233
  125.2 5.6 %collective-permute-start.7 = (bf16[384,512]{1,0:T(8,128)(2,1)S(1)}, bf16[384,512]{1,0:T(8,128)(2,1)S(1)}, u32[]{:S(2)}, u32[]{:S(2)}) collective-permute-start(bf16[384,512]{1,0:T(8,128)(2,1)S(1)} %bitcast.18), channel_id=1, source_target_pairs={{0,1},{1,0},{2,3},{3,2},{4,5},{5,4},{6,7},{7,6},{8,9},{9,8},{10,11... | collective-permute-start | bytes 1179656 | tf_op jit(solution)/shard_map/ppermute | solution.py:236

commit v9 on v8

--- a/solution.py
+++ b/solution.py
@@ -54,11 +54,6 @@
     return list(zip(ids.reshape(-1).tolist(), to.reshape(-1).tolist()))
 
 
-def final_groups():
-    ids = np.arange(np.prod(SIZES)).reshape(2, 2, 2, 2, -1)
-    return ids.transpose(3, 2, 1, 0, 4).reshape(16, -1).T.tolist()
-
-
 def role_pairs(source):
     ids = role_ids().reshape(-1, 2)
     return list(zip(ids[:, source].tolist(), ids[:, 1 - source].tolist()))
@@ -80,7 +75,7 @@
     token[0] = core[0]
 
 
-def rotate_kernel(place, act, grad, b_in, b_out, b_in_o, grad_o, b_out_o, out):
+def rotate_kernel(place, act, grad, b_in, b_out, b_in_o, b_out_o, grad_o, out, held, sem):
     half = grad.shape[1]
 
     def joined(low, high):
@@ -97,7 +92,10 @@
 
     @pl.when(place[3] == 1)
     def _():
-        out[...] = (dot(grad_o[...], b_out_o[...]) + dot(grad[...], b_out[...])).astype(bf16)
+        load = pltpu.make_async_copy(grad_o, held, sem)
+        load.start()
+        load.wait()
+        out[...] = (dot(held[...], b_out_o[...]) + dot(grad[...], b_out[...])).astype(bf16)
 
 
 def outer_kernel(queries, place, token, own, other, train, train_o, e_out, e_in, out):
@@ -202,18 +200,17 @@
     )
     part = call(
         rotate_kernel,
-        (place, query_act, query_grad, basis_in, basis_out, basis_in_o, grad_o, basis_out_o),
-        [SMEM] + [VMEM] * 7,
+        (place, query_act, query_grad, basis_in, basis_out, basis_in_o, basis_out_o, grad_o),
+        [SMEM] + [VMEM] * 6 + [ANY],
         shape((queries, width), bf16),
         VMEM,
         2 * queries * width * width,
         32,
+        (pltpu.VMEM((queries, half), bf16), pltpu.SemaphoreType.DMA),
     )
     eighth = summed(mixed(part.reshape(8, -1, width)))
     eighth, train_rot = lax.optimization_barrier((eighth, train_rot))
     far = lax.ppermute(eighth.astype(bf16), ALL, mixed_pairs()).astype(f32)
-    train_rot = train_rot.reshape(2, 2, 2, 2, -1, half).transpose(3, 2, 1, 0, 4, 5)
-    train_rot = train_rot.reshape(train, half)
     train_o = lax.ppermute(train_rot, "core", SWAP)
     rot = (eighth + far).astype(bf16)
     rot, train_o = lax.optimization_barrier((rot, train_o))
@@ -230,7 +227,9 @@
         32,
     )
     inner_sum = summed(near(partial_inner.reshape(8, -1, half)))
-    inner_sum = inner_sum + lax.ppermute(inner_sum, "z_a", SWAP)
+    inner_sum = jnp.sum(
+        lax.all_to_all(spread(inner_sum, 2), "z_a", 0, 0, tiled=True), axis=0
+    )
     factor = 1.0 / float(eig_in.shape[0]) ** 0.5
     inner = near(spread((inner_sum * factor).astype(bf16), 8)).reshape(train, half)
     inner_o = lax.ppermute(inner, "core", SWAP)
@@ -243,10 +242,7 @@
         2 * train * half * width,
         32,
     )
-    final = lax.all_to_all(
-        partial_out.reshape(16, -1, half), ALL, 0, 0, axis_index_groups=final_groups(), tiled=True
-    )
-    return summed(final)
+    return summed(lax.all_to_all(partial_out.reshape(16, -1, half), ROW, 0, 0, tiled=True))
 
 
 def solution(mesh):

time: 158 us -> 158 us (level); the launches traced: 158 us -> 156 us
  blocking collectives: 85.2 us -> 91.5 us
  waiting for transfers between devices: 14.3 us -> 8.4 us
  starting transfers between devices: 50.1 us -> 47 us
    all_to_all x1 -> x2, blocking collectives: 25.6 us -> 32 us  [the longest x1 22.4 us: per_device(): lax.all_to_all(partial_out.reshape(16, -1, half), ROW, 0, 0, tiled=True)]
    ppermute x1 -> x0, waiting for transfers between devices: 6.01 us -> none  [per_device(): inner_sum = inner_sum + lax.ppermute(inner_sum, 'z_a', SWAP)]
    ppermute x1 -> x0, starting transfers between devices: 2.82 us -> none  [per_device(): inner_sum = inner_sum + lax.ppermute(inner_sum, 'z_a', SWAP)]
  transfers between devices with their start and end apart: 8 -> 7, of which waited for: 5 -> 4; matrix products, arithmetic and copies ran while one was open for 0% -> 0% of each run, Pallas kernels for 0% -> 0%
where the time goes in v9:
time: 158 us; the launch traced here: 156 us
  blocking collectives  91.5 us (58%)
  starting transfers between devices  47 us (30%)
  waiting for transfers between devices  8.4 us (5%)
  Pallas kernels  7.55 us (5%)
    all_to_all x1, blocking collectives, per_device(): lax.all_to_all(partial_out.reshape(16, -1, half), ROW, 0, 0, tiled=True)  22.4 us
    all_to_all x1, blocking collectives, per_device(): own = mixed(spread(rot, 8)).reshape(queries, width)  19.7 us
    ppermute x1, starting transfers between devices, per_device(): train_o = lax.ppermute(train_rot, 'core', SWAP)  17.3 us
    all_to_all x1, blocking collectives, per_device(): eighth = summed(mixed(part.reshape(8, -1, width)))  15.9 us
    all_to_all x1, blocking collectives, per_device(): inner_sum = summed(near(partial_inner.reshape(8, -1, half)))  14.1 us
    ppermute x1, starting transfers between devices, per_device(): other = lax.ppermute(own, 'core', SWAP)  10.6 us
    all_to_all x1, blocking collectives, per_device(): near(spread((inner_sum * factor).astype(bf16), 8)).reshape(train, half)  9.75 us
    all_to_all x1, blocking collectives, per_device(): lax.all_to_all(spread(inner_sum, 2), 'z_a', 0, 0, tiled=True)  9.54 us
  transfers between devices with their start and end apart: 7, of which 4 were waited for; matrix products, arithmetic and copies ran while one was open for 0% of the time, Pallas kernels for 0%

profile of v9, /device:TPU:1, one launch (start us, length us, event | category | flops | bytes accessed | tf_op | source)
XLA Modules:
  0.0 156.1 jit_solution(12814141609024876601)
XLA Ops:
  0.0 8.8 %collective-permute-start = (bf16[1024,512]{1,0:T(8,128)(2,1)}, bf16[1024,512]{1,0:T(8,128)(2,1)S(1)}, u32[]{:S(2)}, u32[]{:S(2)}) collective-permute-start(bf16[1024,512]{1,0:T(8,128)(2,1)} %b_in.1), channel_id=1, source_target_pairs={{1,0},{2,3},{5,4},{6,7},{8,9},{11,10},{12,13},{15,14},{17,16},{18,... | collective-permute-start | bytes 3145736 | tf_op jit(solution)/shard_map/ppermute | solution.py:185
  8.8 1.3 collective-permute-start.1
  10.1 1.3 collective-permute-start.2
  11.6 0.5 shard_map.73.token
  12.1 2.8 %collective-permute-done.2.grad_o = bf16[768,512]{1,0:T(8,128)(2,1)} collective-permute-done((bf16[768,512]{1,0:T(8,128)(2,1)}, bf16[768,512]{1,0:T(8,128)(2,1)}, u32[]{:S(2)}, u32[]{:S(2)}) %collective-permute-start.2) | collective-permute-done | bytes 786464 | tf_op jit(solution)/shard_map/ppermute | solution.py:187
  14.9 3.5 %shard_map.74 = bf16[768,1024]{1,0:T(8,128)(2,1)S(1)} custom-call(s32[4]{0:T(128)S(1)} %pad_add_fusion.place, bf16[768,1024]{1,0:T(8,128)(2,1)S(1)} %copy-done.1, bf16[768,512]{1,0:T(8,128)(2,1)S(1)} %copy-done.3, bf16[1024,512]{1,0:T(8,128)(2,1)S(1)} %copy-done.2, bf16[512,1024]{1,0:T(8,128)(2,1)S(1)} %copy-done, ...), custom_call_target="tpu_custom_call" | custom-call | flops 1610612736 | bytes 4194304 | tf_op jit(solution)/shard_map/pallas_call | solution.py:144
  18.4 15.9 %all_to_all.30 = bf16[8,96,1024]{2,1,0:T(8,128)(2,1)S(1)} all-to-all(bf16[8,96,1024]{2,1,0:T(8,128)(2,1)S(1)} %bitcast.11), channel_id=1, replica_groups={{0,33,64,97,128,161,192,225},{3,34,67,98,131,162,195,226},{4,37,68,101,..., dimensions={0} | all-to-all | bytes 3145728 | tf_op jit(solution)/shard_map/all_to_all | solution.py:211
  34.4 0.3 convert_reduce_fusion
  34.7 3.5 %collective-permute-start.3 = (bf16[96,1024]{1,0:T(8,128)(2,1)S(1)}, bf16[96,1024]{1,0:T(8,128)(2,1)S(1)}, u32[]{:S(2)}, u32[]{:S(2)}) collective-permute-start(bf16[96,1024]{1,0:T(8,128)(2,1)S(1)} %convert_element_type.26), channel_id=1, source_target_pairs={{0,257},{1,5},{3,258},{2,6},{4,261},{5,1},{7,262},{6,2},{9,264},{8... | collective-permute-start | bytes 589832 | tf_op jit(solution)/shard_map/ppermute | solution.py:213
  38.2 17.3 %collective-permute-start.4 = (bf16[384,512]{1,0:T(8,128)(2,1)S(1)}, bf16[384,512]{1,0:T(8,128)(2,1)S(1)}, u32[]{:S(2)}, u32[]{:S(2)}) collective-permute-start(bf16[384,512]{1,0:T(8,128)(2,1)S(1)} %copy-done.4), channel_id=1, source_target_pairs={{0,1},{1,0},{2,3},{3,2},{4,5},{5,4},{6,7},{7,6},{8,9},{9,8},{10,11... | collective-permute-start | bytes 1179656 | tf_op jit(solution)/shard_map/ppermute | solution.py:214
  55.5 1.3 collective-permute-done.4.train_o
  56.8 0.2 broadcast_in_dim.6
  57.0 19.7 %all_to_all.31 = bf16[8,96,1024]{2,1,0:T(8,128)(2,1)S(1)} all-to-all(bf16[8,96,1024]{2,1,0:T(8,128)(2,1)S(1)} %broadcast_in_dim.6), channel_id=1, replica_groups={{0,33,64,97,128,161,192,225},{3,34,67,98,131,162,195,226},{4,37,68,101,..., dimensions={0} | all-to-all | bytes 3145728 | tf_op jit(solution)/shard_map/all_to_all | solution.py:217
  76.6 10.6 %collective-permute-start.5 = (bf16[768,1024]{1,0:T(8,128)(2,1)S(1)}, bf16[768,1024]{1,0:T(8,128)(2,1)S(1)}, u32[]{:S(2)}, u32[]{:S(2)}) collective-permute-start(bf16[768,1024]{1,0:T(8,128)(2,1)S(1)} %bitcast.12), channel_id=1, source_target_pairs={{0,1},{1,0},{2,3},{3,2},{4,5},{5,4},{6,7},{7,6},{8,9},{9,8},{10,11... | collective-permute-start | bytes 4718600 | tf_op jit(solution)/shard_map/ppermute | solution.py:218
  87.2 3.0 %collective-permute-done.5.other = bf16[768,1024]{1,0:T(8,128)(2,1)S(1)} collective-permute-done((bf16[768,1024]{1,0:T(8,128)(2,1)S(1)}, bf16[768,1024]{1,0:T(8,128)(2,1)S(1)}, u32[]{:S(2)}, u32[]{:S(2)}) %collective-permute-start.5) | collective-permute-done | bytes 1572896 | tf_op jit(solution)/shard_map/ppermute | solution.py:218
  90.2 2.9 %shard_map.75 = bf16[384,512]{1,0:T(8,128)(2,1)S(1)} custom-call(s32[4]{0:T(128)S(1)} %pad_add_fusion.place, s32[1]{0:T(128)} %shard_map.73.token, bf16[768,1024]{1,0:T(8,128)(2,1)S(1)} %bitcast.13, bf16[768,1024]{1,0:T(8,128)(2,1)S(1)} %collective-permute-done.5.other, bf16[384,512]{1,0:T(8,128)(2,1)S(1)} %copy-done.4, ...), custom_call_target="tpu_custom_call" | custom-call | flops 1207959552 | bytes 4194304 | tf_op jit(solution)/shard_map/pallas_call | solution.py:144
  93.1 14.1 %all_to_all.32 = bf16[8,48,512]{2,1,0:T(8,128)(2,1)S(1)} all-to-all(bf16[8,48,512]{2,1,0:T(8,128)(2,1)S(1)} %bitcast.17), channel_id=1, replica_groups=mesh['z_hi'=2,'y'=8,'x'=4,'z_a'=2,'z_b'=2,'core'=2] {'x','z_b'}, dimensions={0} | all-to-all | bytes 786432 | tf_op jit(solution)/shard_map/all_to_all | solution.py:229
  107.3 9.5 %all_to_all.33 = f32[2,48,512]{2,1,0:T(8,128)S(1)} all-to-all(f32[2,48,512]{2,1,0:T(8,128)S(1)} %broadcast_in_dim.7), channel_id=1, replica_groups=mesh['z_hi'=2,'y'=8,'x'=4,'z_a'=2,'z_b'=2,'core'=2] {'z_a'}, dimensions={0} | all-to-all | bytes 393216 | tf_op jit(solution)/shard_map/all_to_all | solution.py:231
  117.0 9.8 %all_to_all.34 = bf16[8,48,512]{2,1,0:T(8,128)(2,1)S(1)} all-to-all(bf16[8,48,512]{2,1,0:T(8,128)(2,1)S(1)} %broadcast_in_dim.8), channel_id=1, replica_groups=mesh['z_hi'=2,'y'=8,'x'=4,'z_a'=2,'z_b'=2,'core'=2] {'x','z_b'}, dimensions={0} | all-to-all | bytes 786432 | tf_op jit(solution)/shard_map/all_to_all | solution.py:234
  126.7 4.3 %collective-permute-start.6 = (bf16[384,512]{1,0:T(8,128)(2,1)S(1)}, bf16[384,512]{1,0:T(8,128)(2,1)S(1)}, u32[]{:S(2)}, u32[]{:S(2)}) collective-permute-start(bf16[384,512]{1,0:T(8,128)(2,1)S(1)} %bitcast.14), channel_id=1, source_target_pairs={{0,1},{1,0},{2,3},{3,2},{4,5},{5,4},{6,7},{7,6},{8,9},{9,8},{10,11... | collective-permute-start | bytes 1179656 | tf_op jit(solution)/shard_map/ppermute | solution.py:235
  131.0 1.3 collective-permute-done.6.other
  132.3 0.6 shard_map.76
  132.9 22.4 %all_to_all.35 = bf16[16,24,512]{2,1,0:T(8,128)(2,1)S(1)} all-to-all(bf16[16,24,512]{2,1,0:T(8,128)(2,1)S(1)} %bitcast.16), channel_id=1, replica_groups=mesh['z_hi'=2,'y'=8,'x'=4,'z_a'=2,'z_b'=2,'core'=2] {'z_hi','y'}, dimensions={0} | all-to-all | bytes 786432 | tf_op jit(solution)/shard_map/all_to_all | solution.py:245
  155.4 0.7 convert_reduce_fusion.1
  (25 shorter events, 0.3 us)
Async XLA Ops:
  0.0 14.9 %collective-permute-start = (bf16[1024,512]{1,0:T(8,128)(2,1)}, bf16[1024,512]{1,0:T(8,128)(2,1)S(1)}, u32[]{:S(2)}, u32[]{:S(2)}) collective-permute-start(bf16[1024,512]{1,0:T(8,128)(2,1)} %b_in.1), channel_id=1, source_target_pairs={{1,0},{2,3},{5,4},{6,7},{8,9},{11,10},{12,13},{15,14},{17,16},{18,... | collective-permute-start | bytes 3145736 | tf_op jit(solution)/shard_map/ppermute | solution.py:185
  8.8 6.0 %collective-permute-start.1 = (bf16[512,1024]{1,0:T(8,128)(2,1)}, bf16[512,1024]{1,0:T(8,128)(2,1)S(1)}, u32[]{:S(2)}, u32[]{:S(2)}) collective-permute-start(bf16[512,1024]{1,0:T(8,128)(2,1)} %b_out.3), channel_id=1, source_target_pairs={{0,1},{3,2},{4,5},{7,6},{9,8},{10,11},{13,12},{14,15},{16,17},{19,... | collective-permute-start | bytes 3145736 | tf_op jit(solution)/shard_map/ppermute | solution.py:186
  10.1 4.7 %collective-permute-start.2 = (bf16[768,512]{1,0:T(8,128)(2,1)}, bf16[768,512]{1,0:T(8,128)(2,1)}, u32[]{:S(2)}, u32[]{:S(2)}) collective-permute-start(bf16[768,512]{1,0:T(8,128)(2,1)} %grad.1), channel_id=1, source_target_pairs={{0,1},{3,2},{4,5},{7,6},{9,8},{10,11},{13,12},{14,15},{16,17},{19,... | collective-permute-start | bytes 2359304 | tf_op jit(solution)/shard_map/ppermute | solution.py:187
  11.5 3.3 %copy-start = (bf16[512,1024]{1,0:T(8,128)(2,1)S(1)}, bf16[512,1024]{1,0:T(8,128)(2,1)}, u32[]{:S(2)}) copy-start(bf16[512,1024]{1,0:T(8,128)(2,1)} %b_out.3) | copy-start | bytes 3145732
  11.5 3.3 %copy-start.1 = (bf16[768,1024]{1,0:T(8,128)(2,1)S(1)}, bf16[768,1024]{1,0:T(8,128)(2,1)}, u32[]{:S(2)}) copy-start(bf16[768,1024]{1,0:T(8,128)(2,1)} %act.1) | copy-start | bytes 4718596
  11.6 3.3 %copy-start.2 = (bf16[1024,512]{1,0:T(8,128)(2,1)S(1)}, bf16[1024,512]{1,0:T(8,128)(2,1)}, u32[]{:S(2)}) copy-start(bf16[1024,512]{1,0:T(8,128)(2,1)} %b_in.1) | copy-start | bytes 3145732
  11.6 3.4 %copy-start.3 = (bf16[768,512]{1,0:T(8,128)(2,1)S(1)}, bf16[768,512]{1,0:T(8,128)(2,1)}, u32[]{:S(2)}) copy-start(bf16[768,512]{1,0:T(8,128)(2,1)} %grad.1) | copy-start | bytes 2359300
  34.4 3.8 %copy-start.4 = (bf16[384,512]{1,0:T(8,128)(2,1)S(1)}, bf16[384,512]{1,0:T(8,128)(2,1)}, u32[]{:S(2)}) copy-start(bf16[384,512]{1,0:T(8,128)(2,1)} %train) | copy-start | bytes 1179652
  34.7 20.8 %collective-permute-start.3 = (bf16[96,1024]{1,0:T(8,128)(2,1)S(1)}, bf16[96,1024]{1,0:T(8,128)(2,1)S(1)}, u32[]{:S(2)}, u32[]{:S(2)}) collective-permute-start(bf16[96,1024]{1,0:T(8,128)(2,1)S(1)} %convert_element_type.26), channel_id=1, source_target_pairs={{0,257},{1,5},{3,258},{2,6},{4,261},{5,1},{7,262},{6,2},{9,264},{8... | collective-permute-start | bytes 589832 | tf_op jit(solution)/shard_map/ppermute | solution.py:213
  38.2 18.6 %collective-permute-start.4 = (bf16[384,512]{1,0:T(8,128)(2,1)S(1)}, bf16[384,512]{1,0:T(8,128)(2,1)S(1)}, u32[]{:S(2)}, u32[]{:S(2)}) collective-permute-start(bf16[384,512]{1,0:T(8,128)(2,1)S(1)} %copy-done.4), channel_id=1, source_target_pairs={{0,1},{1,0},{2,3},{3,2},{4,5},{5,4},{6,7},{7,6},{8,9},{9,8},{10,11... | collective-permute-start | bytes 1179656 | tf_op jit(solution)/shard_map/ppermute | solution.py:214
  57.0 33.3 %copy-start.5 = (f32[16384]{0:T(1024)S(1)}, f32[16384]{0:T(1024)}, u32[]{:S(2)}) copy-start(f32[16384]{0:T(1024)} %param.13) | copy-start | bytes 196612
  57.0 33.3 %copy-start.6 = (f32[16384]{0:T(1024)S(1)}, f32[16384]{0:T(1024)}, u32[]{:S(2)}) copy-start(f32[16384]{0:T(1024)} %param.12) | copy-start | bytes 196612
  76.6 13.6 %collective-permute-start.5 = (bf16[768,1024]{1,0:T(8,128)(2,1)S(1)}, bf16[768,1024]{1,0:T(8,128)(2,1)S(1)}, u32[]{:S(2)}, u32[]{:S(2)}) collective-permute-start(bf16[768,1024]{1,0:T(8,128)(2,1)S(1)} %bitcast.12), channel_id=1, source_target_pairs={{0,1},{1,0},{2,3},{3,2},{4,5},{5,4},{6,7},{7,6},{8,9},{9,8},{10,11... | collective-permute-start | bytes 4718600 | tf_op jit(solution)/shard_map/ppermute | solution.py:218
  126.7 5.6 %collective-permute-start.6 = (bf16[384,512]{1,0:T(8,128)(2,1)S(1)}, bf16[384,512]{1,0:T(8,128)(2,1)S(1)}, u32[]{:S(2)}, u32[]{:S(2)}) collective-permute-start(bf16[384,512]{1,0:T(8,128)(2,1)S(1)} %bitcast.14), channel_id=1, source_target_pairs={{0,1},{1,0},{2,3},{3,2},{4,5},{5,4},{6,7},{7,6},{8,9},{9,8},{10,11... | collective-permute-start | bytes 1179656 | tf_op jit(solution)/shard_map/ppermute | solution.py:235

commit v10 on v8

--- a/solution.py
+++ b/solution.py
@@ -14,7 +14,7 @@
 COL = (*CHIPS, "core")
 ALL = ROW + COL
 SIZES = (2, 8, 4, 2, 2, 2)
-NEAR = ("x", "z_b")
+NEAR = ("x", "z_a")
 SWAP = [(0, 1), (1, 0)]
 MIB = 1024 * 1024
 
@@ -52,11 +52,6 @@
     to[..., 0] = ids[::-1, ..., 0]
     to[..., 1] = ids[:, :, :, ::-1, :, 1]
     return list(zip(ids.reshape(-1).tolist(), to.reshape(-1).tolist()))
-
-
-def final_groups():
-    ids = np.arange(np.prod(SIZES)).reshape(2, 2, 2, 2, -1)
-    return ids.transpose(3, 2, 1, 0, 4).reshape(16, -1).T.tolist()
 
 
 def role_pairs(source):
@@ -212,8 +207,6 @@
     eighth = summed(mixed(part.reshape(8, -1, width)))
     eighth, train_rot = lax.optimization_barrier((eighth, train_rot))
     far = lax.ppermute(eighth.astype(bf16), ALL, mixed_pairs()).astype(f32)
-    train_rot = train_rot.reshape(2, 2, 2, 2, -1, half).transpose(3, 2, 1, 0, 4, 5)
-    train_rot = train_rot.reshape(train, half)
     train_o = lax.ppermute(train_rot, "core", SWAP)
     rot = (eighth + far).astype(bf16)
     rot, train_o = lax.optimization_barrier((rot, train_o))
@@ -230,7 +223,7 @@
         32,
     )
     inner_sum = summed(near(partial_inner.reshape(8, -1, half)))
-    inner_sum = inner_sum + lax.ppermute(inner_sum, "z_a", SWAP)
+    inner_sum = inner_sum + lax.ppermute(inner_sum, "z_b", SWAP)
     factor = 1.0 / float(eig_in.shape[0]) ** 0.5
     inner = near(spread((inner_sum * factor).astype(bf16), 8)).reshape(train, half)
     inner_o = lax.ppermute(inner, "core", SWAP)
@@ -243,10 +236,7 @@
         2 * train * half * width,
         32,
     )
-    final = lax.all_to_all(
-        partial_out.reshape(16, -1, half), ALL, 0, 0, axis_index_groups=final_groups(), tiled=True
-    )
-    return summed(final)
+    return summed(lax.all_to_all(partial_out.reshape(16, -1, half), ROW, 0, 0, tiled=True))
 
 
 def solution(mesh):

time: 158 us -> 164 us (1.038)
  blocking collectives: 85.2 us -> 94.6 us
  starting transfers between devices: 50.1 us -> 47.4 us
  waiting for transfers between devices: 14.3 us -> 12.1 us
    all_to_all x1, blocking collectives: 9.76 us -> 16.6 us  [per_device(): near(spread((inner_sum * factor).astype(bf16), 8)).reshape(train, half)]
    all_to_all x1, blocking collectives: 14.1 us -> 20 us  [per_device(): inner_sum = summed(near(partial_inner.reshape(8, -1, half)))]
    all_to_all x1, blocking collectives: 25.6 us -> 22.3 us  [per_device(): lax.all_to_all(partial_out.reshape(16, -1, half), ROW, 0, 0, tiled=True)]
    ppermute x1, waiting for transfers between devices: 6.01 us -> 3.85 us  [per_device(): inner_sum = inner_sum + lax.ppermute(inner_sum, 'z_b', SWAP)]
    ppermute x1, starting transfers between devices: 4.27 us -> 2.44 us  [per_device(): inner_o = lax.ppermute(inner, 'core', SWAP)]
where the time goes in v10:
time: 164 us; the launch traced here: 162 us
  blocking collectives  94.6 us (58%)
  starting transfers between devices  47.4 us (29%)
  waiting for transfers between devices  12.1 us (7%)
  Pallas kernels  6.45 us (4%)
    all_to_all x1, blocking collectives, per_device(): lax.all_to_all(partial_out.reshape(16, -1, half), ROW, 0, 0, tiled=True)  22.3 us
    all_to_all x1, blocking collectives, per_device(): inner_sum = summed(near(partial_inner.reshape(8, -1, half)))  20 us
    all_to_all x1, blocking collectives, per_device(): own = mixed(spread(rot, 8)).reshape(queries, width)  19.7 us
    ppermute x1, starting transfers between devices, per_device(): train_o = lax.ppermute(train_rot, 'core', SWAP)  17.8 us
    all_to_all x1, blocking collectives, per_device(): near(spread((inner_sum * factor).astype(bf16), 8)).reshape(train, half)  16.6 us
    all_to_all x1, blocking collectives, per_device(): eighth = summed(mixed(part.reshape(8, -1, width)))  16 us
    ppermute x1, starting transfers between devices, per_device(): other = lax.ppermute(own, 'core', SWAP)  10.6 us
    ppermute x1, starting transfers between devices, per_device(): basis_in_o = lax.ppermute(basis_in, ALL, role_pairs(1))  8.84 us
  transfers between devices with their start and end apart: 8, of which 5 were waited for; matrix products, arithmetic and copies ran while one was open for 0% of the time, Pallas kernels for 0%

profile of v10, /device:TPU:1, one launch (start us, length us, event | category | flops | bytes accessed | tf_op | source)
XLA Modules:
  0.0 162.2 jit_solution(8203737623057670144)
XLA Ops:
  0.0 8.8 %collective-permute-start = (bf16[1024,512]{1,0:T(8,128)(2,1)}, bf16[1024,512]{1,0:T(8,128)(2,1)S(1)}, u32[]{:S(2)}, u32[]{:S(2)}) collective-permute-start(bf16[1024,512]{1,0:T(8,128)(2,1)} %b_in.1), channel_id=1, source_target_pairs={{1,0},{2,3},{5,4},{6,7},{8,9},{11,10},{12,13},{15,14},{17,16},{18,... | collective-permute-start | bytes 3145736 | tf_op jit(solution)/shard_map/ppermute | solution.py:182
  8.8 1.3 collective-permute-start.1
  10.1 1.3 collective-permute-start.2
  11.6 0.5 shard_map.73.token
  12.1 2.7 %collective-permute-done.2.grad_o = bf16[768,512]{1,0:T(8,128)(2,1)S(1)} collective-permute-done((bf16[768,512]{1,0:T(8,128)(2,1)}, bf16[768,512]{1,0:T(8,128)(2,1)S(1)}, u32[]{:S(2)}, u32[]{:S(2)}) %collective-permute-start.2) | collective-permute-done | bytes 786464 | tf_op jit(solution)/shard_map/ppermute | solution.py:184
  14.8 2.4 %shard_map.74 = bf16[768,1024]{1,0:T(8,128)(2,1)S(1)} custom-call(s32[4]{0:T(128)S(1)} %pad_add_fusion.place, bf16[768,1024]{1,0:T(8,128)(2,1)S(1)} %copy-done.1, bf16[768,512]{1,0:T(8,128)(2,1)S(1)} %copy-done.3, bf16[1024,512]{1,0:T(8,128)(2,1)S(1)} %copy-done.2, bf16[512,1024]{1,0:T(8,128)(2,1)S(1)} %copy-done, ...), custom_call_target="tpu_custom_call" | custom-call | flops 1610612736 | bytes 4194304 | tf_op jit(solution)/shard_map/pallas_call | solution.py:141
  17.1 16.0 %all_to_all.25 = bf16[8,96,1024]{2,1,0:T(8,128)(2,1)S(1)} all-to-all(bf16[8,96,1024]{2,1,0:T(8,128)(2,1)S(1)} %bitcast.11), channel_id=1, replica_groups={{0,33,64,97,128,161,192,225},{3,34,67,98,131,162,195,226},{4,37,68,101,..., dimensions={0} | all-to-all | bytes 3145728 | tf_op jit(solution)/shard_map/all_to_all | solution.py:207
  33.2 0.3 convert_reduce_fusion
  33.5 3.3 %collective-permute-start.3 = (bf16[96,1024]{1,0:T(8,128)(2,1)S(1)}, bf16[96,1024]{1,0:T(8,128)(2,1)S(1)}, u32[]{:S(2)}, u32[]{:S(2)}) collective-permute-start(bf16[96,1024]{1,0:T(8,128)(2,1)S(1)} %convert_element_type.22), channel_id=1, source_target_pairs={{0,257},{1,5},{3,258},{2,6},{4,261},{5,1},{7,262},{6,2},{9,264},{8... | collective-permute-start | bytes 589832 | tf_op jit(solution)/shard_map/ppermute | solution.py:209
  36.8 17.8 %collective-permute-start.4 = (bf16[384,512]{1,0:T(8,128)(2,1)S(1)}, bf16[384,512]{1,0:T(8,128)(2,1)S(1)}, u32[]{:S(2)}, u32[]{:S(2)}) collective-permute-start(bf16[384,512]{1,0:T(8,128)(2,1)S(1)} %copy-done.4), channel_id=1, source_target_pairs={{0,1},{1,0},{2,3},{3,2},{4,5},{5,4},{6,7},{7,6},{8,9},{9,8},{10,11... | collective-permute-start | bytes 1179656 | tf_op jit(solution)/shard_map/ppermute | solution.py:210
  54.7 1.3 collective-permute-done.4.train_o
  56.2 19.7 %all_to_all.26 = bf16[8,96,1024]{2,1,0:T(8,128)(2,1)S(1)} all-to-all(bf16[8,96,1024]{2,1,0:T(8,128)(2,1)S(1)} %broadcast_in_dim.4), channel_id=1, replica_groups={{0,33,64,97,128,161,192,225},{3,34,67,98,131,162,195,226},{4,37,68,101,..., dimensions={0} | all-to-all | bytes 3145728 | tf_op jit(solution)/shard_map/all_to_all | solution.py:213
  75.8 10.6 %collective-permute-start.5 = (bf16[768,1024]{1,0:T(8,128)(2,1)S(1)}, bf16[768,1024]{1,0:T(8,128)(2,1)S(1)}, u32[]{:S(2)}, u32[]{:S(2)}) collective-permute-start(bf16[768,1024]{1,0:T(8,128)(2,1)S(1)} %bitcast.12), channel_id=1, source_target_pairs={{0,1},{1,0},{2,3},{3,2},{4,5},{5,4},{6,7},{7,6},{8,9},{9,8},{10,11... | collective-permute-start | bytes 4718600 | tf_op jit(solution)/shard_map/ppermute | solution.py:214
  86.4 3.0 %collective-permute-done.5.other = bf16[768,1024]{1,0:T(8,128)(2,1)S(1)} collective-permute-done((bf16[768,1024]{1,0:T(8,128)(2,1)S(1)}, bf16[768,1024]{1,0:T(8,128)(2,1)S(1)}, u32[]{:S(2)}, u32[]{:S(2)}) %collective-permute-start.5) | collective-permute-done | bytes 1572896 | tf_op jit(solution)/shard_map/ppermute | solution.py:214
  89.4 3.0 %shard_map.75 = bf16[384,512]{1,0:T(8,128)(2,1)S(1)} custom-call(s32[4]{0:T(128)S(1)} %pad_add_fusion.place, s32[1]{0:T(128)} %shard_map.73.token, bf16[768,1024]{1,0:T(8,128)(2,1)S(1)} %bitcast.13, bf16[768,1024]{1,0:T(8,128)(2,1)S(1)} %collective-permute-done.5.other, bf16[384,512]{1,0:T(8,128)(2,1)S(1)} %copy-done.4, ...), custom_call_target="tpu_custom_call" | custom-call | flops 1207959552 | bytes 4194304 | tf_op jit(solution)/shard_map/pallas_call | solution.py:141
  92.4 20.0 %all_to_all.27 = bf16[8,48,512]{2,1,0:T(8,128)(2,1)S(1)} all-to-all(bf16[8,48,512]{2,1,0:T(8,128)(2,1)S(1)} %bitcast.17), channel_id=1, replica_groups=mesh['z_hi'=2,'y'=8,'x'=4,'z_a'=2,'z_b'=2,'core'=2] {'x','z_a'}, dimensions={0} | all-to-all | bytes 786432 | tf_op jit(solution)/shard_map/all_to_all | solution.py:225
  112.5 1.9 %collective-permute-start.6 = (f32[48,512]{1,0:T(8,128)S(1)}, f32[48,512]{1,0:T(8,128)S(1)}, u32[]{:S(2)}, u32[]{:S(2)}) collective-permute-start(f32[48,512]{1,0:T(8,128)S(1)} %convert_reduce_fusion.2), channel_id=1, source_target_pairs={{0,2},{2,0},{1,3},{3,1},{4,6},{6,4},{5,7},{7,5},{8,10},{10,8},{9,1... | collective-permute-start | bytes 294920 | tf_op jit(solution)/shard_map/ppermute | solution.py:226
  114.4 3.8 %collective-permute-done.6 = f32[48,512]{1,0:T(8,128)S(1)} collective-permute-done((f32[48,512]{1,0:T(8,128)S(1)}, f32[48,512]{1,0:T(8,128)S(1)}, u32[]{:S(2)}, u32[]{:S(2)}) %collective-permute-start.6) | collective-permute-done | bytes 98336 | tf_op jit(solution)/shard_map/ppermute | solution.py:226
  118.3 16.6 %all_to_all.28 = bf16[8,48,512]{2,1,0:T(8,128)(2,1)S(1)} all-to-all(bf16[8,48,512]{2,1,0:T(8,128)(2,1)S(1)} %broadcast_in_dim.5), channel_id=1, replica_groups=mesh['z_hi'=2,'y'=8,'x'=4,'z_a'=2,'z_b'=2,'core'=2] {'x','z_a'}, dimensions={0} | all-to-all | bytes 786432 | tf_op jit(solution)/shard_map/all_to_all | solution.py:228
  134.9 2.4 %collective-permute-start.7 = (bf16[384,512]{1,0:T(8,128)(2,1)S(1)}, bf16[384,512]{1,0:T(8,128)(2,1)S(1)}, u32[]{:S(2)}, u32[]{:S(2)}) collective-permute-start(bf16[384,512]{1,0:T(8,128)(2,1)S(1)} %bitcast.14), channel_id=1, source_target_pairs={{0,1},{1,0},{2,3},{3,2},{4,5},{5,4},{6,7},{7,6},{8,9},{9,8},{10,11... | collective-permute-start | bytes 1179656 | tf_op jit(solution)/shard_map/ppermute | solution.py:229
  137.3 1.3 collective-permute-done.7.other
  138.7 0.6 shard_map.76
  139.3 22.3 %all_to_all.29 = bf16[16,24,512]{2,1,0:T(8,128)(2,1)S(1)} all-to-all(bf16[16,24,512]{2,1,0:T(8,128)(2,1)S(1)} %bitcast.16), channel_id=1, replica_groups=mesh['z_hi'=2,'y'=8,'x'=4,'z_a'=2,'z_b'=2,'core'=2] {'z_hi','y'}, dimensions={0} | all-to-all | bytes 786432 | tf_op jit(solution)/shard_map/all_to_all | solution.py:239
  161.6 0.7 convert_reduce_fusion.1
  (24 shorter events, 0.5 us)
Async XLA Ops:
  0.0 14.7 %collective-permute-start = (bf16[1024,512]{1,0:T(8,128)(2,1)}, bf16[1024,512]{1,0:T(8,128)(2,1)S(1)}, u32[]{:S(2)}, u32[]{:S(2)}) collective-permute-start(bf16[1024,512]{1,0:T(8,128)(2,1)} %b_in.1), channel_id=1, source_target_pairs={{1,0},{2,3},{5,4},{6,7},{8,9},{11,10},{12,13},{15,14},{17,16},{18,... | collective-permute-start | bytes 3145736 | tf_op jit(solution)/shard_map/ppermute | solution.py:182
  8.8 5.9 %collective-permute-start.1 = (bf16[512,1024]{1,0:T(8,128)(2,1)}, bf16[512,1024]{1,0:T(8,128)(2,1)S(1)}, u32[]{:S(2)}, u32[]{:S(2)}) collective-permute-start(bf16[512,1024]{1,0:T(8,128)(2,1)} %b_out.3), channel_id=1, source_target_pairs={{0,1},{3,2},{4,5},{7,6},{9,8},{10,11},{13,12},{14,15},{16,17},{19,... | collective-permute-start | bytes 3145736 | tf_op jit(solution)/shard_map/ppermute | solution.py:183
  10.1 4.6 %collective-permute-start.2 = (bf16[768,512]{1,0:T(8,128)(2,1)}, bf16[768,512]{1,0:T(8,128)(2,1)S(1)}, u32[]{:S(2)}, u32[]{:S(2)}) collective-permute-start(bf16[768,512]{1,0:T(8,128)(2,1)} %grad.1), channel_id=1, source_target_pairs={{0,1},{3,2},{4,5},{7,6},{9,8},{10,11},{13,12},{14,15},{16,17},{19,... | collective-permute-start | bytes 2359304 | tf_op jit(solution)/shard_map/ppermute | solution.py:184
  11.5 3.2 %copy-start = (bf16[512,1024]{1,0:T(8,128)(2,1)S(1)}, bf16[512,1024]{1,0:T(8,128)(2,1)}, u32[]{:S(2)}) copy-start(bf16[512,1024]{1,0:T(8,128)(2,1)} %b_out.3) | copy-start | bytes 3145732
  11.5 3.2 %copy-start.1 = (bf16[768,1024]{1,0:T(8,128)(2,1)S(1)}, bf16[768,1024]{1,0:T(8,128)(2,1)}, u32[]{:S(2)}) copy-start(bf16[768,1024]{1,0:T(8,128)(2,1)} %act.1) | copy-start | bytes 4718596
  11.6 3.2 %copy-start.2 = (bf16[1024,512]{1,0:T(8,128)(2,1)S(1)}, bf16[1024,512]{1,0:T(8,128)(2,1)}, u32[]{:S(2)}) copy-start(bf16[1024,512]{1,0:T(8,128)(2,1)} %b_in.1) | copy-start | bytes 3145732
  11.6 3.2 %copy-start.3 = (bf16[768,512]{1,0:T(8,128)(2,1)S(1)}, bf16[768,512]{1,0:T(8,128)(2,1)}, u32[]{:S(2)}) copy-start(bf16[768,512]{1,0:T(8,128)(2,1)} %grad.1) | copy-start | bytes 2359300
  33.2 3.6 %copy-start.4 = (bf16[384,512]{1,0:T(8,128)(2,1)S(1)}, bf16[384,512]{1,0:T(8,128)(2,1)}, u32[]{:S(2)}) copy-start(bf16[384,512]{1,0:T(8,128)(2,1)} %train) | copy-start | bytes 1179652
  33.5 21.1 %collective-permute-start.3 = (bf16[96,1024]{1,0:T(8,128)(2,1)S(1)}, bf16[96,1024]{1,0:T(8,128)(2,1)S(1)}, u32[]{:S(2)}, u32[]{:S(2)}) collective-permute-start(bf16[96,1024]{1,0:T(8,128)(2,1)S(1)} %convert_element_type.22), channel_id=1, source_target_pairs={{0,257},{1,5},{3,258},{2,6},{4,261},{5,1},{7,262},{6,2},{9,264},{8... | collective-permute-start | bytes 589832 | tf_op jit(solution)/shard_map/ppermute | solution.py:209
  36.8 19.2 %collective-permute-start.4 = (bf16[384,512]{1,0:T(8,128)(2,1)S(1)}, bf16[384,512]{1,0:T(8,128)(2,1)S(1)}, u32[]{:S(2)}, u32[]{:S(2)}) collective-permute-start(bf16[384,512]{1,0:T(8,128)(2,1)S(1)} %copy-done.4), channel_id=1, source_target_pairs={{0,1},{1,0},{2,3},{3,2},{4,5},{5,4},{6,7},{7,6},{8,9},{9,8},{10,11... | collective-permute-start | bytes 1179656 | tf_op jit(solution)/shard_map/ppermute | solution.py:210
  56.1 33.3 %copy-start.5 = (f32[16384]{0:T(1024)S(1)}, f32[16384]{0:T(1024)}, u32[]{:S(2)}) copy-start(f32[16384]{0:T(1024)} %param.13) | copy-start | bytes 196612
  56.1 33.3 %copy-start.6 = (f32[16384]{0:T(1024)S(1)}, f32[16384]{0:T(1024)}, u32[]{:S(2)}) copy-start(f32[16384]{0:T(1024)} %param.12) | copy-start | bytes 196612
  75.8 13.6 %collective-permute-start.5 = (bf16[768,1024]{1,0:T(8,128)(2,1)S(1)}, bf16[768,1024]{1,0:T(8,128)(2,1)S(1)}, u32[]{:S(2)}, u32[]{:S(2)}) collective-permute-start(bf16[768,1024]{1,0:T(8,128)(2,1)S(1)} %bitcast.12), channel_id=1, source_target_pairs={{0,1},{1,0},{2,3},{3,2},{4,5},{5,4},{6,7},{7,6},{8,9},{9,8},{10,11... | collective-permute-start | bytes 4718600 | tf_op jit(solution)/shard_map/ppermute | solution.py:214
  112.5 5.8 %collective-permute-start.6 = (f32[48,512]{1,0:T(8,128)S(1)}, f32[48,512]{1,0:T(8,128)S(1)}, u32[]{:S(2)}, u32[]{:S(2)}) collective-permute-start(f32[48,512]{1,0:T(8,128)S(1)} %convert_reduce_fusion.2), channel_id=1, source_target_pairs={{0,2},{2,0},{1,3},{3,1},{4,6},{6,4},{5,7},{7,5},{8,10},{10,8},{9,1... | collective-permute-start | bytes 294920 | tf_op jit(solution)/shard_map/ppermute | solution.py:226
  134.9 3.8 %collective-permute-start.7 = (bf16[384,512]{1,0:T(8,128)(2,1)S(1)}, bf16[384,512]{1,0:T(8,128)(2,1)S(1)}, u32[]{:S(2)}, u32[]{:S(2)}) collective-permute-start(bf16[384,512]{1,0:T(8,128)(2,1)S(1)} %bitcast.14), channel_id=1, source_target_pairs={{0,1},{1,0},{2,3},{3,2},{4,5},{5,4},{6,7},{7,6},{8,9},{9,8},{10,11... | collective-permute-start | bytes 1179656 | tf_op jit(solution)/shard_map/ppermute | solution.py:229

commit v11 on v10

--- a/solution.py
+++ b/solution.py
@@ -14,7 +14,7 @@
 COL = (*CHIPS, "core")
 ALL = ROW + COL
 SIZES = (2, 8, 4, 2, 2, 2)
-NEAR = ("x", "z_a")
+NEAR = ("x", "z_b")
 SWAP = [(0, 1), (1, 0)]
 MIB = 1024 * 1024
 
@@ -223,7 +223,8 @@
         32,
     )
     inner_sum = summed(near(partial_inner.reshape(8, -1, half)))
-    inner_sum = inner_sum + lax.ppermute(inner_sum, "z_b", SWAP)
+    far_inner = lax.ppermute(inner_sum.astype(bf16), "z_a", SWAP)
+    inner_sum = inner_sum + far_inner.astype(f32)
     factor = 1.0 / float(eig_in.shape[0]) ** 0.5
     inner = near(spread((inner_sum * factor).astype(bf16), 8)).reshape(train, half)
     inner_o = lax.ppermute(inner, "core", SWAP)

time: 164 us -> 154 us (0.939)
  blocking collectives: 94.6 us -> 81.7 us
  starting transfers between devices: 47.4 us -> 51.4 us
    all_to_all x1, blocking collectives: 16.6 us -> 9.35 us  [per_device(): near(spread((inner_sum * factor).astype(bf16), 8)).reshape(train, half)]
    all_to_all x1, blocking collectives: 20 us -> 14.1 us  [per_device(): inner_sum = summed(near(partial_inner.reshape(8, -1, half)))]
    ppermute x1, starting transfers between devices: 2.44 us -> 5.57 us  [per_device(): inner_o = lax.ppermute(inner, 'core', SWAP)]
where the time goes in v11:
time: 154 us; the launch traced here: 153 us
  blocking collectives  81.7 us (53%)
  starting transfers between devices  51.4 us (33%)
  waiting for transfers between devices  11.7 us (8%)
  Pallas kernels  6.45 us (4%)
    all_to_all x1, blocking collectives, per_device(): lax.all_to_all(partial_out.reshape(16, -1, half), ROW, 0, 0, tiled=True)  22.5 us
    all_to_all x1, blocking collectives, per_device(): own = mixed(spread(rot, 8)).reshape(queries, width)  19.7 us
    ppermute x1, starting transfers between devices, per_device(): train_o = lax.ppermute(train_rot, 'core', SWAP)  17.8 us
    all_to_all x1, blocking collectives, per_device(): eighth = summed(mixed(part.reshape(8, -1, width)))  16 us
    all_to_all x1, blocking collectives, per_device(): inner_sum = summed(near(partial_inner.reshape(8, -1, half)))  14.1 us
    ppermute x1, starting transfers between devices, per_device(): other = lax.ppermute(own, 'core', SWAP)  10.6 us
    all_to_all x1, blocking collectives, per_device(): near(spread((inner_sum * factor).astype(bf16), 8)).reshape(train, half)  9.35 us
    ppermute x1, starting transfers between devices, per_device(): basis_in_o = lax.ppermute(basis_in, ALL, role_pairs(1))  8.84 us
  transfers between devices with their start and end apart: 8, of which 5 were waited for; matrix products, arithmetic and copies ran while one was open for 0% of the time, Pallas kernels for 0%

profile of v11, /device:TPU:1, one launch (start us, length us, event | category | flops | bytes accessed | tf_op | source)
XLA Modules:
  0.0 152.9 jit_solution(11575646911788063412)
XLA Ops:
  0.0 8.8 %collective-permute-start = (bf16[1024,512]{1,0:T(8,128)(2,1)}, bf16[1024,512]{1,0:T(8,128)(2,1)S(1)}, u32[]{:S(2)}, u32[]{:S(2)}) collective-permute-start(bf16[1024,512]{1,0:T(8,128)(2,1)} %b_in.1), channel_id=1, source_target_pairs={{1,0},{2,3},{5,4},{6,7},{8,9},{11,10},{12,13},{15,14},{17,16},{18,... | collective-permute-start | bytes 3145736 | tf_op jit(solution)/shard_map/ppermute | solution.py:182
  8.8 1.3 collective-permute-start.1
  10.1 1.3 collective-permute-start.2
  11.6 0.5 shard_map.73.token
  12.1 2.7 %collective-permute-done.2.grad_o = bf16[768,512]{1,0:T(8,128)(2,1)S(1)} collective-permute-done((bf16[768,512]{1,0:T(8,128)(2,1)}, bf16[768,512]{1,0:T(8,128)(2,1)S(1)}, u32[]{:S(2)}, u32[]{:S(2)}) %collective-permute-start.2) | collective-permute-done | bytes 786464 | tf_op jit(solution)/shard_map/ppermute | solution.py:184
  14.8 2.4 %shard_map.74 = bf16[768,1024]{1,0:T(8,128)(2,1)S(1)} custom-call(s32[4]{0:T(128)S(1)} %pad_add_fusion.place, bf16[768,1024]{1,0:T(8,128)(2,1)S(1)} %copy-done.1, bf16[768,512]{1,0:T(8,128)(2,1)S(1)} %copy-done.3, bf16[1024,512]{1,0:T(8,128)(2,1)S(1)} %copy-done.2, bf16[512,1024]{1,0:T(8,128)(2,1)S(1)} %copy-done, ...), custom_call_target="tpu_custom_call" | custom-call | flops 1610612736 | bytes 4194304 | tf_op jit(solution)/shard_map/pallas_call | solution.py:141
  17.1 16.0 %all_to_all.25 = bf16[8,96,1024]{2,1,0:T(8,128)(2,1)S(1)} all-to-all(bf16[8,96,1024]{2,1,0:T(8,128)(2,1)S(1)} %bitcast.11), channel_id=1, replica_groups={{0,33,64,97,128,161,192,225},{3,34,67,98,131,162,195,226},{4,37,68,101,..., dimensions={0} | all-to-all | bytes 3145728 | tf_op jit(solution)/shard_map/all_to_all | solution.py:207
  33.2 0.3 convert_reduce_fusion
  33.5 3.3 %collective-permute-start.3 = (bf16[96,1024]{1,0:T(8,128)(2,1)S(1)}, bf16[96,1024]{1,0:T(8,128)(2,1)S(1)}, u32[]{:S(2)}, u32[]{:S(2)}) collective-permute-start(bf16[96,1024]{1,0:T(8,128)(2,1)S(1)} %convert_element_type.28), channel_id=1, source_target_pairs={{0,257},{1,5},{3,258},{2,6},{4,261},{5,1},{7,262},{6,2},{9,264},{8... | collective-permute-start | bytes 589832 | tf_op jit(solution)/shard_map/ppermute | solution.py:209
  36.8 17.8 %collective-permute-start.4 = (bf16[384,512]{1,0:T(8,128)(2,1)S(1)}, bf16[384,512]{1,0:T(8,128)(2,1)S(1)}, u32[]{:S(2)}, u32[]{:S(2)}) collective-permute-start(bf16[384,512]{1,0:T(8,128)(2,1)S(1)} %copy-done.4), channel_id=1, source_target_pairs={{0,1},{1,0},{2,3},{3,2},{4,5},{5,4},{6,7},{7,6},{8,9},{9,8},{10,11... | collective-permute-start | bytes 1179656 | tf_op jit(solution)/shard_map/ppermute | solution.py:210
  54.7 1.3 collective-permute-done.4.train_o
  56.2 19.7 %all_to_all.26 = bf16[8,96,1024]{2,1,0:T(8,128)(2,1)S(1)} all-to-all(bf16[8,96,1024]{2,1,0:T(8,128)(2,1)S(1)} %broadcast_in_dim.4), channel_id=1, replica_groups={{0,33,64,97,128,161,192,225},{3,34,67,98,131,162,195,226},{4,37,68,101,..., dimensions={0} | all-to-all | bytes 3145728 | tf_op jit(solution)/shard_map/all_to_all | solution.py:213
  75.8 10.6 %collective-permute-start.5 = (bf16[768,1024]{1,0:T(8,128)(2,1)S(1)}, bf16[768,1024]{1,0:T(8,128)(2,1)S(1)}, u32[]{:S(2)}, u32[]{:S(2)}) collective-permute-start(bf16[768,1024]{1,0:T(8,128)(2,1)S(1)} %bitcast.12), channel_id=1, source_target_pairs={{0,1},{1,0},{2,3},{3,2},{4,5},{5,4},{6,7},{7,6},{8,9},{9,8},{10,11... | collective-permute-start | bytes 4718600 | tf_op jit(solution)/shard_map/ppermute | solution.py:214
  86.4 3.0 %collective-permute-done.5.other = bf16[768,1024]{1,0:T(8,128)(2,1)S(1)} collective-permute-done((bf16[768,1024]{1,0:T(8,128)(2,1)S(1)}, bf16[768,1024]{1,0:T(8,128)(2,1)S(1)}, u32[]{:S(2)}, u32[]{:S(2)}) %collective-permute-start.5) | collective-permute-done | bytes 1572896 | tf_op jit(solution)/shard_map/ppermute | solution.py:214
  89.4 3.0 %shard_map.75 = bf16[384,512]{1,0:T(8,128)(2,1)S(1)} custom-call(s32[4]{0:T(128)S(1)} %pad_add_fusion.place, s32[1]{0:T(128)} %shard_map.73.token, bf16[768,1024]{1,0:T(8,128)(2,1)S(1)} %bitcast.13, bf16[768,1024]{1,0:T(8,128)(2,1)S(1)} %collective-permute-done.5.other, bf16[384,512]{1,0:T(8,128)(2,1)S(1)} %copy-done.4, ...), custom_call_target="tpu_custom_call" | custom-call | flops 1207959552 | bytes 4194304 | tf_op jit(solution)/shard_map/pallas_call | solution.py:141
  92.4 14.1 %all_to_all.27 = bf16[8,48,512]{2,1,0:T(8,128)(2,1)S(1)} all-to-all(bf16[8,48,512]{2,1,0:T(8,128)(2,1)S(1)} %bitcast.17), channel_id=1, replica_groups=mesh['z_hi'=2,'y'=8,'x'=4,'z_a'=2,'z_b'=2,'core'=2] {'x','z_b'}, dimensions={0} | all-to-all | bytes 786432 | tf_op jit(solution)/shard_map/all_to_all | solution.py:225
  106.6 2.8 %collective-permute-start.6 = (bf16[48,512]{1,0:T(8,128)(2,1)S(1)}, bf16[48,512]{1,0:T(8,128)(2,1)S(1)}, u32[]{:S(2)}, u32[]{:S(2)}) collective-permute-start(bf16[48,512]{1,0:T(8,128)(2,1)S(1)} %convert_element_type.32), channel_id=1, source_target_pairs={{0,4},{4,0},{1,5},{5,1},{2,6},{6,2},{3,7},{7,3},{8,12},{12,8},{9,1... | collective-permute-start | bytes 147464 | tf_op jit(solution)/shard_map/ppermute | solution.py:226
  109.4 3.4 %collective-permute-done.6 = bf16[48,512]{1,0:T(8,128)(2,1)S(1)} collective-permute-done((bf16[48,512]{1,0:T(8,128)(2,1)S(1)}, bf16[48,512]{1,0:T(8,128)(2,1)S(1)}, u32[]{:S(2)}, u32[]{:S(2)}) %collective-permute-start.6) | collective-permute-done | bytes 49184 | tf_op jit(solution)/shard_map/ppermute | solution.py:226
  112.9 9.4 %all_to_all.28 = bf16[8,48,512]{2,1,0:T(8,128)(2,1)S(1)} all-to-all(bf16[8,48,512]{2,1,0:T(8,128)(2,1)S(1)} %broadcast_in_dim.5), channel_id=1, replica_groups=mesh['z_hi'=2,'y'=8,'x'=4,'z_a'=2,'z_b'=2,'core'=2] {'x','z_b'}, dimensions={0} | all-to-all | bytes 786432 | tf_op jit(solution)/shard_map/all_to_all | solution.py:229
  122.2 5.6 %collective-permute-start.7 = (bf16[384,512]{1,0:T(8,128)(2,1)S(1)}, bf16[384,512]{1,0:T(8,128)(2,1)S(1)}, u32[]{:S(2)}, u32[]{:S(2)}) collective-permute-start(bf16[384,512]{1,0:T(8,128)(2,1)S(1)} %bitcast.14), channel_id=1, source_target_pairs={{0,1},{1,0},{2,3},{3,2},{4,5},{5,4},{6,7},{7,6},{8,9},{9,8},{10,11... | collective-permute-start | bytes 1179656 | tf_op jit(solution)/shard_map/ppermute | solution.py:230
  127.8 1.3 collective-permute-done.7.other
  129.2 0.6 shard_map.76
  129.8 22.5 %all_to_all.29 = bf16[16,24,512]{2,1,0:T(8,128)(2,1)S(1)} all-to-all(bf16[16,24,512]{2,1,0:T(8,128)(2,1)S(1)} %bitcast.16), channel_id=1, replica_groups=mesh['z_hi'=2,'y'=8,'x'=4,'z_a'=2,'z_b'=2,'core'=2] {'z_hi','y'}, dimensions={0} | all-to-all | bytes 786432 | tf_op jit(solution)/shard_map/all_to_all | solution.py:240
  152.2 0.7 convert_reduce_fusion.1
  (25 shorter events, 0.5 us)
Async XLA Ops:
  0.0 14.7 %collective-permute-start = (bf16[1024,512]{1,0:T(8,128)(2,1)}, bf16[1024,512]{1,0:T(8,128)(2,1)S(1)}, u32[]{:S(2)}, u32[]{:S(2)}) collective-permute-start(bf16[1024,512]{1,0:T(8,128)(2,1)} %b_in.1), channel_id=1, source_target_pairs={{1,0},{2,3},{5,4},{6,7},{8,9},{11,10},{12,13},{15,14},{17,16},{18,... | collective-permute-start | bytes 3145736 | tf_op jit(solution)/shard_map/ppermute | solution.py:182
  8.8 5.9 %collective-permute-start.1 = (bf16[512,1024]{1,0:T(8,128)(2,1)}, bf16[512,1024]{1,0:T(8,128)(2,1)S(1)}, u32[]{:S(2)}, u32[]{:S(2)}) collective-permute-start(bf16[512,1024]{1,0:T(8,128)(2,1)} %b_out.3), channel_id=1, source_target_pairs={{0,1},{3,2},{4,5},{7,6},{9,8},{10,11},{13,12},{14,15},{16,17},{19,... | collective-permute-start | bytes 3145736 | tf_op jit(solution)/shard_map/ppermute | solution.py:183
  10.1 4.6 %collective-permute-start.2 = (bf16[768,512]{1,0:T(8,128)(2,1)}, bf16[768,512]{1,0:T(8,128)(2,1)S(1)}, u32[]{:S(2)}, u32[]{:S(2)}) collective-permute-start(bf16[768,512]{1,0:T(8,128)(2,1)} %grad.1), channel_id=1, source_target_pairs={{0,1},{3,2},{4,5},{7,6},{9,8},{10,11},{13,12},{14,15},{16,17},{19,... | collective-permute-start | bytes 2359304 | tf_op jit(solution)/shard_map/ppermute | solution.py:184
  11.5 3.2 %copy-start = (bf16[512,1024]{1,0:T(8,128)(2,1)S(1)}, bf16[512,1024]{1,0:T(8,128)(2,1)}, u32[]{:S(2)}) copy-start(bf16[512,1024]{1,0:T(8,128)(2,1)} %b_out.3) | copy-start | bytes 3145732
  11.5 3.2 %copy-start.1 = (bf16[768,1024]{1,0:T(8,128)(2,1)S(1)}, bf16[768,1024]{1,0:T(8,128)(2,1)}, u32[]{:S(2)}) copy-start(bf16[768,1024]{1,0:T(8,128)(2,1)} %act.1) | copy-start | bytes 4718596
  11.6 3.2 %copy-start.2 = (bf16[1024,512]{1,0:T(8,128)(2,1)S(1)}, bf16[1024,512]{1,0:T(8,128)(2,1)}, u32[]{:S(2)}) copy-start(bf16[1024,512]{1,0:T(8,128)(2,1)} %b_in.1) | copy-start | bytes 3145732
  11.6 3.2 %copy-start.3 = (bf16[768,512]{1,0:T(8,128)(2,1)S(1)}, bf16[768,512]{1,0:T(8,128)(2,1)}, u32[]{:S(2)}) copy-start(bf16[768,512]{1,0:T(8,128)(2,1)} %grad.1) | copy-start | bytes 2359300
  33.2 3.6 %copy-start.4 = (bf16[384,512]{1,0:T(8,128)(2,1)S(1)}, bf16[384,512]{1,0:T(8,128)(2,1)}, u32[]{:S(2)}) copy-start(bf16[384,512]{1,0:T(8,128)(2,1)} %train) | copy-start | bytes 1179652
  33.5 21.1 %collective-permute-start.3 = (bf16[96,1024]{1,0:T(8,128)(2,1)S(1)}, bf16[96,1024]{1,0:T(8,128)(2,1)S(1)}, u32[]{:S(2)}, u32[]{:S(2)}) collective-permute-start(bf16[96,1024]{1,0:T(8,128)(2,1)S(1)} %convert_element_type.28), channel_id=1, source_target_pairs={{0,257},{1,5},{3,258},{2,6},{4,261},{5,1},{7,262},{6,2},{9,264},{8... | collective-permute-start | bytes 589832 | tf_op jit(solution)/shard_map/ppermute | solution.py:209
  36.8 19.2 %collective-permute-start.4 = (bf16[384,512]{1,0:T(8,128)(2,1)S(1)}, bf16[384,512]{1,0:T(8,128)(2,1)S(1)}, u32[]{:S(2)}, u32[]{:S(2)}) collective-permute-start(bf16[384,512]{1,0:T(8,128)(2,1)S(1)} %copy-done.4), channel_id=1, source_target_pairs={{0,1},{1,0},{2,3},{3,2},{4,5},{5,4},{6,7},{7,6},{8,9},{9,8},{10,11... | collective-permute-start | bytes 1179656 | tf_op jit(solution)/shard_map/ppermute | solution.py:210
  56.1 33.3 %copy-start.5 = (f32[16384]{0:T(1024)S(1)}, f32[16384]{0:T(1024)}, u32[]{:S(2)}) copy-start(f32[16384]{0:T(1024)} %param.13) | copy-start | bytes 196612
  56.1 33.3 %copy-start.6 = (f32[16384]{0:T(1024)S(1)}, f32[16384]{0:T(1024)}, u32[]{:S(2)}) copy-start(f32[16384]{0:T(1024)} %param.12) | copy-start | bytes 196612
  75.8 13.6 %collective-permute-start.5 = (bf16[768,1024]{1,0:T(8,128)(2,1)S(1)}, bf16[768,1024]{1,0:T(8,128)(2,1)S(1)}, u32[]{:S(2)}, u32[]{:S(2)}) collective-permute-start(bf16[768,1024]{1,0:T(8,128)(2,1)S(1)} %bitcast.12), channel_id=1, source_target_pairs={{0,1},{1,0},{2,3},{3,2},{4,5},{5,4},{6,7},{7,6},{8,9},{9,8},{10,11... | collective-permute-start | bytes 4718600 | tf_op jit(solution)/shard_map/ppermute | solution.py:214
  106.6 6.3 %collective-permute-start.6 = (bf16[48,512]{1,0:T(8,128)(2,1)S(1)}, bf16[48,512]{1,0:T(8,128)(2,1)S(1)}, u32[]{:S(2)}, u32[]{:S(2)}) collective-permute-start(bf16[48,512]{1,0:T(8,128)(2,1)S(1)} %convert_element_type.32), channel_id=1, source_target_pairs={{0,4},{4,0},{1,5},{5,1},{2,6},{6,2},{3,7},{7,3},{8,12},{12,8},{9,1... | collective-permute-start | bytes 147464 | tf_op jit(solution)/shard_map/ppermute | solution.py:226
  122.2 6.9 %collective-permute-start.7 = (bf16[384,512]{1,0:T(8,128)(2,1)S(1)}, bf16[384,512]{1,0:T(8,128)(2,1)S(1)}, u32[]{:S(2)}, u32[]{:S(2)}) collective-permute-start(bf16[384,512]{1,0:T(8,128)(2,1)S(1)} %bitcast.14), channel_id=1, source_target_pairs={{0,1},{1,0},{2,3},{3,2},{4,5},{5,4},{6,7},{7,6},{8,9},{9,8},{10,11... | collective-permute-start | bytes 1179656 | tf_op jit(solution)/shard_map/ppermute | solution.py:230
